TPU v7x, 128 devices: a whole 4x4x4 slice. The times are simulated.
128 devices in a mesh: dp: 8 (over y, core), mp: 16 (over x, z).
Axes of the slice: x: 4, y: 4, z: 4, core: 2. Of those that a mesh axis runs over, the one named last changes fastest.
Arguments:
- query_rows: bfloat16 [32768, 16, 128], P('dp', 'mp'), may hold values from -8 to 8
- key_rows: bfloat16 [32768, 16, 128], P('dp', 'mp'), may hold values from -8 to 8
- value_rows: bfloat16 [32768, 16, 128], P('dp', 'mp'), may hold values from -6 to 6
- residual: bfloat16 [16384, 16, 384], P('dp', 'mp'), may hold values from -40 to 40
- lengths: int32 [256], replicated, may hold values from 1 to 256, as said below
- assignment: int32 [256], replicated, may hold values from 0 to 7, as said below
- out_proj: bfloat16 [1024, 1536], P(None, 'mp'), may hold values from -0.1875 to 0.1875
- norm_gain: float32 [1536], replicated, may hold values from 0.5 to 1.5
- norm_bias: float32 [1536], replicated, may hold values from -3 to 3
- glu_proj: bfloat16 [1536, 3072], P(None, 'mp'), may hold values from -0.15625 to 0.15625
- conv_taps: float32 [31, 1536], replicated, may hold values from -1 to 1
- batch_scale: float32 [1536], replicated, may hold values from 0.25 to 1.75
- batch_shift: float32 [1536], replicated, may hold values from -3 to 3
- down_proj: bfloat16 [1536, 1536], P(None, 'mp'), may hold values from -0.15625 to 0.15625
Outputs:
- encoded: bfloat16 [65536, 1536], P(('dp', 'mp'))
Inputs may be any that keep to these rules, and one draw needn't show every extreme that they name: `lengths`: utterance u starts in data group u // 32; a data group holds its utterances in order of u from its first frame on, and its frames after them are padding. In every draw every data group sends exactly 256 frames in each of its 4 utterances to one and the same data group, so that this group receives 4 * 256 frames from every data group; the utterances one data group sends to one data group never have more frames together. `assignment`: every data group sends exactly 4 of its utterances to each data group, itself included. In its new group an utterance lies after those of lower number, from the first frame on, and the frames after them are padding.
All inputs are finite; a program needn't handle non-finite values.
Results may differ from a plain program's by a relative error of at most 0.0034.
Values may be sent and summed in bfloat16 or wider, within the bound.
No kernel may reach another device: no remote copies, remote signals or barrier semaphores. Data moves between devices by JAX's collectives and lax.ppermute only.
A program may use at most 128 MiB of HBM per device.

v0:
```python
import jax
import jax.numpy as jnp
from jax import lax
from jax.sharding import PartitionSpec as P

HD = 64
KERNEL = 31
HALF = 15
MAXLEN = 256
PIECES = 4
QBLK = 512


EPS = 1e-05
MASKED = -1e30


def with_halo(cells, sides, width):
    for axis, dim in sides:
        count = lax.axis_size(axis)
        ends = count - 1
        head = lax.slice_in_dim(cells, 0, width, axis=dim)
        tail = lax.slice_in_dim(cells, cells.shape[dim] - width, cells.shape[dim], axis=dim)
        cells = jnp.concatenate(
            [
                lax.ppermute(tail, axis, [(i, (i + 1) % count) for i in range(ends)]),
                cells,
                lax.ppermute(head, axis, [((i + 1) % count, i) for i in range(ends)]),
            ],
            axis=dim,
        )
    return cells


def unpack_pairs(packed):
    pair_rows, head_count, pair_width = packed.shape
    width = pair_width // 2
    return (
        packed.reshape(pair_rows, head_count, 2, width)
        .transpose(0, 2, 1, 3)
        .reshape(pair_rows * 2, head_count * width)
    )


def unpack_fours(packed):
    four_rows, block_count, four_width = packed.shape
    width = four_width // 4
    return (
        packed.reshape(four_rows, block_count, 4, width)
        .transpose(0, 2, 1, 3)
        .reshape(four_rows * 4, block_count * width)
    )


def utterance_tables(lengths, assignment, per_group):
    utterance_count = lengths.shape[0]
    utterance = jnp.arange(utterance_count, dtype=jnp.int32)
    source = utterance // per_group
    earlier = utterance[None, :] < utterance[:, None]
    same_source = source[None, :] == source[:, None]
    same_target = assignment[None, :] == assignment[:, None]
    span_table = jnp.broadcast_to(lengths[None, :], (utterance_count, utterance_count))
    nothing = jnp.zeros_like(span_table)
    before_start = jnp.sum(jnp.where(earlier & same_source, span_table, nothing), axis=1)
    after_start = jnp.sum(jnp.where(earlier & same_target, span_table, nothing), axis=1)
    slot_first = jnp.sum(
        jnp.where(earlier & same_source & same_target, span_table, nothing), axis=1
    )
    return (source, before_start, after_start, slot_first)


def find_frames(data_group, owner_group, first_frame, lengths, frames, lookup):
    position = jnp.arange(frames, dtype=jnp.int32)[:, None]
    matches = (
        (owner_group[None, :] == data_group)
        & (position >= first_frame[None, :])
        & (position < first_frame[None, :] + lengths[None, :])
    )
    utterance = jnp.arange(lengths.shape[0], dtype=jnp.int32)[None, :]
    occupied_slots = jnp.any(matches, axis=1)
    segment = jnp.where(occupied_slots, jnp.sum(jnp.where(matches, utterance, 0), axis=1), -1)
    shifted = jnp.sum(jnp.where(matches, lookup[None, :] - first_frame[None, :], 0), axis=1)
    source_row = jnp.where(occupied_slots, jnp.arange(frames, dtype=jnp.int32) + shifted, 0)
    return (segment, occupied_slots, source_row)


def outgoing_rows(
    data_group, groups, per_group, capacity, lengths, assignment, before_start, slot_first
):
    first_id = data_group * per_group
    own_length = lax.dynamic_slice_in_dim(lengths, first_id, per_group)
    own_target = lax.dynamic_slice_in_dim(assignment, first_id, per_group)
    own_before = lax.dynamic_slice_in_dim(before_start, first_id, per_group)
    own_slot = lax.dynamic_slice_in_dim(slot_first, first_id, per_group)
    slot_index = jnp.arange(groups * capacity, dtype=jnp.int32)
    target = (slot_index // capacity)[:, None]
    slot_place = (slot_index % capacity)[:, None]
    matches = (
        (own_target[None, :] == target)
        & (slot_place >= own_slot[None, :])
        & (slot_place < own_slot[None, :] + own_length[None, :])
    )
    valid_slot = jnp.any(matches, axis=1)
    send_frame = jnp.sum(
        jnp.where(matches, own_before[None, :] - own_slot[None, :] + slot_place, 0), axis=1
    )
    return (send_frame, valid_slot)


def pack_outgoing(stacked, send_frame, valid_slot):
    picked = jnp.take(stacked, send_frame, axis=0)
    return jnp.where(valid_slot[:, None], picked, jnp.zeros((), stacked.dtype))


def finalize_rows(received_rows, occupied_slots, incoming_row):
    picked = jnp.take(received_rows, incoming_row, axis=0)
    return jnp.where(occupied_slots[:, None], picked, jnp.zeros((), received_rows.dtype))


def attend(query_rows, key_rows, value_rows, segment, live_count):
    group_rows, width_per_head = query_rows.shape
    head_count = width_per_head // HD
    window = QBLK + 2 * MAXLEN
    score_scale = HD ** (-0.5)
    queries = query_rows.reshape(group_rows, head_count, HD)
    keyset = key_rows.reshape(group_rows, head_count, HD)
    valueset = value_rows.reshape(group_rows, head_count, HD)

    def attend_block(block_index, context):
        first_row = (block_index * QBLK).astype(jnp.int32)
        window_low = jnp.clip(first_row - MAXLEN, 0, group_rows - window)
        query_block = lax.dynamic_slice_in_dim(queries, first_row, QBLK, 0)
        key_block = lax.dynamic_slice_in_dim(keyset, window_low, window, 0)
        value_block = lax.dynamic_slice_in_dim(valueset, window_low, window, 0)
        segment_query = lax.dynamic_slice_in_dim(segment, first_row, QBLK, 0)
        segment_key = lax.dynamic_slice_in_dim(segment, window_low, window, 0)
        allowed = (segment_query[:, None] == segment_key[None, :]) & (segment_key[None, :] >= 0)
        scores = (
            jnp.einsum("qhd,khd->hqk", query_block, key_block, preferred_element_type=jnp.float32)
            * score_scale
        )
        scores = jnp.where(allowed[None], scores, MASKED)
        highest = jnp.max(scores, axis=2, keepdims=True)
        exponentials = jnp.exp(scores - highest)
        denominator = jnp.sum(exponentials, axis=2, keepdims=True)
        weights = (exponentials / denominator).astype(jnp.bfloat16)
        blended = jnp.einsum(
            "hqk,khd->qhd", weights, value_block, preferred_element_type=jnp.float32
        )
        blended = jnp.where((segment_query >= 0)[:, None, None], blended, 0.0).astype(jnp.bfloat16)
        return lax.dynamic_update_slice_in_dim(
            context, blended.reshape(QBLK, width_per_head), first_row, 0
        )

    blocks = (live_count + QBLK - 1) // QBLK
    return lax.fori_loop(
        0, blocks, attend_block, jnp.zeros((group_rows, width_per_head), jnp.bfloat16)
    )


def front(context_rows, carried_rows, out_proj, norm_gain, norm_bias, glu_proj):
    carried = carried_rows.astype(jnp.float32) + jnp.dot(
        context_rows,
        lax.all_gather(out_proj, "mp", axis=1, tiled=True),
        preferred_element_type=jnp.float32,
    )
    average = jnp.mean(carried, axis=1, keepdims=True)
    centred = carried - average
    variance = jnp.mean(centred * centred, axis=1, keepdims=True)
    normed = (centred * lax.rsqrt(variance + EPS) * norm_gain + norm_bias).astype(jnp.bfloat16)
    halves = jnp.dot(
        normed,
        lax.all_gather(glu_proj, "mp", axis=1, tiled=True),
        preferred_element_type=jnp.float32,
    )
    feature_count = halves.shape[1] // 2
    gated_rows = (halves[:, :feature_count] * jax.nn.sigmoid(halves[:, feature_count:])).astype(
        jnp.bfloat16
    )
    return (carried, gated_rows)


def depthwise(gated_rows, segment, conv_taps):
    output_rows = gated_rows.shape[0] - 2 * HALF
    centre = segment[HALF : HALF + output_rows]
    accumulated = jnp.zeros((output_rows, gated_rows.shape[1]), jnp.float32)
    for tap_index in range(KERNEL):
        same_segment = (segment[tap_index : tap_index + output_rows] == centre)[:, None]
        term = jnp.where(
            same_segment, gated_rows[tap_index : tap_index + output_rows].astype(jnp.float32), 0.0
        )
        accumulated = accumulated + term * conv_taps[tap_index]
    return accumulated


def on_device(
    query_rows,
    key_rows,
    value_rows,
    residual,
    lengths,
    assignment,
    out_proj,
    norm_gain,
    norm_bias,
    glu_proj,
    conv_taps,
    batch_scale,
    batch_shift,
    down_proj,
):
    query_flat = unpack_pairs(query_rows)
    key_flat = unpack_pairs(key_rows)
    value_flat = unpack_pairs(value_rows)
    residual_flat = unpack_fours(residual)
    data_group = lax.axis_index("dp")
    slab_index = lax.axis_index("mp")
    groups = lax.axis_size("dp")
    slab_count = lax.axis_size("mp")
    group_rows = query_flat.shape[0]
    slab_rows = group_rows // slab_count
    width_per_head = query_flat.shape[1]
    per_group = lengths.shape[0] // groups
    capacity = PIECES * MAXLEN
    source, before_start, after_start, slot_first = utterance_tables(lengths, assignment, per_group)
    receive_table = source * capacity + slot_first
    segment, occupied_slots, incoming_row = find_frames(
        data_group, assignment, after_start, lengths, group_rows, receive_table
    )
    send_frame, valid_slot = outgoing_rows(
        data_group, groups, per_group, capacity, lengths, assignment, before_start, slot_first
    )
    padded_segment = jnp.pad(segment, (HALF, HALF), constant_values=-2)
    wide_segment = lax.dynamic_slice_in_dim(
        padded_segment, slab_index * slab_rows, slab_rows + 2 * HALF
    )
    centre_segment = wide_segment[HALF : HALF + slab_rows]
    members = [query_flat, key_flat, value_flat, residual_flat]
    stacked = jnp.concatenate(members, axis=1)
    received_rows = lax.all_to_all(
        pack_outgoing(stacked, send_frame, valid_slot),
        "dp",
        split_axis=0,
        concat_axis=0,
        tiled=True,
    )
    balanced_rows = finalize_rows(received_rows, occupied_slots, incoming_row)
    context = attend(
        balanced_rows[:, :width_per_head],
        balanced_rows[:, width_per_head : 2 * width_per_head],
        balanced_rows[:, 2 * width_per_head : 3 * width_per_head],
        segment,
        jnp.sum(occupied_slots.astype(jnp.int32)),
    )
    portion_carried = balanced_rows[:, 3 * width_per_head :]
    context_slab, carried_slab = (
        lax.all_to_all(context, "mp", split_axis=0, concat_axis=1, tiled=True),
        lax.all_to_all(portion_carried, "mp", split_axis=0, concat_axis=1, tiled=True),
    )
    carried, gated_rows = front(
        context_slab, carried_slab, out_proj, norm_gain, norm_bias, glu_proj
    )
    wide_gated = with_halo(gated_rows, (("mp", 0),), HALF)
    convolved = depthwise(wide_gated, wide_segment, conv_taps)
    affine = convolved * batch_scale + batch_shift
    swished = (affine * jax.nn.sigmoid(affine)).astype(jnp.bfloat16)
    lowered = jnp.dot(
        swished,
        lax.all_gather(down_proj, "mp", axis=1, tiled=True),
        preferred_element_type=jnp.float32,
    )
    return jnp.where((centre_segment >= 0)[:, None], carried + lowered, 0.0).astype(jnp.bfloat16)


def solution(mesh):
    in_specs = (
        P("dp", "mp", None),
        P("dp", "mp", None),
        P("dp", "mp", None),
        P("dp", "mp", None),
        P(),
        P(),
        P(None, "mp"),
        P(),
        P(),
        P(None, "mp"),
        P(),
        P(),
        P(),
        P(None, "mp"),
    )
    out_specs = P(("dp", "mp"), None)
    return jax.shard_map(
        on_device, mesh=mesh, in_specs=in_specs, out_specs=out_specs, check_vma=False
    )
```

profile of v0, /device:TPU:104, one launch (start us, length us, event | category | flops | bytes accessed | tf_op | source)
XLA Modules:
  0.0 384.4 jit_solution(14243296738832522248)
XLA Ops:
  8.0 4.0 %reshape_transpose_reshape.12 = bf16[8192,64]{1,0:T(8,128)(2,1)} reshape(bf16[4096,1,128]{2,0,1:T(8,128)(2,1)} %param.18) | data formatting | bytes 2097152 | tf_op jit(solution)/shard_map/reshape;transpose;reshape | solution.py:41
  15.7 3.2 reshape_transpose_reshape.15
  19.9 8.1 %pad_maximum_fusion = bf16[8192,288]{1,0:T(8,128)(2,1)} fusion(bf16[8192,96]{1,0:T(8,128)(2,1)S(1)} %reshape_transpose_reshape.15, bf16[8192,64]{1,0:T(8,128)(2,1)} %reshape_transpose_reshape.14, bf16[8192,64]{1,0:T(8,128)(2,1)} %reshape_transpose_reshape.13, bf16[8192,64]{1,0:T(8,128)(2,1)} %reshape_transpose_reshape.12), kind=kLoop, calls=%fused_computation.55 | loop fusion | flops 18874368 | bytes 9437184 | tf_op jit(solution)/shard_map/concatenate | solution.py:239
  28.0 36.1 %gather_fusion = bf16[8192,288]{1,0:T(8,128)(2,1)} fusion(bf16[8192,288]{1,0:T(8,128)(2,1)} %pad_maximum_fusion, s32[8192]{0:T(1024)S(1)} %fusion.64), kind=kCustom, calls=%fused_computation.clone | custom fusion | bytes 9469952 | tf_op jit(solution)/shard_map/jit(_take)/gather | solution.py:111
  64.6 7.8 %select_select_fusion.1 = bf16[8192,288]{1,0:T(8,128)(2,1)} fusion(bf16[8192,288]{1,0:T(8,128)(2,1)} %gather_fusion, pred[8192]{0:T(1024)(128)(4,1)S(1)} %compare_and_fusion.4, pred[8192]{0:T(1024)(128)(4,1)S(1)} %fusion.66), kind=kLoop, calls=%fused_computation.57 | loop fusion | flops 4718592 | bytes 9453568 | tf_op jit(solution)/shard_map/jit(_where)/select_n | solution.py:112
  72.5 8.0 %copy.38 = bf16[8,1024,288]{1,2,0:T(8,128)(2,1)} copy(bf16[8,1024,288]{2,1,0:T(8,128)(2,1)} %bitcast.72) | data formatting | bytes 9437184 | tf_op jit(solution)/shard_map/all_to_all | solution.py:240
  80.4 5.1 %all-to-all-start = ((bf16[8,1024,288]{1,2,0:T(8,128)(2,1)}), bf16[8,1024,288]{1,2,0:T(8,128)(2,1)}, u32[]{:S(2)}, u32[]{:S(2)}) async-start(bf16[8,1024,288]{1,2,0:T(8,128)(2,1)} %copy.38), calls=%async_computation | async-start | bytes 9437184 | tf_op jit(solution)/shard_map/all_to_all | solution.py:240
  88.4 5.1 %select_reduce_fusion.1 = (s32[8192]{0:T(1024)S(1)}, s32[8192]{0:T(1024)S(1)}) fusion(s32[256]{0:T(256)S(1)} %get-tuple-element.232, s32[256]{0:T(256)S(1)} %get-tuple-element.167, pred[256]{0:T(512)(128)(4,1)S(1)} %broadcast_compare_fusion.3, s32[256]{0:T(256)S(1)} %get-tuple-element.231), kind=kLoop, calls=%fused_computation.50 | loop fusion | flops 16760832 | bytes 68864 | tf_op jit(solution)/shard_map/reduce_sum | solution.py:81
  95.8 43.7 %all-to-all-done = bf16[8,1024,288]{1,2,0:T(8,128)(2,1)} async-done(((bf16[8,1024,288]{1,2,0:T(8,128)(2,1)}), bf16[8,1024,288]{1,2,0:T(8,128)(2,1)}, u32[]{:S(2)}, u32[]{:S(2)}) %all-to-all-start) | async-done | bytes 4718624 | tf_op jit(solution)/shard_map/all_to_all | solution.py:240
  139.5 8.0 %copy.39 = bf16[8,1024,288]{2,1,0:T(8,128)(2,1)} copy(bf16[8,1024,288]{1,2,0:T(8,128)(2,1)} %all-to-all-done) | data formatting | bytes 9437184 | tf_op jit(solution)/shard_map/all_to_all | solution.py:240
  147.5 36.1 %gather_fusion.1 = bf16[8192,288]{1,0:T(8,128)(2,1)} fusion(bf16[8192,288]{1,0:T(8,128)(2,1)} %bitcast.71, s32[8192]{0:T(1024)S(1)} %get-tuple-element.199), kind=kCustom, calls=%fused_computation.1.clone | custom fusion | bytes 9469952 | tf_op jit(solution)/shard_map/jit(_take)/gather | solution.py:116
  183.6 6.9 %select_select_fusion = bf16[8192,288]{1,0:T(8,128)(2,1)S(1)} fusion(bf16[8192,288]{1,0:T(8,128)(2,1)} %gather_fusion.1, pred[8192]{0:T(1024)(128)(4,1)S(1)} %compare_and_fusion.3, pred[8192]{0:T(1024)(128)(4,1)S(1)} %fusion.55), kind=kLoop, calls=%fused_computation.56 | loop fusion | flops 4718592 | bytes 9453568 | tf_op jit(solution)/shard_map/jit(_where)/select_n | solution.py:117
  190.5 3.5 slice_bitcast_fusion
  197.4 2.7 copy.42
  200.1 2.7 copy.43
  205.3 7.0 %all-to-all-start.1 = ((bf16[16,512,96]{1,2,0:T(8,128)(2,1)}), bf16[16,512,96]{1,2,0:T(8,128)(2,1)S(1)}, u32[]{:S(2)}, u32[]{:S(2)}) async-start(bf16[16,512,96]{1,2,0:T(8,128)(2,1)} %copy.40), calls=%async_computation.1 | async-start | bytes 3145728 | tf_op jit(solution)/shard_map/all_to_all | solution.py:258
  212.3 63.4 %while.12 = (s32[]{:T(128)}, bf16[8192,64]{0,1:T(8,128)(2,1)S(1)}, s32[]{:T(128)}, s32[8192]{0:T(1024)S(1)}, bf16[8192,1,64]{0,2,1:T(8,128)(2,1)}, /*index=5*/bf...) while((s32[]{:T(128)}, bf16[8192,64]{0,1:T(8,128)(2,1)S(1)}, ...), condition=%wide.region_12.14_spmd, body=%wide.region_9.13_spmd.sunk | while | flops 139526656 | bytes 6716647 | solution.py:156
  276.8 7.2 %all-to-all-start.2 = ((bf16[16,512,64]{1,2,0:T(8,128)(2,1)}), bf16[16,512,64]{1,2,0:T(8,128)(2,1)}, u32[]{:S(2)}, u32[]{:S(2)}) async-start(bf16[16,512,64]{1,2,0:T(8,128)(2,1)} %bitcast.60), calls=%async_computation.2 | async-start | bytes 2097152 | tf_op jit(solution)/shard_map/all_to_all | solution.py:257
  291.0 3.8 all-to-all-done.2
  294.8 5.1 %fusion.72 = (f32[512]{0:T(512)S(1)}, f32[512,1536]{1,0:T(8,128)S(1)}) fusion(f32[512,1536]{1,0:T(8,128)} %copy.45, bf16[512,1024]{0,1:T(8,128)(2,1)} %bitcast.15, bf16[1024,1536]{0,1:T(8,128)(2,1)} %all-gather.4.cloned.1.call-done), kind=kOutput, calls=%fused_computation.234 | convolution fusion | flops 1612185088 | bytes 10487808 | tf_op jit(solution)/shard_map/dot_general | solution.py:162
  300.6 7.7 %fusion.22 = f32[512,3072]{1,0:T(8,128)S(1)} fusion(bf16[1536,3072]{0,1:T(8,128)(2,1)} %all-gather.6.cloned.1.call-done, f32[512,1536]{1,0:T(8,128)S(1)} %get-tuple-element.234, f32[1536]{0:T(1024)S(1)} %copy-done.7, f32[1536]{0:T(1024)S(1)} %copy-done.8, f32[512]{0:T(512)S(1)} %add_rsqrt_fusion, f32[512]{0:T(512)S(1)} %broadcast_multiply_fusion), kind=kOutput, calls=%fused_computation.74 | convolution fusion | flops 4835770368 | bytes 18890752 | tf_op jit(solution)/shard_map/dot_general | solution.py:171
  310.3 3.7 collective-permute-start
  317.1 5.0 %collective-permute-done.1 = bf16[15,1536]{1,0:T(8,128)(2,1)} collective-permute-done((bf16[15,1536]{1,0:T(8,128)(2,1)S(1)}, bf16[15,1536]{1,0:T(8,128)(2,1)}, u32[]{:S(2)}, u32[]{:S(2)}) %collective-permute-start.1) | collective-permute-done | bytes 46112 | tf_op jit(solution)/shard_map/ppermute | solution.py:28
  322.2 55.4 %fusion.21 = bf16[512,1536]{1,0:T(8,128)(2,1)} fusion(f32[512,1536]{1,0:T(8,128)S(1)} %get-tuple-element.234, bf16[1536,1536]{0,1:T(8,128)(2,1)} %all-gather.8.cloned.1.call-done, pred[512]{0:T(512)(128)(4,1)} %get-tuple-element.209, bf16[512,1536]{1,0:T(8,128)(2,1)} %copy-done.1, bf16[15,1536]{1,0:T(8,128)(2,1)} %collective-permute-done.1, ...), kind=kOutput, calls=%fused_computation.70 | convolution fusion | flops 2590507008 | bytes 11320832 | tf_op jit(solution)/shard_map/dot_general | solution.py:267
  (146 shorter events, 93.6 us)
Async XLA Ops:
  6.5 5.4 %copy-start.2 = (bf16[4096,1,128]{2,0,1:T(8,128)(2,1)S(1)}, bf16[4096,1,128]{2,0,1:T(8,128)(2,1)}, u32[]{:S(2)}) copy-start(bf16[4096,1,128]{2,0,1:T(8,128)(2,1)} %param.19) | copy-start | bytes 3145732
  6.5 288.2 %all-gather.4.cloned.1.call-start = ((), (), s32[]{:S(2)}) async-start(), calls=%async_computation.3 | async-start | bytes 3342336 | tf_op jit(solution)/shard_map/all_gather | solution.py:164
  7.3 293.1 %all-gather.6.cloned.1.call-start = ((), (), s32[]{:S(2)}) async-start(), calls=%async_computation.4 | async-start | bytes 10027008 | tf_op jit(solution)/shard_map/all_gather | solution.py:173
  8.0 5.8 %copy-start.3 = (bf16[4096,1,128]{2,0,1:T(8,128)(2,1)S(1)}, bf16[4096,1,128]{2,0,1:T(8,128)(2,1)}, u32[]{:S(2)}) copy-start(bf16[4096,1,128]{2,0,1:T(8,128)(2,1)} %param.20) | copy-start | bytes 3145732
  13.8 5.1 %copy-start.5 = (s32[256]{0:T(256)S(1)}, s32[256]{0:T(256)}, u32[]{:S(2)}) copy-start(s32[256]{0:T(256)} %param.23) | copy-start | bytes 3076
  13.8 5.2 %copy-start.6 = (s32[256]{0:T(256)S(1)}, s32[256]{0:T(256)}, u32[]{:S(2)}) copy-start(s32[256]{0:T(256)} %param.22) | copy-start | bytes 3076
  80.4 14.4 %copy-start.4 = (f32[31,1536]{1,0:T(8,128)S(1)}, f32[31,1536]{1,0:T(8,128)}, u32[]{:S(2)}) copy-start(f32[31,1536]{1,0:T(8,128)} %param.28) | copy-start | bytes 571396
  80.4 59.0 %all-to-all-start = ((bf16[8,1024,288]{1,2,0:T(8,128)(2,1)}), bf16[8,1024,288]{1,2,0:T(8,128)(2,1)}, u32[]{:S(2)}, u32[]{:S(2)}) async-start(bf16[8,1024,288]{1,2,0:T(8,128)(2,1)} %copy.38), calls=%async_computation | async-start | bytes 9437184 | tf_op jit(solution)/shard_map/all_to_all | solution.py:240
  85.5 231.6 %all-gather.8.cloned.1.call-start = ((), (), s32[]{:S(2)}) async-start(), calls=%async_computation.5 | async-start | bytes 5013504 | tf_op jit(solution)/shard_map/all_gather | solution.py:269
  205.3 71.5 %all-to-all-start.1 = ((bf16[16,512,96]{1,2,0:T(8,128)(2,1)}), bf16[16,512,96]{1,2,0:T(8,128)(2,1)S(1)}, u32[]{:S(2)}, u32[]{:S(2)}) async-start(bf16[16,512,96]{1,2,0:T(8,128)(2,1)} %copy.40), calls=%async_computation.1 | async-start | bytes 3145728 | tf_op jit(solution)/shard_map/all_to_all | solution.py:258
  276.8 9.4 %copy-start = (bf16[16,512,96]{1,2,0:T(8,128)(2,1)}, bf16[16,512,96]{1,2,0:T(8,128)(2,1)S(1)}, u32[]{:S(2)}) copy-start(bf16[16,512,96]{1,2,0:T(8,128)(2,1)S(1)} %all-to-all-done.1) | copy-start | bytes 4718596
  276.8 18.0 %all-to-all-start.2 = ((bf16[16,512,64]{1,2,0:T(8,128)(2,1)}), bf16[16,512,64]{1,2,0:T(8,128)(2,1)}, u32[]{:S(2)}, u32[]{:S(2)}) async-start(bf16[16,512,64]{1,2,0:T(8,128)(2,1)} %bitcast.60), calls=%async_computation.2 | async-start | bytes 2097152 | tf_op jit(solution)/shard_map/all_to_all | solution.py:257
  299.9 0.7 copy-start.7
  299.9 0.7 copy-start.8
  309.1 1.2 copy-start.1
  310.3 6.9 %collective-permute-start = (bf16[15,1536]{1,0:T(8,128)(2,1)S(1)}, bf16[15,1536]{1,0:T(8,128)(2,1)}, u32[]{:S(2)}, u32[]{:S(2)}) collective-permute-start(bf16[15,1536]{1,0:T(8,128)(2,1)S(1)} %get-tuple-element.195), channel_id=1, source_target_pairs={{0,1},{1,2},{2,3},{3,4},{4,5},{5,6},{6,7},{7,8},{8,9},{9,10},{10,1... | collective-permute-start | bytes 138248 | tf_op jit(solution)/shard_map/ppermute | solution.py:26
  314.0 8.2 %collective-permute-start.1 = (bf16[15,1536]{1,0:T(8,128)(2,1)S(1)}, bf16[15,1536]{1,0:T(8,128)(2,1)}, u32[]{:S(2)}, u32[]{:S(2)}) collective-permute-start(bf16[15,1536]{1,0:T(8,128)(2,1)S(1)} %get-tuple-element.196), channel_id=1, source_target_pairs={{1,0},{2,1},{3,2},{4,3},{5,4},{6,5},{7,6},{8,7},{9,8},{10,9},{11,1... | collective-permute-start | bytes 138248 | tf_op jit(solution)/shard_map/ppermute | solution.py:28
Sparse Core Ops, SparseCore 0:
  9.5 48.2 all-gather.3
  60.0 75.4 all-gather.5
  137.7 53.6 all-gather.7
where the time goes:
time: 392 us; the launch traced here: 384 us
  local copies, waits for them, and re-layouts  120 us (31%)
  matrix products  120 us (31%)
  waiting for transfers between devices  54.2 us (14%)
  other arithmetic  48.9 us (12%)
  starting transfers between devices  25.8 us (7%)
  between operations  14.3 us (4%)
    dot_general x1, matrix products, on_device(): jnp.dot(swished, lax.all_gather(down_proj, 'mp', axis=1, tiled=True), pre...  55.4 us
    all_to_all x1, waiting for transfers between devices, on_device(): lax.all_to_all(pack_outgoing(stacked, send_frame, valid_slot), 'dp', spli...  43.7 us
    gather x1, local copies, waits for them, and re-layouts, finalize_rows(): picked = jnp.take(received_rows, incoming_row, axis=0)  36.1 us
    gather x1, local copies, waits for them, and re-layouts, pack_outgoing(): picked = jnp.take(stacked, send_frame, axis=0)  36.1 us
    dot_general x16, matrix products, attend_block(): jnp.einsum('qhd,khd->hqk', query_block, key_block, preferred_element_type...  27.2 us
    dot_general x16, matrix products, attend_block(): jnp.einsum('hqk,khd->qhd', weights, value_block, preferred_element_type=j...  24.6 us
    all_to_all x2, local copies, waits for them, and re-layouts, on_device(): lax.all_to_all(pack_outgoing(stacked, send_frame, valid_slot), 'dp', spli...  16 us
    reduce_sum x16, other arithmetic, attend_block(): denominator = jnp.sum(exponentials, axis=2, keepdims=True)  8.24 us
  transfers between devices with their start and end apart: 8, of which 3 were waited for; matrix products, arithmetic and copies ran while one was open for 61% of the time, Pallas kernels for 0%

commit v1 on v0

v1 whole, which is shorter than its diff:
```python
import functools

import jax
import jax.numpy as jnp
from jax import lax
from jax.experimental import pallas as pl
from jax.experimental.pallas import tpu as pltpu
from jax.sharding import PartitionSpec as P

HD = 64
KERNEL = 31
HALF = 15
MAXLEN = 256
EPS = 1e-05
MASKED = -1e30

CELL = MAXLEN // 4
F32 = jnp.float32
BF16 = jnp.bfloat16
NT = (((1,), (1,)), ((), ()))


def cell_tables(data_group, lengths_ref, assignment_ref, start_ref, size_ref, seen_ref):
    per_group = 32
    for t in range(8):
        seen_ref[t] = 0

    def step(i, at):
        u = data_group * per_group + i
        t = assignment_ref[u]
        n = lengths_ref[u]
        k = seen_ref[t]
        seen_ref[t] = k + 1
        start_ref[4 * t + k] = at
        size_ref[4 * t + k] = n
        return at + n

    lax.fori_loop(0, per_group, step, jnp.int32(0))


def pack_kernel(group_ref, lengths_ref, assignment_ref, x_ref, o_ref, flat, start_ref, size_ref, seen_ref):
    cell_tables(group_ref[0], lengths_ref, assignment_ref, start_ref, size_ref, seen_ref)
    rows = x_ref.shape[0]

    def widen(i, _):
        r = pl.multiple_of(i * 64, 64)
        for b in range(3):
            flat[b, pl.ds(r, 64), :] = x_ref[pl.ds(r, 64), 128 * b : 128 * b + 128].astype(F32)
        return 0

    lax.fori_loop(0, rows // 64, widen, 0)
    for b in range(3):
        flat[b, rows : rows + 72, :] = jnp.zeros((72, 128), F32)
    lane = lax.broadcasted_iota(jnp.int32, (CELL, 384), 1)
    frame = 4 * lax.broadcasted_iota(jnp.int32, (CELL, 384), 0) + lane // 96

    def cell(c, _):
        b = start_ref[c]
        n = size_ref[c]
        row = b // 4
        phase = b - 4 * row
        now = jnp.concatenate([flat[i, pl.ds(row, CELL), :] for i in range(3)], axis=1)
        later = jnp.concatenate([flat[i, pl.ds(row + 1, CELL), :] for i in range(3)], axis=1)
        at = pl.multiple_of(c * CELL, CELL)
        for p in range(4):

            @pl.when(phase == p)
            def _():
                mixed = now if p == 0 else jnp.where(lane >= 96 * p, now, later)
                moved = mixed if p == 0 else jnp.concatenate([mixed[:, 96 * p :], mixed[:, : 96 * p]], axis=1)
                o_ref[pl.ds(at, CELL), :] = jnp.where(frame < n, moved, 0.0).astype(BF16)

        return 0

    lax.fori_loop(0, 32, cell, 0)


def attend_kernel(
    group_ref, lengths_ref, assignment_ref, q_ref, k_ref, v_ref, o_ref, qf, kf, vf, start_ref, size_ref, seen_ref
):
    cell_tables(group_ref[0], lengths_ref, assignment_ref, start_ref, size_ref, seen_ref)
    rows = q_ref.shape[0]

    def widen(i, _):
        r = pl.multiple_of(i * 128, 128)
        qf[pl.ds(r, 128), :] = q_ref[pl.ds(r, 128), :].astype(F32) * (HD**-0.5)
        kf[pl.ds(r, 128), :] = k_ref[pl.ds(r, 128), :].astype(F32)
        vf[pl.ds(r, 128), :] = v_ref[pl.ds(r, 128), :].astype(F32)
        return 0

    lax.fori_loop(0, rows // 128, widen, 0)
    for ref in (qf, kf, vf):
        ref[rows : rows + 136, :] = jnp.zeros((136, 128), F32)
    lane = lax.broadcasted_iota(jnp.int32, (CELL, 128), 1)
    low = lane < 64
    frame = 4 * lax.broadcasted_iota(jnp.int32, (CELL, 128), 0) + lane // 64
    lane2 = lax.broadcasted_iota(jnp.int32, (2 * CELL, 128), 1)
    low2 = lane2 < 64
    column = lax.broadcasted_iota(jnp.int32, (1, MAXLEN), 1)
    key_frame = 2 * (column % 128) + column // 128

    def doubled(ref, row, shift):
        now = ref[pl.ds(row, 2 * CELL), :]
        later = ref[pl.ds(row + 1, 2 * CELL), :]
        even = jnp.where(lane2 >= shift, now, later)
        other = pltpu.roll(even, 64, 1)
        swap = shift > 0
        first = jnp.where(low2, even, other)
        second = jnp.where(low2, other, even)
        return jnp.concatenate(
            [jnp.where(swap, second, first), jnp.where(swap, first, second)], axis=0
        ).astype(BF16)

    def cell(c):
        b = start_ref[c]
        n = size_ref[c]
        row = b // 2
        shift = 64 * (b - 2 * row)
        u0 = qf[pl.ds(row, CELL, stride=2), :]
        u1 = qf[pl.ds(row + 1, CELL, stride=2), :]
        u2 = qf[pl.ds(row + 2, CELL, stride=2), :]
        v0 = pltpu.roll(jnp.where(lane >= shift, u0, u1), shift, 1)
        v1 = pltpu.roll(jnp.where(lane >= shift, u1, u2), shift, 1)
        queries = jnp.concatenate(
            [
                jnp.where(low, v0, 0.0),
                jnp.where(low, 0.0, v0),
                jnp.where(low, v1, 0.0),
                jnp.where(low, 0.0, v1),
            ],
            axis=0,
        ).astype(BF16)
        keys = doubled(kf, row, shift)
        values = doubled(vf, row, shift)
        scores = lax.dot_general(queries, keys, NT, preferred_element_type=F32)
        scores = jnp.where(key_frame < n, scores, MASKED)
        exponentials = jnp.exp(scores - jnp.max(scores, axis=1, keepdims=True))
        total = jnp.sum(exponentials, axis=1, keepdims=True)
        weights = (exponentials / total).astype(BF16)
        context = jnp.dot(weights, values, preferred_element_type=F32)
        at = pl.multiple_of(c * CELL, CELL)
        first = jnp.where(low, context[0:64], context[64:128])
        second = jnp.where(low, context[128:192], context[192:256])
        o_ref[pl.ds(at, CELL), 0:128] = jnp.where(frame < n, first, 0.0).astype(BF16)
        o_ref[pl.ds(at, CELL), 128:256] = jnp.where(frame + 2 < n, second, 0.0).astype(BF16)

    def some(i, _):
        cell(2 * i)
        cell(2 * i + 1)
        return 0

    lax.fori_loop(0, 16, some, 0)


def compact_kernel(width, after_ref, x_ref, o_ref, flat):
    lanes = 4 * width
    blocks = lanes // 128
    total = flat.shape[1]
    slabs = o_ref.shape[0]

    def clear(i, _):
        r = pl.multiple_of(i * 16, 16)
        for b in range(blocks):
            flat[b, pl.ds(r, 16), :] = jnp.zeros((16, 128), F32)
        return 0

    lax.fori_loop(0, total // 16, clear, 0)
    lane = lax.broadcasted_iota(jnp.int32, (CELL, lanes), 1)

    def cell(c, _):
        first = after_ref[c]
        row = first // 4
        phase = first - 4 * row
        block = x_ref[pl.ds(pl.multiple_of(c * CELL, CELL), CELL), :].astype(F32)
        for p in range(4):

            @pl.when(phase == p)
            def _():
                s = p * width
                moved = block if p == 0 else jnp.concatenate([block[:, lanes - s :], block[:, : lanes - s]], axis=1)
                here = moved if p == 0 else jnp.where(lane >= s, moved, 0.0)
                for b in range(blocks):
                    at = (b, pl.ds(row + 8, CELL), slice(None))
                    flat[at] = flat[at] + here[:, 128 * b : 128 * b + 128]
                if p > 0:
                    below = jnp.where(lane >= s, 0.0, moved)
                    for b in range((s + 127) // 128):
                        at = (b, pl.ds(row + 9, CELL), slice(None))
                        flat[at] = flat[at] + below[:, 128 * b : 128 * b + 128]

        return 0

    lax.fori_loop(0, 32, cell, 0)

    def window(m, _):
        for b in range(blocks):
            o_ref[m, :, 128 * b : 128 * b + 128] = flat[b, pl.ds(pl.multiple_of(m * 128, 128), 144), :].astype(BF16)
        return 0

    lax.fori_loop(0, slabs, window, 0)


WIN = 144
EDGE = 8


def rest_kernel(
    slab_ref,
    ends_ref,
    x_ref,
    c_ref,
    w_ref,
    gain_ref,
    bias_ref,
    taps_ref,
    scale_ref,
    shift_ref,
    o_ref,
    wo,
    wg,
    wd,
    ctx,
    carried,
    normed,
    gated,
    segment,
    swished,
    turned,
    sems,
):
    slab = slab_ref[0]
    piece = 176

    def fetch(g, _):
        c = g // 16
        m = g - 16 * c
        base = pl.multiple_of(g * piece, 16)
        for s in range(3):
            pltpu.make_async_copy(
                w_ref.at[pl.ds(base, 32), pl.ds(512 * s, 512)],
                wo.at[pl.ds(pl.multiple_of(96 * m + 32 * s, 16), 32), pl.ds(pl.multiple_of(512 * c, 512), 512)],
                sems.at[0],
            ).start()
        return 0

    def fetch_glu(g, _):
        c = g // 16
        m = g - 16 * c
        base = pl.multiple_of(g * piece + 32, 16)
        pltpu.make_async_copy(
            w_ref.at[pl.ds(base, 96), :],
            wg.at[pl.ds(pl.multiple_of(192 * m + 96 * c, 16), 96), :],
            sems.at[1],
        ).start()
        return 0

    def fetch_down(g, _):
        c = g // 16
        m = g - 16 * c
        base = pl.multiple_of(g * piece + 128, 16)
        pltpu.make_async_copy(
            w_ref.at[pl.ds(base, 48), :],
            wd.at[pl.ds(pl.multiple_of(96 * m + 48 * c, 16), 48), :],
            sems.at[2],
        ).start()
        return 0

    lax.fori_loop(0, 32, fetch, 0)
    lax.fori_loop(0, 32, fetch_glu, 0)
    lax.fori_loop(0, 32, fetch_down, 0)

    for j in range(4):
        frame = 512 * slab - 4 * EDGE + j + 4 * lax.broadcasted_iota(jnp.int32, (WIN, 128), 0)

        def count(i, number):
            return number + jnp.where(frame >= ends_ref[i], 1, 0)

        number = lax.fori_loop(0, 32, count, jnp.where(frame >= 0, 0, -1))
        segment[j] = number.astype(F32)

    low = lax.broadcasted_iota(jnp.int32, (WIN, 128), 1) < 64

    def heads(h, _):
        at = pl.ds(pl.multiple_of(128 * h, 128), 128)
        for j in range(4):
            part = slice(128 * (j // 2), 128 * (j // 2) + 128)
            left = c_ref[2 * h, :, part].astype(F32)
            right = c_ref[2 * h + 1, :, part].astype(F32)
            if j % 2 == 0:
                right = pltpu.roll(right, 64, 1)
            else:
                left = pltpu.roll(left, 64, 1)
            ctx[WIN * j : WIN * j + WIN, at] = jnp.where(low, left, right).astype(BF16)
        return 0

    lax.fori_loop(0, 8, heads, 0)

    lane = lax.broadcasted_iota(jnp.int32, (WIN, 384), 1)

    def features(g, _):
        at = pl.ds(pl.multiple_of(384 * g, 128), 384)
        for j in range(4):
            whole = None
            for f in range(4):
                block = x_ref[4 * g + f].astype(F32)
                s = 96 * ((f - j) % 4)
                if s:
                    block = jnp.concatenate([block[:, 384 - s :], block[:, : 384 - s]], axis=1)
                if whole is None:
                    whole = block
                else:
                    whole = jnp.where(lane >= 96 * f, block, whole)
            carried[WIN * j : WIN * j + WIN, at] = whole
        return 0

    lax.fori_loop(0, 4, features, 0)

    pltpu.make_async_copy(wo, wo, sems.at[0]).wait()

    def project(n, _):
        at = pl.ds(pl.multiple_of(256 * n, 256), 256)
        carried[:, at] = carried[:, at] + lax.dot_general(
            ctx[...], wo[at, :], NT, preferred_element_type=F32
        )
        return 0

    lax.fori_loop(0, 6, project, 0)

    def norm(i, _):
        at = pl.ds(pl.multiple_of(32 * i, 32), 32)
        rows = carried[at, :]
        centred = rows - jnp.mean(rows, axis=1, keepdims=True)
        variance = jnp.mean(centred * centred, axis=1, keepdims=True)
        normed[at, :] = (centred * lax.rsqrt(variance + EPS) * gain_ref[...] + bias_ref[...]).astype(BF16)
        return 0

    lax.fori_loop(0, 4 * WIN // 32, norm, 0)

    pltpu.make_async_copy(wg, wg, sems.at[1]).wait()

    def glu(n, _):
        value = lax.dot_general(
            normed[...], wg[pl.ds(pl.multiple_of(256 * n, 256), 256), :], NT, preferred_element_type=F32
        )
        gate = lax.dot_general(
            normed[...], wg[pl.ds(pl.multiple_of(1536 + 256 * n, 256), 256), :], NT, preferred_element_type=F32
        )
        out = (value * jax.nn.sigmoid(gate)).astype(BF16).astype(F32)
        for j in range(4):
            for b in range(2):
                gated[2 * n + b, j] = out[WIN * j : WIN * j + WIN, 128 * b : 128 * b + 128]
        return 0

    lax.fori_loop(0, 6, glu, 0)

    def conv(b, _):
        at = pl.ds(pl.multiple_of(128 * b, 128), 128)
        taps = taps_ref[:, at]
        scale = scale_ref[:, at]
        shift = shift_ref[:, at]

        def chunk(i, _):
            row = EDGE + i * 8
            mine = [segment[j, pl.ds(pl.multiple_of(row, 8), 8), :] for j in range(4)]
            sums = [jnp.zeros((8, 128), F32) for _ in range(4)]
            for d in range(-4, 5):
                for p in range(4):
                    used = [j for j in range(4) if -HALF <= 4 * d + p - j <= HALF]
                    if not used:
                        continue
                    values = gated[b, p, pl.ds(row + d, 8), :]
                    owner = segment[p, pl.ds(row + d, 8), :]
                    for j in used:
                        t = 4 * d + p - j + HALF
                        sums[j] = sums[j] + jnp.where(owner == mine[j], values, 0.0) * taps[t : t + 1]
            for j in range(4):
                affine = sums[j] * scale + shift
                turned[0, pl.ds(pl.multiple_of(128 * j + 8 * i, 8), 8), :] = affine * jax.nn.sigmoid(affine)
            return 0

        lax.fori_loop(0, 16, chunk, 0)
        swished[:, at] = turned[0].astype(BF16)
        return 0

    lax.fori_loop(0, 12, conv, 0)

    pltpu.make_async_copy(wd, wd, sems.at[2]).wait()
    live = ends_ref[31]

    def down(n, _):
        at = pl.ds(pl.multiple_of(256 * n, 256), 256)
        lowered = lax.dot_general(swished[...], wd[at, :], NT, preferred_element_type=F32)
        for j in range(4):
            frame = 512 * slab + j + 4 * lax.broadcasted_iota(jnp.int32, (128, 256), 0)
            rows = carried[WIN * j + EDGE : WIN * j + EDGE + 128, at] + lowered[128 * j : 128 * j + 128]
            rows = jnp.where(frame < live, rows, 0.0)
            for b in range(2):
                turned[b, pl.ds(j, 128, stride=4), :] = rows[:, 128 * b : 128 * b + 128]
        o_ref[:, at] = jnp.concatenate([turned[0], turned[1]], axis=1).astype(BF16)
        return 0

    lax.fori_loop(0, 6, down, 0)


SMEM = pl.BlockSpec(memory_space=pltpu.SMEM)
VMEM = pl.BlockSpec(memory_space=pltpu.VMEM)
BIG = 60 * 1024 * 1024


def pack(group, lengths, assignment, x):
    rows = x.shape[0]
    return pl.pallas_call(
        pack_kernel,
        out_shape=jax.ShapeDtypeStruct((32 * CELL, 384), BF16),
        in_specs=[SMEM, SMEM, SMEM, VMEM],
        out_specs=VMEM,
        scratch_shapes=[
            pltpu.VMEM((3, rows + 72, 128), F32),
            pltpu.SMEM((32,), jnp.int32),
            pltpu.SMEM((32,), jnp.int32),
            pltpu.SMEM((8,), jnp.int32),
        ],
        compiler_params=pltpu.CompilerParams(vmem_limit_bytes=24 * 1024 * 1024),
        cost_estimate=pl.CostEstimate(flops=20_000_000, bytes_accessed=3_200_000, transcendentals=0),
        name="pack_cells",
    )(group, lengths, assignment, x)


def attend(group, lengths, assignment, q, k, v):
    rows = q.shape[0]
    return pl.pallas_call(
        attend_kernel,
        out_shape=jax.ShapeDtypeStruct((32 * CELL, 256), BF16),
        in_specs=[SMEM, SMEM, SMEM, VMEM, VMEM, VMEM],
        out_specs=VMEM,
        scratch_shapes=[
            pltpu.VMEM((rows + 136, 128), F32),
            pltpu.VMEM((rows + 136, 128), F32),
            pltpu.VMEM((rows + 136, 128), F32),
            pltpu.SMEM((32,), jnp.int32),
            pltpu.SMEM((32,), jnp.int32),
            pltpu.SMEM((8,), jnp.int32),
        ],
        compiler_params=pltpu.CompilerParams(vmem_limit_bytes=32 * 1024 * 1024),
        cost_estimate=pl.CostEstimate(flops=2_000_000_000, bytes_accessed=4_200_000, transcendentals=2_000_000),
        name="attend_cells",
    )(group, lengths, assignment, q, k, v)


def compact(width, after, cells, slabs):
    lanes = 4 * width
    return pl.pallas_call(
        functools.partial(compact_kernel, width),
        out_shape=jax.ShapeDtypeStruct((slabs, WIN, lanes), BF16),
        in_specs=[SMEM, VMEM],
        out_specs=VMEM,
        scratch_shapes=[pltpu.VMEM((lanes // 128, 32 * CELL + 80, 128), F32)],
        compiler_params=pltpu.CompilerParams(vmem_limit_bytes=24 * 1024 * 1024),
        cost_estimate=pl.CostEstimate(flops=20_000_000, bytes_accessed=3_200_000, transcendentals=0),
        name="compact_cells",
    )(after, cells)


def rest(slab, ends, x, c, w, gain, bias, taps, scale, shift):
    return pl.pallas_call(
        rest_kernel,
        out_shape=jax.ShapeDtypeStruct((512, 1536), BF16),
        in_specs=[SMEM, SMEM, VMEM, VMEM, pl.BlockSpec(memory_space=pl.ANY)] + [VMEM] * 5,
        out_specs=VMEM,
        scratch_shapes=[
            pltpu.VMEM((1536, 1024), BF16),
            pltpu.VMEM((3072, 1536), BF16),
            pltpu.VMEM((1536, 1536), BF16),
            pltpu.VMEM((4 * WIN, 1024), BF16),
            pltpu.VMEM((4 * WIN, 1536), F32),
            pltpu.VMEM((4 * WIN, 1536), BF16),
            pltpu.VMEM((12, 4, WIN, 128), F32),
            pltpu.VMEM((4, WIN, 128), F32),
            pltpu.VMEM((512, 1536), BF16),
            pltpu.VMEM((2, 512, 128), F32),
            pltpu.SemaphoreType.DMA((3,)),
        ],
        compiler_params=pltpu.CompilerParams(vmem_limit_bytes=BIG),
        cost_estimate=pl.CostEstimate(flops=9_000_000_000, bytes_accessed=25_000_000, transcendentals=2_000_000),
        name="project_and_convolve",
    )(slab, ends, x, c, w, gain, bias, taps, scale, shift)


def target_tables(data_group, lengths, assignment):
    count = lengths.shape[0]
    number = jnp.arange(count, dtype=jnp.int32)
    mine = assignment == data_group
    place = jnp.sum(jnp.where((number[None, :] < number[:, None]) & mine[None, :], 1, 0), axis=1)
    slot = jnp.arange(32, dtype=jnp.int32)
    spans = jnp.sum(jnp.where(mine[None, :] & (place[None, :] == slot[:, None]), lengths[None, :], 0), axis=1)
    first = jnp.sum(jnp.where(slot[None, :] < slot[:, None], spans[None, :], 0), axis=1)
    return first, first + spans


def on_device(
    query_rows,
    key_rows,
    value_rows,
    residual,
    lengths,
    assignment,
    out_proj,
    norm_gain,
    norm_bias,
    glu_proj,
    conv_taps,
    batch_scale,
    batch_shift,
    down_proj,
):
    data_group = lax.axis_index("dp").astype(jnp.int32)
    slab = lax.axis_index("mp").astype(jnp.int32)
    groups = lax.axis_size("dp")
    slabs = lax.axis_size("mp")
    core = data_group % 2
    op = lax.dynamic_slice_in_dim(out_proj.T, core * 512, 512, 1)
    op = jnp.concatenate([op[0:32], op[32:64], op[64:96]], axis=1)
    glu = lax.dynamic_slice_in_dim(glu_proj.T, core * 96, 96, 0)
    dn = lax.dynamic_slice_in_dim(down_proj.T, core * 48, 48, 0)
    mine = jnp.concatenate([op, glu, dn], axis=0)
    chips = [[(2 * p + c) * slabs + m for c in range(2) for m in range(slabs)] for p in range(groups // 2)]
    weights = lax.all_gather(mine, ("dp", "mp"), axis=0, tiled=True, axis_index_groups=chips)

    group = data_group.reshape(1)
    x_cells = pack(group, lengths, assignment, residual.reshape(residual.shape[0], 384))
    x_here = lax.all_to_all(
        x_cells.reshape(groups, 4 * CELL, 384), "dp", split_axis=0, concat_axis=0, tiled=True
    )
    c_cells = attend(
        group,
        lengths,
        assignment,
        query_rows.reshape(-1, 128),
        key_rows.reshape(-1, 128),
        value_rows.reshape(-1, 128),
    )
    c_here = lax.all_to_all(
        c_cells.reshape(groups, 4 * CELL, 256), "dp", split_axis=0, concat_axis=0, tiled=True
    )
    first, ends = target_tables(data_group, lengths, assignment)
    x_slab = lax.all_to_all(
        compact(96, first, x_here.reshape(-1, 384), slabs), "mp", split_axis=0, concat_axis=0, tiled=True
    )
    c_slab = lax.all_to_all(
        compact(64, first, c_here.reshape(-1, 256), slabs), "mp", split_axis=0, concat_axis=0, tiled=True
    )
    row = lambda a: a.reshape(1, -1)
    return rest(
        slab.reshape(1),
        ends,
        x_slab,
        c_slab,
        weights,
        row(norm_gain),
        row(norm_bias),
        conv_taps,
        row(batch_scale),
        row(batch_shift),
    )


def solution(mesh):
    in_specs = (
        P("dp", "mp", None),
        P("dp", "mp", None),
        P("dp", "mp", None),
        P("dp", "mp", None),
        P(),
        P(),
        P(None, "mp"),
        P(),
        P(),
        P(None, "mp"),
        P(),
        P(),
        P(),
        P(None, "mp"),
    )
    out_specs = P(("dp", "mp"), None)
    return jax.shard_map(
        on_device, mesh=mesh, in_specs=in_specs, out_specs=out_specs, check_vma=False
    )
```

time: 392 us -> 183 us (0.47)
  the two profiles are of different devices: /device:TPU:104 before, /device:TPU:0 now
where the time goes in v1:
time: 183 us
  Pallas kernels  77.8 us (43%)
  waiting for transfers between devices  60.5 us (33%)
  starting transfers between devices  20 us (11%)
  between operations  13.6 us (7%)
  local copies, waits for them, and re-layouts  9.2 us (5%)
    pallas_call x1, Pallas kernels, rest(): pl.pallas_call(rest_kernel, out_shape=jax.ShapeDtypeStruct((512, 1536), B...  45.1 us
    all_to_all x1, waiting for transfers between devices, on_device(): lax.all_to_all(compact(96, first, x_here.reshape(-1, 384), slabs), 'mp',...  20.5 us
    pallas_call x1, Pallas kernels, attend(): pl.pallas_call(attend_kernel, out_shape=jax.ShapeDtypeStruct((32 * CELL,...  17.7 us
    all_to_all x1, waiting for transfers between devices, on_device(): lax.all_to_all(x_cells.reshape(groups, 4 * CELL, 384), 'dp', split_axis=0...  16.1 us
    all_to_all x1, waiting for transfers between devices, on_device(): lax.all_to_all(compact(64, first, c_here.reshape(-1, 256), slabs), 'mp',...  13.1 us
    pallas_call x2, Pallas kernels, compact(): pl.pallas_call(functools.partial(compact_kernel, width), out_shape=jax.Sh...  11 us
    all_to_all x1, waiting for transfers between devices, on_device(): lax.all_to_all(c_cells.reshape(groups, 4 * CELL, 256), 'dp', split_axis=0...  10.7 us
    all_to_all x1, starting transfers between devices, on_device(): lax.all_to_all(compact(64, first, c_here.reshape(-1, 256), slabs), 'mp',...  7.99 us
  transfers between devices with their start and end apart: 5, of which 4 were waited for; matrix products, arithmetic and copies ran while one was open for 2% of the time, Pallas kernels for 18%

profile of v1, /device:TPU:0, one launch (start us, length us, event | category | flops | bytes accessed | tf_op | source)
XLA Modules:
  0.0 182.8 jit_solution(16219525315665046611)
XLA Ops:
  6.5 1.0 dynamic-slice_bitcast_fusion.2
  7.7 1.1 dynamic-slice_bitcast_fusion.1
  8.8 0.8 pad_maximum_fusion
  9.7 1.2 copy-done.8
  10.9 17.7 %attend_cells.1 = bf16[2048,256]{1,0:T(8,128)(2,1)S(1)} custom-call(s32[1]{0:T(128)} %bitcast.1.group_ref, s32[256]{0:T(256)S(1)} %copy-done.4, s32[256]{0:T(256)S(1)} %copy-done.5, bf16[4096,128]{1,0:T(8,128)(2,1)S(1)} %bitcast.21, bf16[4096,128]{1,0:T(8,128)(2,1)S(1)} %bitcast.22, bf16[4096,128]{1,0:T(8,128)(2,1)S(1)} %bitcast.23), custom_call_target="tpu_custom_call" | custom-call | flops 2000000000 | bytes 4200000 | tf_op jit(solution)/shard_map/attend_cells/pallas_call | solution.py:431
  28.6 1.0 copy-done.3
  29.6 4.7 %all-to-all-start.2 = ((bf16[8,256,256]{2,1,0:T(8,128)(2,1)}), bf16[8,256,256]{2,1,0:T(8,128)(2,1)S(1)}, u32[]{:S(2)}, u32[]{:S(2)}) async-start(bf16[8,256,256]{2,1,0:T(8,128)(2,1)} %bitcast.20), calls=%async_computation.2 | async-start | bytes 2097152 | tf_op jit(solution)/shard_map/all_to_all | solution.py:542
  34.3 4.1 %pack_cells.1 = bf16[2048,384]{1,0:T(8,128)(2,1)S(1)} custom-call(s32[1]{0:T(128)} %bitcast.1.group_ref, s32[256]{0:T(256)S(1)} %copy-done.4, s32[256]{0:T(256)S(1)} %copy-done.5, bf16[2048,384]{1,0:T(8,128)(2,1)S(1)} %bitcast.19), custom_call_target="tpu_custom_call" | custom-call | flops 20000000 | bytes 3200000 | tf_op jit(solution)/shard_map/pack_cells/pallas_call | solution.py:412
  38.4 1.1 copy-done.1
  39.5 10.7 %all-to-all-done.2 = bf16[8,256,256]{2,1,0:T(8,128)(2,1)S(1)} async-done(((bf16[8,256,256]{2,1,0:T(8,128)(2,1)}), bf16[8,256,256]{2,1,0:T(8,128)(2,1)S(1)}, u32[]{:S(2)}, u32[]{:S(2)}) %all-to-all-start.2) | async-done | bytes 1048608 | tf_op jit(solution)/shard_map/all_to_all | solution.py:542
  50.3 3.6 %all-to-all-start = ((bf16[8,256,384]{2,1,0:T(8,128)(2,1)}), bf16[8,256,384]{2,1,0:T(8,128)(2,1)S(1)}, u32[]{:S(2)}, u32[]{:S(2)}) async-start(bf16[8,256,384]{2,1,0:T(8,128)(2,1)} %bitcast.17), calls=%async_computation | async-start | bytes 3145728 | tf_op jit(solution)/shard_map/all_to_all | solution.py:531
  54.2 5.0 %compact_cells.3 = bf16[16,144,256]{2,1,0:T(8,128)(2,1)} custom-call(s32[32]{0:T(128)S(1)} %select_reduce_fusion.2.after_ref, bf16[2048,256]{1,0:T(8,128)(2,1)S(1)} %bitcast.18), custom_call_target="tpu_custom_call" | custom-call | flops 20000000 | bytes 3200000 | tf_op jit(solution)/shard_map/compact_cells/pallas_call | solution.py:452
  59.2 16.1 %all-to-all-done = bf16[8,256,384]{2,1,0:T(8,128)(2,1)S(1)} async-done(((bf16[8,256,384]{2,1,0:T(8,128)(2,1)}), bf16[8,256,384]{2,1,0:T(8,128)(2,1)S(1)}, u32[]{:S(2)}, u32[]{:S(2)}) %all-to-all-start) | async-done | bytes 1572896 | tf_op jit(solution)/shard_map/all_to_all | solution.py:531
  75.4 8.0 %all-to-all-start.3 = ((bf16[16,144,256]{2,1,0:T(8,128)(2,1)}), bf16[16,144,256]{2,1,0:T(8,128)(2,1)}, u32[]{:S(2)}, u32[]{:S(2)}) async-start(bf16[16,144,256]{2,1,0:T(8,128)(2,1)} %compact_cells.3), calls=%async_computation.3 | async-start | bytes 2359296 | tf_op jit(solution)/shard_map/all_to_all | solution.py:549
  83.4 6.0 %compact_cells.2 = bf16[16,144,384]{2,1,0:T(8,128)(2,1)} custom-call(s32[32]{0:T(128)S(1)} %select_reduce_fusion.2.after_ref, bf16[2048,384]{1,0:T(8,128)(2,1)S(1)} %bitcast.16), custom_call_target="tpu_custom_call" | custom-call | flops 20000000 | bytes 3200000 | tf_op jit(solution)/shard_map/compact_cells/pallas_call | solution.py:452
  89.3 13.1 %all-to-all-done.3.c_ref = bf16[16,144,256]{2,1,0:T(8,128)(2,1)} async-done(((bf16[16,144,256]{2,1,0:T(8,128)(2,1)}), bf16[16,144,256]{2,1,0:T(8,128)(2,1)}, u32[]{:S(2)}, u32[]{:S(2)}) %all-to-all-start.3) | async-done | bytes 1179680 | tf_op jit(solution)/shard_map/all_to_all | solution.py:549
  102.4 3.7 %all-to-all-start.1 = ((bf16[16,144,384]{2,1,0:T(8,128)(2,1)}), bf16[16,144,384]{2,1,0:T(8,128)(2,1)S(1)}, u32[]{:S(2)}, u32[]{:S(2)}) async-start(bf16[16,144,384]{2,1,0:T(8,128)(2,1)} %compact_cells.2), calls=%async_computation.1 | async-start | bytes 3538944 | tf_op jit(solution)/shard_map/all_to_all | solution.py:546
  106.2 0.6 add.16.ends_ref
  106.7 0.6 reshape.56.gain_ref
  107.4 0.6 reshape.57.bias_ref
  108.5 0.6 reshape.59.shift_ref
  109.1 20.5 %all-to-all-done.1.x_ref = bf16[16,144,384]{2,1,0:T(8,128)(2,1)S(1)} async-done(((bf16[16,144,384]{2,1,0:T(8,128)(2,1)}), bf16[16,144,384]{2,1,0:T(8,128)(2,1)S(1)}, u32[]{:S(2)}, u32[]{:S(2)}) %all-to-all-start.1) | async-done | bytes 1769504 | tf_op jit(solution)/shard_map/all_to_all | solution.py:546
  129.6 1.2 copy-done.9
  130.9 45.1 %project_and_convolve.1 = bf16[512,1536]{1,0:T(8,128)(2,1)} custom-call(s32[1]{0:T(128)} %bitcast.slab_ref, s32[32]{0:T(128)} %add.16.ends_ref, bf16[16,144,384]{2,1,0:T(8,128)(2,1)} %copy-done.9, bf16[16,144,256]{2,1,0:T(8,128)(2,1)} %all-to-all-done.3.c_ref, bf16[5632,1536]{1,0:T(8,128)(2,1)} %all-gather.2.cloned.1.call-done.w_ref, ...), custom_call_target="tpu_custom_call" | custom-call | flops 8999999488 | bytes 25000000 | tf_op jit(solution)/shard_map/project_and_convolve/pallas_call | solution.py:465
  (34 shorter events, 1.2 us)
Async XLA Ops:
  6.5 1.1 copy-start
  6.5 123.1 %all-gather.2.cloned.1.call-start = ((), (), s32[]{:S(2)}) async-start(), calls=%async_computation.4 | async-start | bytes 17842176 | tf_op jit(solution)/shard_map/all_gather | solution.py:527
  7.6 2.0 %copy-start.4 = (s32[256]{0:T(256)S(1)}, s32[256]{0:T(256)}, u32[]{:S(2)}) copy-start(s32[256]{0:T(256)} %lengths_ref.3) | copy-start | bytes 3076
  7.6 2.0 %copy-start.5 = (s32[256]{0:T(256)S(1)}, s32[256]{0:T(256)}, u32[]{:S(2)}) copy-start(s32[256]{0:T(256)} %assignment_ref.3) | copy-start | bytes 3076
  7.7 2.0 %copy-start.6 = (bf16[4096,1,128]{2,0,1:T(8,128)(2,1)S(1)}, bf16[4096,1,128]{2,0,1:T(8,128)(2,1)}, u32[]{:S(2)}) copy-start(bf16[4096,1,128]{2,0,1:T(8,128)(2,1)} %param.14) | copy-start | bytes 3145732
  7.7 2.0 %copy-start.7 = (bf16[4096,1,128]{2,0,1:T(8,128)(2,1)S(1)}, bf16[4096,1,128]{2,0,1:T(8,128)(2,1)}, u32[]{:S(2)}) copy-start(bf16[4096,1,128]{2,0,1:T(8,128)(2,1)} %param.15) | copy-start | bytes 3145732
  9.7 1.2 copy-start.8
  28.6 1.0 copy-start.3
  29.6 4.7 %copy-start.2 = (bf16[2048,1,384]{2,0,1:T(8,128)(2,1)S(1)}, bf16[2048,1,384]{2,0,1:T(8,128)(2,1)}, u32[]{:S(2)}) copy-start(bf16[2048,1,384]{2,0,1:T(8,128)(2,1)} %param.17) | copy-start | bytes 4718596
  29.6 20.7 %all-to-all-start.2 = ((bf16[8,256,256]{2,1,0:T(8,128)(2,1)}), bf16[8,256,256]{2,1,0:T(8,128)(2,1)S(1)}, u32[]{:S(2)}, u32[]{:S(2)}) async-start(bf16[8,256,256]{2,1,0:T(8,128)(2,1)} %bitcast.20), calls=%async_computation.2 | async-start | bytes 2097152 | tf_op jit(solution)/shard_map/all_to_all | solution.py:542
  38.4 1.1 copy-start.1
  50.3 25.1 %all-to-all-start = ((bf16[8,256,384]{2,1,0:T(8,128)(2,1)}), bf16[8,256,384]{2,1,0:T(8,128)(2,1)S(1)}, u32[]{:S(2)}, u32[]{:S(2)}) async-start(bf16[8,256,384]{2,1,0:T(8,128)(2,1)} %bitcast.17), calls=%async_computation | async-start | bytes 3145728 | tf_op jit(solution)/shard_map/all_to_all | solution.py:531
  75.4 27.1 %all-to-all-start.3 = ((bf16[16,144,256]{2,1,0:T(8,128)(2,1)}), bf16[16,144,256]{2,1,0:T(8,128)(2,1)}, u32[]{:S(2)}, u32[]{:S(2)}) async-start(bf16[16,144,256]{2,1,0:T(8,128)(2,1)} %compact_cells.3), calls=%async_computation.3 | async-start | bytes 2359296 | tf_op jit(solution)/shard_map/all_to_all | solution.py:549
  89.3 17.4 %copy-start.10 = (f32[1536]{0:T(1024)S(1)}, f32[1536]{0:T(1024)}, u32[]{:S(2)}) copy-start(f32[1536]{0:T(1024)} %param.21) | copy-start | bytes 18436
  89.3 18.0 %copy-start.11 = (f32[1536]{0:T(1024)S(1)}, f32[1536]{0:T(1024)}, u32[]{:S(2)}) copy-start(f32[1536]{0:T(1024)} %param.22) | copy-start | bytes 18436
  89.3 18.6 %copy-start.12 = (f32[1536]{0:T(1024)S(1)}, f32[1536]{0:T(1024)}, u32[]{:S(2)}) copy-start(f32[1536]{0:T(1024)} %param.25) | copy-start | bytes 18436
  89.3 19.2 %copy-start.13 = (f32[1536]{0:T(1024)S(1)}, f32[1536]{0:T(1024)}, u32[]{:S(2)}) copy-start(f32[1536]{0:T(1024)} %param.26) | copy-start | bytes 18436
  102.4 27.2 %all-to-all-start.1 = ((bf16[16,144,384]{2,1,0:T(8,128)(2,1)}), bf16[16,144,384]{2,1,0:T(8,128)(2,1)S(1)}, u32[]{:S(2)}, u32[]{:S(2)}) async-start(bf16[16,144,384]{2,1,0:T(8,128)(2,1)} %compact_cells.2), calls=%async_computation.1 | async-start | bytes 3538944 | tf_op jit(solution)/shard_map/all_to_all | solution.py:546
  129.6 1.2 copy-start.9
Sparse Core Ops, SparseCore 0:
  9.8 76.2 all-gather.1

commit v2 on v1

--- a/solution.py
+++ b/solution.py
@@ -76,8 +76,9 @@
 
 
 def attend_kernel(
-    group_ref, lengths_ref, assignment_ref, q_ref, k_ref, v_ref, o_ref, qf, kf, vf, start_ref, size_ref, seen_ref
+    group_ref, lengths_ref, assignment_ref, q_ref, k_ref, v_ref, *rest
 ):
+    outs, (qf, kf, vf, o_ref, start_ref, size_ref, seen_ref) = rest[:8], rest[8:]
     cell_tables(group_ref[0], lengths_ref, assignment_ref, start_ref, size_ref, seen_ref)
     rows = q_ref.shape[0]
 
@@ -150,9 +151,13 @@
         return 0
 
     lax.fori_loop(0, 16, some, 0)
-
-
-def compact_kernel(width, after_ref, x_ref, o_ref, flat):
+    for s in range(8):
+        at = pl.multiple_of((group_ref[0] ^ s) * 4 * CELL, 4 * CELL)
+        outs[s][...] = o_ref[pl.ds(at, 4 * CELL), :]
+
+
+def compact_kernel(width, group_ref, after_ref, *rest):
+    parts, (o_ref, flat) = rest[:-2], rest[-2:]
     lanes = 4 * width
     blocks = lanes // 128
     total = flat.shape[1]
@@ -167,11 +172,11 @@
     lax.fori_loop(0, total // 16, clear, 0)
     lane = lax.broadcasted_iota(jnp.int32, (CELL, lanes), 1)
 
-    def cell(c, _):
-        first = after_ref[c]
+    def cell(x_ref, from_group, k):
+        first = after_ref[4 * from_group + k]
         row = first // 4
         phase = first - 4 * row
-        block = x_ref[pl.ds(pl.multiple_of(c * CELL, CELL), CELL), :].astype(F32)
+        block = x_ref[pl.ds(pl.multiple_of(k * CELL, CELL), CELL), :].astype(F32)
         for p in range(4):
 
             @pl.when(phase == p)
@@ -188,9 +193,21 @@
                         at = (b, pl.ds(row + 9, CELL), slice(None))
                         flat[at] = flat[at] + below[:, 128 * b : 128 * b + 128]
 
-        return 0
-
-    lax.fori_loop(0, 32, cell, 0)
+    if len(parts) == 1:
+
+        def whole(c, _):
+            cell(parts[0], 0, c)
+            return 0
+
+        lax.fori_loop(0, 32, whole, 0)
+    else:
+        for s, part in enumerate(parts):
+
+            def some(k, _):
+                cell(part, group_ref[0] ^ s, k)
+                return 0
+
+            lax.fori_loop(0, 4, some, 0)
 
     def window(m, _):
         for b in range(blocks):
@@ -202,12 +219,42 @@
 
 WIN = 144
 EDGE = 8
+
+
+def widen_kernel(slab_ref, ends_ref, x_ref, o_ref, segment_ref):
+    slab = slab_ref[0]
+    lane = lax.broadcasted_iota(jnp.int32, (WIN, 384), 1)
+
+    def features(g, _):
+        at = pl.ds(pl.multiple_of(384 * g, 128), 384)
+        blocks = [x_ref[4 * g + f].astype(F32) for f in range(4)]
+        for j in range(4):
+            whole = None
+            for f in range(4):
+                s = 96 * ((f - j) % 4)
+                block = blocks[f]
+                if s:
+                    block = jnp.concatenate([block[:, 384 - s :], block[:, : 384 - s]], axis=1)
+                whole = block if whole is None else jnp.where(lane >= 96 * f, block, whole)
+            o_ref[WIN * j : WIN * j + WIN, at] = whole.astype(BF16)
+        return 0
+
+    lax.fori_loop(0, 4, features, 0)
+    for j in range(4):
+        frame = 512 * slab - 4 * EDGE + j + 4 * lax.broadcasted_iota(jnp.int32, (WIN, 128), 0)
+
+        def count(i, number):
+            return number + jnp.where(frame >= ends_ref[i], 1, 0)
+
+        number = lax.fori_loop(0, 32, count, jnp.where(frame >= 0, 0, -1))
+        segment_ref[j] = number.astype(F32)
 
 
 def rest_kernel(
     slab_ref,
     ends_ref,
     x_ref,
+    segment,
     c_ref,
     w_ref,
     gain_ref,
@@ -223,7 +270,7 @@
     carried,
     normed,
     gated,
-    segment,
+    sums,
     swished,
     turned,
     sems,
@@ -268,15 +315,6 @@
     lax.fori_loop(0, 32, fetch, 0)
     lax.fori_loop(0, 32, fetch_glu, 0)
     lax.fori_loop(0, 32, fetch_down, 0)
-
-    for j in range(4):
-        frame = 512 * slab - 4 * EDGE + j + 4 * lax.broadcasted_iota(jnp.int32, (WIN, 128), 0)
-
-        def count(i, number):
-            return number + jnp.where(frame >= ends_ref[i], 1, 0)
-
-        number = lax.fori_loop(0, 32, count, jnp.where(frame >= 0, 0, -1))
-        segment[j] = number.astype(F32)
 
     low = lax.broadcasted_iota(jnp.int32, (WIN, 128), 1) < 64
 
@@ -295,31 +333,11 @@
 
     lax.fori_loop(0, 8, heads, 0)
 
-    lane = lax.broadcasted_iota(jnp.int32, (WIN, 384), 1)
-
-    def features(g, _):
-        at = pl.ds(pl.multiple_of(384 * g, 128), 384)
-        for j in range(4):
-            whole = None
-            for f in range(4):
-                block = x_ref[4 * g + f].astype(F32)
-                s = 96 * ((f - j) % 4)
-                if s:
-                    block = jnp.concatenate([block[:, 384 - s :], block[:, : 384 - s]], axis=1)
-                if whole is None:
-                    whole = block
-                else:
-                    whole = jnp.where(lane >= 96 * f, block, whole)
-            carried[WIN * j : WIN * j + WIN, at] = whole
-        return 0
-
-    lax.fori_loop(0, 4, features, 0)
-
     pltpu.make_async_copy(wo, wo, sems.at[0]).wait()
 
     def project(n, _):
         at = pl.ds(pl.multiple_of(256 * n, 256), 256)
-        carried[:, at] = carried[:, at] + lax.dot_general(
+        carried[:, at] = x_ref[:, at].astype(F32) + lax.dot_general(
             ctx[...], wo[at, :], NT, preferred_element_type=F32
         )
         return 0
@@ -327,14 +345,14 @@
     lax.fori_loop(0, 6, project, 0)
 
     def norm(i, _):
-        at = pl.ds(pl.multiple_of(32 * i, 32), 32)
+        at = pl.ds(pl.multiple_of(16 * i, 16), 16)
         rows = carried[at, :]
         centred = rows - jnp.mean(rows, axis=1, keepdims=True)
         variance = jnp.mean(centred * centred, axis=1, keepdims=True)
         normed[at, :] = (centred * lax.rsqrt(variance + EPS) * gain_ref[...] + bias_ref[...]).astype(BF16)
         return 0
 
-    lax.fori_loop(0, 4 * WIN // 32, norm, 0)
+    lax.fori_loop(0, 4 * WIN // 16, norm, 0, unroll=4)
 
     pltpu.make_async_copy(wg, wg, sems.at[1]).wait()
 
@@ -354,35 +372,42 @@
     lax.fori_loop(0, 6, glu, 0)
 
     def conv(b, _):
-        at = pl.ds(pl.multiple_of(128 * b, 128), 128)
-        taps = taps_ref[:, at]
-        scale = scale_ref[:, at]
-        shift = shift_ref[:, at]
-
-        def chunk(i, _):
-            row = EDGE + i * 8
-            mine = [segment[j, pl.ds(pl.multiple_of(row, 8), 8), :] for j in range(4)]
-            sums = [jnp.zeros((8, 128), F32) for _ in range(4)]
-            for d in range(-4, 5):
-                for p in range(4):
-                    used = [j for j in range(4) if -HALF <= 4 * d + p - j <= HALF]
-                    if not used:
-                        continue
-                    values = gated[b, p, pl.ds(row + d, 8), :]
-                    owner = segment[p, pl.ds(row + d, 8), :]
-                    for j in used:
-                        t = 4 * d + p - j + HALF
-                        sums[j] = sums[j] + jnp.where(owner == mine[j], values, 0.0) * taps[t : t + 1]
-            for j in range(4):
-                affine = sums[j] * scale + shift
-                turned[0, pl.ds(pl.multiple_of(128 * j + 8 * i, 8), 8), :] = affine * jax.nn.sigmoid(affine)
-            return 0
-
-        lax.fori_loop(0, 16, chunk, 0)
-        swished[:, at] = turned[0].astype(BF16)
-        return 0
-
-    lax.fori_loop(0, 12, conv, 0)
+        lanes = [pl.ds(pl.multiple_of(512 * b + 128 * l, 128), 128) for l in range(4)]
+        for first, last in ((-15, -8), (-7, 0), (1, 8), (9, 15)):
+            taps = [
+                {o: jnp.broadcast_to(taps_ref[o + HALF : o + HALF + 1, at], (8, 128)) for o in range(first, last + 1)}
+                for at in lanes
+            ]
+
+            def chunk(i, _):
+                row = EDGE + i * 8
+                for pair in ((0, 1), (2, 3)):
+                    mine = {j: segment[j, pl.ds(pl.multiple_of(row, 8), 8), :] for j in pair}
+                    rows = {j: pl.ds(pl.multiple_of(128 * j + 8 * i, 8), 8) for j in pair}
+                    total = {(l, j): None if first == -15 else sums[l, rows[j], :] for l in range(4) for j in pair}
+                    for e in range(first + pair[0], last + pair[1] + 1):
+                        d, p = e // 4, e % 4
+                        values = [gated[4 * b + l, p, pl.ds(row + d, 8), :] for l in range(4)]
+                        owner = segment[p, pl.ds(row + d, 8), :]
+                        for j in pair:
+                            if not first <= e - j <= last:
+                                continue
+                            same = owner == mine[j]
+                            for l in range(4):
+                                term = jnp.where(same, values[l], 0.0) * taps[l][e - j]
+                                total[l, j] = term if total[l, j] is None else total[l, j] + term
+                    for j in pair:
+                        for l in range(4):
+                            sums[l, rows[j], :] = total[l, j]
+                return 0
+
+            lax.fori_loop(0, 16, chunk, 0)
+        for l, at in enumerate(lanes):
+            affine = sums[l] * scale_ref[:, at] + shift_ref[:, at]
+            swished[:, at] = (affine * jax.nn.sigmoid(affine)).astype(BF16)
+        return 0
+
+    lax.fori_loop(0, 3, conv, 0)
 
     pltpu.make_async_copy(wd, wd, sems.at[2]).wait()
     live = ends_ref[31]
@@ -430,13 +455,14 @@
     rows = q.shape[0]
     return pl.pallas_call(
         attend_kernel,
-        out_shape=jax.ShapeDtypeStruct((32 * CELL, 256), BF16),
+        out_shape=[jax.ShapeDtypeStruct((4 * CELL, 256), BF16)] * 8,
         in_specs=[SMEM, SMEM, SMEM, VMEM, VMEM, VMEM],
-        out_specs=VMEM,
+        out_specs=[VMEM] * 8,
         scratch_shapes=[
             pltpu.VMEM((rows + 136, 128), F32),
             pltpu.VMEM((rows + 136, 128), F32),
             pltpu.VMEM((rows + 136, 128), F32),
+            pltpu.VMEM((32 * CELL, 256), BF16),
             pltpu.SMEM((32,), jnp.int32),
             pltpu.SMEM((32,), jnp.int32),
             pltpu.SMEM((8,), jnp.int32),
@@ -447,25 +473,37 @@
     )(group, lengths, assignment, q, k, v)
 
 
-def compact(width, after, cells, slabs):
+def compact(width, group, after, cells, slabs):
     lanes = 4 * width
     return pl.pallas_call(
         functools.partial(compact_kernel, width),
         out_shape=jax.ShapeDtypeStruct((slabs, WIN, lanes), BF16),
-        in_specs=[SMEM, VMEM],
+        in_specs=[SMEM, SMEM] + [VMEM] * len(cells),
         out_specs=VMEM,
         scratch_shapes=[pltpu.VMEM((lanes // 128, 32 * CELL + 80, 128), F32)],
         compiler_params=pltpu.CompilerParams(vmem_limit_bytes=24 * 1024 * 1024),
         cost_estimate=pl.CostEstimate(flops=20_000_000, bytes_accessed=3_200_000, transcendentals=0),
         name="compact_cells",
-    )(after, cells)
-
-
-def rest(slab, ends, x, c, w, gain, bias, taps, scale, shift):
+    )(group, after, *cells)
+
+
+def widen(slab, ends, x):
+    return pl.pallas_call(
+        widen_kernel,
+        out_shape=[jax.ShapeDtypeStruct((4 * WIN, 1536), BF16), jax.ShapeDtypeStruct((4, WIN, 128), F32)],
+        in_specs=[SMEM, SMEM, VMEM],
+        out_specs=[VMEM, VMEM],
+        compiler_params=pltpu.CompilerParams(vmem_limit_bytes=24 * 1024 * 1024),
+        cost_estimate=pl.CostEstimate(flops=20_000_000, bytes_accessed=4_000_000, transcendentals=0),
+        name="side_by_side",
+    )(slab, ends, x)
+
+
+def rest(slab, ends, x, segment, c, w, gain, bias, taps, scale, shift):
     return pl.pallas_call(
         rest_kernel,
         out_shape=jax.ShapeDtypeStruct((512, 1536), BF16),
-        in_specs=[SMEM, SMEM, VMEM, VMEM, pl.BlockSpec(memory_space=pl.ANY)] + [VMEM] * 5,
+        in_specs=[SMEM, SMEM, VMEM, VMEM, VMEM, pl.BlockSpec(memory_space=pl.ANY)] + [VMEM] * 5,
         out_specs=VMEM,
         scratch_shapes=[
             pltpu.VMEM((1536, 1024), BF16),
@@ -475,7 +513,7 @@
             pltpu.VMEM((4 * WIN, 1536), F32),
             pltpu.VMEM((4 * WIN, 1536), BF16),
             pltpu.VMEM((12, 4, WIN, 128), F32),
-            pltpu.VMEM((4, WIN, 128), F32),
+            pltpu.VMEM((4, 512, 128), F32),
             pltpu.VMEM((512, 1536), BF16),
             pltpu.VMEM((2, 512, 128), F32),
             pltpu.SemaphoreType.DMA((3,)),
@@ -483,7 +521,7 @@
         compiler_params=pltpu.CompilerParams(vmem_limit_bytes=BIG),
         cost_estimate=pl.CostEstimate(flops=9_000_000_000, bytes_accessed=25_000_000, transcendentals=2_000_000),
         name="project_and_convolve",
-    )(slab, ends, x, c, w, gain, bias, taps, scale, shift)
+    )(slab, ends, x, segment, c, w, gain, bias, taps, scale, shift)
 
 
 def target_tables(data_group, lengths, assignment):
@@ -531,29 +569,34 @@
     x_here = lax.all_to_all(
         x_cells.reshape(groups, 4 * CELL, 384), "dp", split_axis=0, concat_axis=0, tiled=True
     )
+    group_later, _ = lax.optimization_barrier((group, x_cells))
     c_cells = attend(
-        group,
+        group_later,
         lengths,
         assignment,
         query_rows.reshape(-1, 128),
         key_rows.reshape(-1, 128),
         value_rows.reshape(-1, 128),
     )
-    c_here = lax.all_to_all(
-        c_cells.reshape(groups, 4 * CELL, 256), "dp", split_axis=0, concat_axis=0, tiled=True
-    )
+    x_here, first_cells = lax.optimization_barrier((x_here, c_cells[0]))
+    c_here = [first_cells] + [
+        lax.ppermute(c_cells[s], "dp", [(i, i ^ s) for i in range(groups)]) for s in range(1, groups)
+    ]
     first, ends = target_tables(data_group, lengths, assignment)
     x_slab = lax.all_to_all(
-        compact(96, first, x_here.reshape(-1, 384), slabs), "mp", split_axis=0, concat_axis=0, tiled=True
+        compact(96, group, first, [x_here.reshape(-1, 384)], slabs), "mp", split_axis=0, concat_axis=0, tiled=True
     )
     c_slab = lax.all_to_all(
-        compact(64, first, c_here.reshape(-1, 256), slabs), "mp", split_axis=0, concat_axis=0, tiled=True
+        compact(64, group, first, c_here, slabs), "mp", split_axis=0, concat_axis=0, tiled=True
     )
+    slab = slab.reshape(1)
+    x_wide, segment = widen(slab, ends, x_slab)
     row = lambda a: a.reshape(1, -1)
     return rest(
-        slab.reshape(1),
+        slab,
         ends,
-        x_slab,
+        x_wide,
+        segment,
         c_slab,
         weights,
         row(norm_gain),

time: 183 us -> 169 us (0.923)
  the two profiles are of different devices: /device:TPU:0 before, /device:TPU:8 now
where the time goes in v2:
time: 169 us; the launch traced here: 168 us
  Pallas kernels  70.6 us (42%)
  waiting for transfers between devices  37.2 us (22%)
  starting transfers between devices  29.3 us (17%)
  local copies, waits for them, and re-layouts  15.8 us (9%)
  between operations  13.7 us (8%)
    pallas_call x1, Pallas kernels, rest(): pl.pallas_call(rest_kernel, out_shape=jax.ShapeDtypeStruct((512, 1536), B...  34.8 us
    pallas_call x1, Pallas kernels, attend(): pl.pallas_call(attend_kernel, out_shape=[jax.ShapeDtypeStruct((4 * CELL,...  17.8 us
    all_to_all x1, waiting for transfers between devices, on_device(): lax.all_to_all(compact(96, group, first, [x_here.reshape(-1, 384)], slabs...  15 us
    ppermute x7, waiting for transfers between devices, on_device(): lax.ppermute(c_cells[s], 'dp', [(i, i ^ s) for i in range(groups)])  11.9 us
    unnamed x58, local copies, waits for them, and re-layouts  11.5 us
    all_to_all x1, waiting for transfers between devices, on_device(): lax.all_to_all(compact(64, group, first, c_here, slabs), 'mp', split_axis...  10.2 us
    pallas_call x2, Pallas kernels, compact(): pl.pallas_call(functools.partial(compact_kernel, width), out_shape=jax.Sh...  9.86 us
    all_to_all x1, starting transfers between devices, on_device(): lax.all_to_all(compact(64, group, first, c_here, slabs), 'mp', split_axis...  9.13 us
  transfers between devices with their start and end apart: 11, of which 7 were waited for; matrix products, arithmetic and copies ran while one was open for 2% of the time, Pallas kernels for 21%

profile of v2, /device:TPU:8, one launch (start us, length us, event | category | flops | bytes accessed | tf_op | source)
XLA Modules:
  0.0 167.8 jit_solution(11248771041100913206)
XLA Ops:
  10.1 4.3 %pack_cells.1 = bf16[2048,384]{1,0:T(8,128)(2,1)S(1)} custom-call(s32[1]{0:T(128)} %bitcast.1.group_ref, s32[256]{0:T(256)S(1)} %copy-done.4, s32[256]{0:T(256)S(1)} %copy-done.5, bf16[2048,384]{1,0:T(8,128)(2,1)S(1)} %bitcast.16), custom_call_target="tpu_custom_call" | custom-call | flops 20000000 | bytes 3200000 | tf_op jit(solution)/shard_map/pack_cells/pallas_call | solution.py:437
  15.6 5.2 %all-to-all-start = ((bf16[8,256,384]{2,1,0:T(8,128)(2,1)}), bf16[8,256,384]{2,1,0:T(8,128)(2,1)S(1)}, u32[]{:S(2)}, u32[]{:S(2)}) async-start(bf16[8,256,384]{2,1,0:T(8,128)(2,1)} %bitcast.15), calls=%async_computation | async-start | bytes 3145728 | tf_op jit(solution)/shard_map/all_to_all | solution.py:569
  21.2 1.3 copy-done.9
  22.5 1.3 copy-done.10
  23.8 17.8 %attend_cells.1 = (bf16[256,256]{1,0:T(8,128)(2,1)S(1)}, bf16[256,256]{1,0:T(8,128)(2,1)S(1)}, bf16[256,256]{1,0:T(8,128)(2,1)S(1)}, bf16[256,256]{1,0:T(8,128)(...) custom-call(s32[1]{0:T(128)} %bitcast.1.group_ref, ...), custom_call_target="tpu_custom_call" | custom-call | flops 2000000000 | bytes 4200000 | tf_op jit(solution)/shard_map/attend_cells/pallas_call | solution.py:456
  45.4 4.7 %compact_cells.2 = bf16[16,144,384]{2,1,0:T(8,128)(2,1)S(1)} custom-call(s32[1]{0:T(128)} %bitcast.1.group_ref, s32[32]{0:T(128)S(1)} %select_reduce_fusion.2.after_ref, bf16[2048,384]{1,0:T(8,128)(2,1)S(1)} %bitcast.14), custom_call_target="tpu_custom_call" | custom-call | flops 20000000 | bytes 3200000 | tf_op jit(solution)/shard_map/compact_cells/pallas_call | solution.py:478
  50.2 1.2 copy-done.1
  51.5 7.9 %all-to-all-start.1 = ((bf16[16,144,384]{2,1,0:T(8,128)(2,1)}), bf16[16,144,384]{2,1,0:T(8,128)(2,1)S(1)}, u32[]{:S(2)}, u32[]{:S(2)}) async-start(bf16[16,144,384]{2,1,0:T(8,128)(2,1)} %copy-done.1), calls=%async_computation.1 | async-start | bytes 3538944 | tf_op jit(solution)/shard_map/all_to_all | solution.py:586
  59.6 1.7 %collective-permute-start.2 = (bf16[256,256]{1,0:T(8,128)(2,1)S(1)}, bf16[256,256]{1,0:T(8,128)(2,1)S(1)}, u32[]{:S(2)}, u32[]{:S(2)}) collective-permute-start(bf16[256,256]{1,0:T(8,128)(2,1)S(1)} %copy-done.21), channel_id=1, source_target_pairs={{0,48},{16,32},{32,16},{48,0},{64,112},{80,96},{96,80},{112,64},{1... | collective-permute-start | bytes 393224 | tf_op jit(solution)/shard_map/ppermute | solution.py:583
  61.3 1.9 %collective-permute-start.3 = (bf16[256,256]{1,0:T(8,128)(2,1)S(1)}, bf16[256,256]{1,0:T(8,128)(2,1)S(1)}, u32[]{:S(2)}, u32[]{:S(2)}) collective-permute-start(bf16[256,256]{1,0:T(8,128)(2,1)S(1)} %copy-done.19), channel_id=1, source_target_pairs={{0,64},{16,80},{32,96},{48,112},{64,0},{80,16},{96,32},{112,48},{1... | collective-permute-start | bytes 393224 | tf_op jit(solution)/shard_map/ppermute | solution.py:583
  63.2 1.3 collective-permute-start.4
  64.6 1.8 %collective-permute-start.5 = (bf16[256,256]{1,0:T(8,128)(2,1)S(1)}, bf16[256,256]{1,0:T(8,128)(2,1)S(1)}, u32[]{:S(2)}, u32[]{:S(2)}) collective-permute-start(bf16[256,256]{1,0:T(8,128)(2,1)S(1)} %copy-done.15), channel_id=1, source_target_pairs={{0,96},{16,112},{32,64},{48,80},{64,32},{80,48},{96,0},{112,16},{1... | collective-permute-start | bytes 393224 | tf_op jit(solution)/shard_map/ppermute | solution.py:583
  66.5 1.2 collective-permute-done.2.rest_3_
  67.7 5.1 %collective-permute-done.3.rest_4_ = bf16[256,256]{1,0:T(8,128)(2,1)S(1)} collective-permute-done((bf16[256,256]{1,0:T(8,128)(2,1)S(1)}, bf16[256,256]{1,0:T(8,128)(2,1)S(1)}, u32[]{:S(2)}, u32[]{:S(2)}) %collective-permute-start.3) | collective-permute-done | bytes 131104 | tf_op jit(solution)/shard_map/ppermute | solution.py:583
  72.8 1.9 %collective-permute-done.4.rest_5_ = bf16[256,256]{1,0:T(8,128)(2,1)S(1)} collective-permute-done((bf16[256,256]{1,0:T(8,128)(2,1)S(1)}, bf16[256,256]{1,0:T(8,128)(2,1)S(1)}, u32[]{:S(2)}, u32[]{:S(2)}) %collective-permute-start.4) | collective-permute-done | bytes 131104 | tf_op jit(solution)/shard_map/ppermute | solution.py:583
  74.6 1.8 %collective-permute-done.5.rest_6_ = bf16[256,256]{1,0:T(8,128)(2,1)S(1)} collective-permute-done((bf16[256,256]{1,0:T(8,128)(2,1)S(1)}, bf16[256,256]{1,0:T(8,128)(2,1)S(1)}, u32[]{:S(2)}, u32[]{:S(2)}) %collective-permute-start.5) | collective-permute-done | bytes 131104 | tf_op jit(solution)/shard_map/ppermute | solution.py:583
  76.5 1.9 %collective-permute-done.6.rest_7_ = bf16[256,256]{1,0:T(8,128)(2,1)S(1)} collective-permute-done((bf16[256,256]{1,0:T(8,128)(2,1)S(1)}, bf16[256,256]{1,0:T(8,128)(2,1)S(1)}, u32[]{:S(2)}, u32[]{:S(2)}) %collective-permute-start.6) | collective-permute-done | bytes 131104 | tf_op jit(solution)/shard_map/ppermute | solution.py:583
  78.4 5.1 %compact_cells.3 = bf16[16,144,256]{2,1,0:T(8,128)(2,1)} custom-call(s32[1]{0:T(128)} %bitcast.1.group_ref, s32[32]{0:T(128)S(1)} %select_reduce_fusion.2.after_ref, bf16[256,256]{1,0:T(8,128)(2,1)S(1)} %get-tuple-element.23.rest_0_, bf16[256,256]{1,0:T(8,128)(2,1)S(1)} %collective-permute-done.rest_1_, bf16[256,256]{1,0:T(8,128)(2,1)S(1)} %collective-permute-done.1.rest_2_, ...), custom_call_target="tpu_custom_call" | custom-call | flops 20000000 | bytes 3200000 | tf_op jit(solution)/shard_map/compact_cells/pallas_call | solution.py:478
  83.5 15.0 %all-to-all-done.1.x_ref = bf16[16,144,384]{2,1,0:T(8,128)(2,1)S(1)} async-done(((bf16[16,144,384]{2,1,0:T(8,128)(2,1)}), bf16[16,144,384]{2,1,0:T(8,128)(2,1)S(1)}, u32[]{:S(2)}, u32[]{:S(2)}) %all-to-all-start.1) | async-done | bytes 1769504 | tf_op jit(solution)/shard_map/all_to_all | solution.py:586
  98.6 9.1 %all-to-all-start.2 = ((bf16[16,144,256]{2,1,0:T(8,128)(2,1)}), bf16[16,144,256]{2,1,0:T(8,128)(2,1)}, u32[]{:S(2)}, u32[]{:S(2)}) async-start(bf16[16,144,256]{2,1,0:T(8,128)(2,1)} %compact_cells.3), calls=%async_computation.2 | async-start | bytes 2359296 | tf_op jit(solution)/shard_map/all_to_all | solution.py:589
  110.1 3.8 %side_by_side.1 = (bf16[576,1536]{1,0:T(8,128)(2,1)S(1)}, f32[4,144,128]{2,1,0:T(8,128)S(1)}) custom-call(s32[1]{0:T(128)} %bitcast.slab_ref, s32[32]{0:T(128)S(1)} %add.16.ends_ref, bf16[16,144,384]{2,1,0:T(8,128)(2,1)S(1)} %all-to-all-done.1.x_ref), custom_call_target="tpu_custom_call" | custom-call | flops 20000000 | bytes 4000000 | tf_op jit(solution)/shard_map/side_by_side/pallas_call | solution.py:491
  113.9 1.2 copy-done.7
  115.9 10.2 %all-to-all-done.2.c_ref = bf16[16,144,256]{2,1,0:T(8,128)(2,1)} async-done(((bf16[16,144,256]{2,1,0:T(8,128)(2,1)}), bf16[16,144,256]{2,1,0:T(8,128)(2,1)}, u32[]{:S(2)}, u32[]{:S(2)}) %all-to-all-start.2) | async-done | bytes 1179680 | tf_op jit(solution)/shard_map/all_to_all | solution.py:589
  126.1 34.8 %project_and_convolve.1 = bf16[512,1536]{1,0:T(8,128)(2,1)} custom-call(s32[1]{0:T(128)} %bitcast.slab_ref, s32[32]{0:T(128)} %copy-done.6, bf16[576,1536]{1,0:T(8,128)(2,1)} %copy-done.7, f32[4,144,128]{2,1,0:T(8,128)} %copy-done.11, bf16[16,144,256]{2,1,0:T(8,128)(2,1)} %all-to-all-done.2.c_ref, bf16[5632,1536]{1,0:T(8,128)(2,1)} %all-gather.2.cloned.1.call-done.w_ref, ...), custom_call_target="tpu_custom_call" | custom-call | flops 8999999488 | bytes 25000000 | tf_op jit(solution)/shard_map/project_and_convolve/pallas_call | solution.py:503
  (77 shorter events, 12.4 us)
Async XLA Ops:
  6.5 119.6 %all-gather.2.cloned.1.call-start = ((), (), s32[]{:S(2)}) async-start(), calls=%async_computation.3 | async-start | bytes 17842176 | tf_op jit(solution)/shard_map/all_gather | solution.py:565
  15.6 5.6 %copy-start.8 = (bf16[4096,1,128]{2,0,1:T(8,128)(2,1)S(1)}, bf16[4096,1,128]{2,0,1:T(8,128)(2,1)}, u32[]{:S(2)}) copy-start(bf16[4096,1,128]{2,0,1:T(8,128)(2,1)} %param.14) | copy-start | bytes 3145732
  15.6 29.9 %all-to-all-start = ((bf16[8,256,384]{2,1,0:T(8,128)(2,1)}), bf16[8,256,384]{2,1,0:T(8,128)(2,1)S(1)}, u32[]{:S(2)}, u32[]{:S(2)}) async-start(bf16[8,256,384]{2,1,0:T(8,128)(2,1)} %bitcast.15), calls=%async_computation | async-start | bytes 3145728 | tf_op jit(solution)/shard_map/all_to_all | solution.py:569
  45.4 4.7 %copy-start.24 = (bf16[256,256]{1,0:T(8,128)(2,1)}, bf16[256,256]{1,0:T(8,128)(2,1)S(1)}, u32[]{:S(2)}) copy-start(bf16[256,256]{1,0:T(8,128)(2,1)S(1)} %get-tuple-element.24) | copy-start | bytes 393220
  51.4 8.0 %copy-start.23 = (bf16[256,256]{1,0:T(8,128)(2,1)S(1)}, bf16[256,256]{1,0:T(8,128)(2,1)}, u32[]{:S(2)}) copy-start(bf16[256,256]{1,0:T(8,128)(2,1)} %copy-done.22) | copy-start | bytes 393220
  51.4 8.2 %copy-start.21 = (bf16[256,256]{1,0:T(8,128)(2,1)S(1)}, bf16[256,256]{1,0:T(8,128)(2,1)}, u32[]{:S(2)}) copy-start(bf16[256,256]{1,0:T(8,128)(2,1)} %copy-done.20) | copy-start | bytes 393220
  51.4 9.9 %copy-start.19 = (bf16[256,256]{1,0:T(8,128)(2,1)S(1)}, bf16[256,256]{1,0:T(8,128)(2,1)}, u32[]{:S(2)}) copy-start(bf16[256,256]{1,0:T(8,128)(2,1)} %copy-done.18) | copy-start | bytes 393220
  51.4 11.8 %copy-start.17 = (bf16[256,256]{1,0:T(8,128)(2,1)S(1)}, bf16[256,256]{1,0:T(8,128)(2,1)}, u32[]{:S(2)}) copy-start(bf16[256,256]{1,0:T(8,128)(2,1)} %copy-done.16) | copy-start | bytes 393220
  51.4 13.1 %copy-start.15 = (bf16[256,256]{1,0:T(8,128)(2,1)S(1)}, bf16[256,256]{1,0:T(8,128)(2,1)}, u32[]{:S(2)}) copy-start(bf16[256,256]{1,0:T(8,128)(2,1)} %copy-done.14) | copy-start | bytes 393220
  51.4 14.9 %copy-start.13 = (bf16[256,256]{1,0:T(8,128)(2,1)S(1)}, bf16[256,256]{1,0:T(8,128)(2,1)}, u32[]{:S(2)}) copy-start(bf16[256,256]{1,0:T(8,128)(2,1)} %copy-done.12) | copy-start | bytes 393220
  51.5 47.1 %all-to-all-start.1 = ((bf16[16,144,384]{2,1,0:T(8,128)(2,1)}), bf16[16,144,384]{2,1,0:T(8,128)(2,1)S(1)}, u32[]{:S(2)}, u32[]{:S(2)}) async-start(bf16[16,144,384]{2,1,0:T(8,128)(2,1)} %copy-done.1), calls=%async_computation.1 | async-start | bytes 3538944 | tf_op jit(solution)/shard_map/all_to_all | solution.py:586
  59.4 5.2 %collective-permute-start = (bf16[256,256]{1,0:T(8,128)(2,1)}, bf16[256,256]{1,0:T(8,128)(2,1)S(1)}, u32[]{:S(2)}, u32[]{:S(2)}) collective-permute-start(bf16[256,256]{1,0:T(8,128)(2,1)} %copy-done.24), channel_id=1, source_target_pairs={{0,16},{16,0},{32,48},{48,32},{64,80},{80,64},{96,112},{112,96},{1... | collective-permute-start | bytes 393224 | tf_op jit(solution)/shard_map/ppermute | solution.py:583
  59.5 6.9 %collective-permute-start.1 = (bf16[256,256]{1,0:T(8,128)(2,1)S(1)}, bf16[256,256]{1,0:T(8,128)(2,1)S(1)}, u32[]{:S(2)}, u32[]{:S(2)}) collective-permute-start(bf16[256,256]{1,0:T(8,128)(2,1)S(1)} %copy-done.23), channel_id=1, source_target_pairs={{0,32},{16,48},{32,0},{48,16},{64,96},{80,112},{96,64},{112,80},{1... | collective-permute-start | bytes 393224 | tf_op jit(solution)/shard_map/ppermute | solution.py:583
  59.6 8.1 %collective-permute-start.2 = (bf16[256,256]{1,0:T(8,128)(2,1)S(1)}, bf16[256,256]{1,0:T(8,128)(2,1)S(1)}, u32[]{:S(2)}, u32[]{:S(2)}) collective-permute-start(bf16[256,256]{1,0:T(8,128)(2,1)S(1)} %copy-done.21), channel_id=1, source_target_pairs={{0,48},{16,32},{32,16},{48,0},{64,112},{80,96},{96,80},{112,64},{1... | collective-permute-start | bytes 393224 | tf_op jit(solution)/shard_map/ppermute | solution.py:583
  61.3 11.4 %collective-permute-start.3 = (bf16[256,256]{1,0:T(8,128)(2,1)S(1)}, bf16[256,256]{1,0:T(8,128)(2,1)S(1)}, u32[]{:S(2)}, u32[]{:S(2)}) collective-permute-start(bf16[256,256]{1,0:T(8,128)(2,1)S(1)} %copy-done.19), channel_id=1, source_target_pairs={{0,64},{16,80},{32,96},{48,112},{64,0},{80,16},{96,32},{112,48},{1... | collective-permute-start | bytes 393224 | tf_op jit(solution)/shard_map/ppermute | solution.py:583
  63.2 11.4 %collective-permute-start.4 = (bf16[256,256]{1,0:T(8,128)(2,1)S(1)}, bf16[256,256]{1,0:T(8,128)(2,1)S(1)}, u32[]{:S(2)}, u32[]{:S(2)}) collective-permute-start(bf16[256,256]{1,0:T(8,128)(2,1)S(1)} %copy-done.17), channel_id=1, source_target_pairs={{0,80},{16,64},{32,112},{48,96},{64,16},{80,0},{96,48},{112,32},{1... | collective-permute-start | bytes 393224 | tf_op jit(solution)/shard_map/ppermute | solution.py:583
  64.6 11.9 %collective-permute-start.5 = (bf16[256,256]{1,0:T(8,128)(2,1)S(1)}, bf16[256,256]{1,0:T(8,128)(2,1)S(1)}, u32[]{:S(2)}, u32[]{:S(2)}) collective-permute-start(bf16[256,256]{1,0:T(8,128)(2,1)S(1)} %copy-done.15), channel_id=1, source_target_pairs={{0,96},{16,112},{32,64},{48,80},{64,32},{80,48},{96,0},{112,16},{1... | collective-permute-start | bytes 393224 | tf_op jit(solution)/shard_map/ppermute | solution.py:583
  66.3 12.1 %collective-permute-start.6 = (bf16[256,256]{1,0:T(8,128)(2,1)S(1)}, bf16[256,256]{1,0:T(8,128)(2,1)S(1)}, u32[]{:S(2)}, u32[]{:S(2)}) collective-permute-start(bf16[256,256]{1,0:T(8,128)(2,1)S(1)} %copy-done.13), channel_id=1, source_target_pairs={{0,112},{16,96},{32,80},{48,64},{64,48},{80,32},{96,16},{112,0},{1... | collective-permute-start | bytes 393224 | tf_op jit(solution)/shard_map/ppermute | solution.py:583
  83.5 24.2 %copy-start.25 = (f32[1536]{0:T(1024)S(1)}, f32[1536]{0:T(1024)}, u32[]{:S(2)}) copy-start(f32[1536]{0:T(1024)} %param.21) | copy-start | bytes 18436
  83.5 24.8 %copy-start.26 = (f32[1536]{0:T(1024)S(1)}, f32[1536]{0:T(1024)}, u32[]{:S(2)}) copy-start(f32[1536]{0:T(1024)} %param.22) | copy-start | bytes 18436
  83.5 25.4 %copy-start.27 = (f32[1536]{0:T(1024)S(1)}, f32[1536]{0:T(1024)}, u32[]{:S(2)}) copy-start(f32[1536]{0:T(1024)} %param.25) | copy-start | bytes 18436
  83.5 26.0 %copy-start.28 = (f32[1536]{0:T(1024)S(1)}, f32[1536]{0:T(1024)}, u32[]{:S(2)}) copy-start(f32[1536]{0:T(1024)} %param.26) | copy-start | bytes 18436
  98.6 27.5 %all-to-all-start.2 = ((bf16[16,144,256]{2,1,0:T(8,128)(2,1)}), bf16[16,144,256]{2,1,0:T(8,128)(2,1)}, u32[]{:S(2)}, u32[]{:S(2)}) async-start(bf16[16,144,256]{2,1,0:T(8,128)(2,1)} %compact_cells.3), calls=%async_computation.2 | async-start | bytes 2359296 | tf_op jit(solution)/shard_map/all_to_all | solution.py:589
  107.7 18.4 %copy-start.6 = (s32[32]{0:T(128)}, s32[32]{0:T(128)S(1)}, u32[]{:S(2)}) copy-start(s32[32]{0:T(128)S(1)} %add.16.ends_ref) | copy-start | bytes 388
  (16 other events, 17.6 us)
Sparse Core Ops, SparseCore 0:
  9.7 95.0 all-gather.1

commit v3 on v2

--- a/solution.py
+++ b/solution.py
@@ -38,7 +38,13 @@
     lax.fori_loop(0, per_group, step, jnp.int32(0))
 
 
-def pack_kernel(group_ref, lengths_ref, assignment_ref, x_ref, o_ref, flat, start_ref, size_ref, seen_ref):
+def turn(x, s):
+    return jnp.concatenate([x[:, s:], x[:, :s]], axis=1)
+
+
+def pack_kernel(
+    group_ref, lengths_ref, assignment_ref, x_ref, o_ref, flat, packed, start_ref, size_ref, seen_ref, sem
+):
     cell_tables(group_ref[0], lengths_ref, assignment_ref, start_ref, size_ref, seen_ref)
     rows = x_ref.shape[0]
 
@@ -54,31 +60,33 @@
     lane = lax.broadcasted_iota(jnp.int32, (CELL, 384), 1)
     frame = 4 * lax.broadcasted_iota(jnp.int32, (CELL, 384), 0) + lane // 96
 
-    def cell(c, _):
+    def cell(c):
         b = start_ref[c]
-        n = size_ref[c]
         row = b // 4
         phase = b - 4 * row
         now = jnp.concatenate([flat[i, pl.ds(row, CELL), :] for i in range(3)], axis=1)
         later = jnp.concatenate([flat[i, pl.ds(row + 1, CELL), :] for i in range(3)], axis=1)
-        at = pl.multiple_of(c * CELL, CELL)
-        for p in range(4):
-
-            @pl.when(phase == p)
-            def _():
-                mixed = now if p == 0 else jnp.where(lane >= 96 * p, now, later)
-                moved = mixed if p == 0 else jnp.concatenate([mixed[:, 96 * p :], mixed[:, : 96 * p]], axis=1)
-                o_ref[pl.ds(at, CELL), :] = jnp.where(frame < n, moved, 0.0).astype(BF16)
-
-        return 0
-
-    lax.fori_loop(0, 32, cell, 0)
+        mixed = jnp.where(lane >= 96 * phase, now, later)
+        mixed = jnp.where(phase >= 2, turn(mixed, 192), mixed)
+        mixed = jnp.where(phase % 2 == 1, turn(mixed, 96), mixed)
+        return jnp.where(frame < size_ref[c], mixed, 0.0).astype(BF16)
+
+    def target(t, _):
+        parts = [cell(4 * t + k) for k in range(4)]
+        at = pl.multiple_of(4 * CELL * t, 4 * CELL)
+        for k, part in enumerate(parts):
+            packed[pl.ds(at + k * CELL, CELL), :] = part
+        pltpu.make_async_copy(packed.at[pl.ds(at, 4 * CELL), :], o_ref.at[pl.ds(at, 4 * CELL), :], sem).start()
+        return 0
+
+    lax.fori_loop(0, 8, target, 0)
+    pltpu.make_async_copy(packed, o_ref, sem).wait()
 
 
 def attend_kernel(
     group_ref, lengths_ref, assignment_ref, q_ref, k_ref, v_ref, *rest
 ):
-    outs, (qf, kf, vf, o_ref, start_ref, size_ref, seen_ref) = rest[:8], rest[8:]
+    outs, (qf, kf, vf, o_ref, start_ref, size_ref, seen_ref, sem) = rest[:8], rest[8:]
     cell_tables(group_ref[0], lengths_ref, assignment_ref, start_ref, size_ref, seen_ref)
     rows = q_ref.shape[0]
 
@@ -112,7 +120,7 @@
             [jnp.where(swap, second, first), jnp.where(swap, first, second)], axis=0
         ).astype(BF16)
 
-    def cell(c):
+    def scored(c):
         b = start_ref[c]
         n = size_ref[c]
         row = b // 2
@@ -133,12 +141,16 @@
         ).astype(BF16)
         keys = doubled(kf, row, shift)
         values = doubled(vf, row, shift)
-        scores = lax.dot_general(queries, keys, NT, preferred_element_type=F32)
+        return n, values, lax.dot_general(queries, keys, NT, preferred_element_type=F32)
+
+    def weighted(n, scores):
         scores = jnp.where(key_frame < n, scores, MASKED)
         exponentials = jnp.exp(scores - jnp.max(scores, axis=1, keepdims=True))
         total = jnp.sum(exponentials, axis=1, keepdims=True)
-        weights = (exponentials / total).astype(BF16)
-        context = jnp.dot(weights, values, preferred_element_type=F32)
+        return exponentials.astype(BF16), total
+
+    def store(c, n, values, exponentials, total):
+        context = jnp.dot(exponentials, values, preferred_element_type=F32) * (1.0 / total)
         at = pl.multiple_of(c * CELL, CELL)
         first = jnp.where(low, context[0:64], context[64:128])
         second = jnp.where(low, context[128:192], context[192:256])
@@ -146,18 +158,26 @@
         o_ref[pl.ds(at, CELL), 128:256] = jnp.where(frame + 2 < n, second, 0.0).astype(BF16)
 
     def some(i, _):
-        cell(2 * i)
-        cell(2 * i + 1)
-        return 0
-
-    lax.fori_loop(0, 16, some, 0)
+        cells = [4 * i + c for c in range(4)]
+        work = [scored(c) for c in cells]
+        shares = [weighted(n, scores) for n, _, scores in work]
+        for c, (n, values, _), share in zip(cells, work, shares):
+            store(c, n, values, *share)
+        return 0
+
+    lax.fori_loop(0, 8, some, 0)
+    copies = []
     for s in range(8):
         at = pl.multiple_of((group_ref[0] ^ s) * 4 * CELL, 4 * CELL)
-        outs[s][...] = o_ref[pl.ds(at, 4 * CELL), :]
-
-
-def compact_kernel(width, group_ref, after_ref, *rest):
-    parts, (o_ref, flat) = rest[:-2], rest[-2:]
+        copies.append(pltpu.make_async_copy(o_ref.at[pl.ds(at, 4 * CELL), :], outs[s], sem.at[s]))
+    for copy in copies:
+        copy.start()
+    for copy in copies:
+        copy.wait()
+
+
+def compact_kernel(width, offset, count, group_ref, after_ref, *rest):
+    parts, (o_ref, flat, windows, sem) = rest[:count], rest[-4:]
     lanes = 4 * width
     blocks = lanes // 128
     total = flat.shape[1]
@@ -169,93 +189,57 @@
             flat[b, pl.ds(r, 16), :] = jnp.zeros((16, 128), F32)
         return 0
 
-    lax.fori_loop(0, total // 16, clear, 0)
+    lax.fori_loop(0, total // 16, clear, 0, unroll=7)
     lane = lax.broadcasted_iota(jnp.int32, (CELL, lanes), 1)
 
-    def cell(x_ref, from_group, k):
-        first = after_ref[4 * from_group + k]
+    def cell(block, first):
         row = first // 4
         phase = first - 4 * row
-        block = x_ref[pl.ds(pl.multiple_of(k * CELL, CELL), CELL), :].astype(F32)
-        for p in range(4):
-
-            @pl.when(phase == p)
-            def _():
-                s = p * width
-                moved = block if p == 0 else jnp.concatenate([block[:, lanes - s :], block[:, : lanes - s]], axis=1)
-                here = moved if p == 0 else jnp.where(lane >= s, moved, 0.0)
-                for b in range(blocks):
-                    at = (b, pl.ds(row + 8, CELL), slice(None))
-                    flat[at] = flat[at] + here[:, 128 * b : 128 * b + 128]
-                if p > 0:
-                    below = jnp.where(lane >= s, 0.0, moved)
-                    for b in range((s + 127) // 128):
-                        at = (b, pl.ds(row + 9, CELL), slice(None))
-                        flat[at] = flat[at] + below[:, 128 * b : 128 * b + 128]
-
-    if len(parts) == 1:
-
-        def whole(c, _):
-            cell(parts[0], 0, c)
+        block = block.astype(F32)
+        block = jnp.where(phase >= 2, turn(block, lanes - 2 * width), block)
+        block = jnp.where(phase % 2 == 1, turn(block, lanes - width), block)
+        own = lane >= phase * width
+        return row, jnp.where(own, block, 0.0), jnp.where(own, 0.0, block)
+
+    def four(x_ref, at, u):
+        moved = [cell(x_ref[pl.ds(at + k * CELL, CELL), :], after_ref[u + k]) for k in range(4)]
+        for row, here, below in moved:
+            for b in range(blocks):
+                at = (b, pl.ds(row + 8, CELL), slice(None))
+                flat[at] = flat[at] + here[:, 128 * b : 128 * b + 128]
+            for b in range(blocks):
+                at = (b, pl.ds(row + 9, CELL), slice(None))
+                flat[at] = flat[at] + below[:, 128 * b : 128 * b + 128]
+
+    if count == 1:
+
+        def some(d, _):
+            four(parts[0], pl.multiple_of(4 * CELL * d, 4 * CELL), 4 * d)
             return 0
 
-        lax.fori_loop(0, 32, whole, 0)
+        lax.fori_loop(0, 8, some, 0)
     else:
         for s, part in enumerate(parts):
-
-            def some(k, _):
-                cell(part, group_ref[0] ^ s, k)
-                return 0
-
-            lax.fori_loop(0, 4, some, 0)
+            four(part, 0, 4 * (group_ref[0] ^ s))
 
     def window(m, _):
         for b in range(blocks):
-            o_ref[m, :, 128 * b : 128 * b + 128] = flat[b, pl.ds(pl.multiple_of(m * 128, 128), 144), :].astype(BF16)
+            windows[m, :, 128 * b : 128 * b + 128] = flat[b, pl.ds(pl.multiple_of(m * 128, 128), 144), :].astype(BF16)
+        pltpu.make_async_copy(windows.at[m], o_ref.at[m, :, pl.ds(offset, lanes)], sem).start()
         return 0
 
     lax.fori_loop(0, slabs, window, 0)
+    pltpu.make_async_copy(windows, o_ref.at[:, :, pl.ds(offset, lanes)], sem).wait()
 
 
 WIN = 144
 EDGE = 8
-
-
-def widen_kernel(slab_ref, ends_ref, x_ref, o_ref, segment_ref):
-    slab = slab_ref[0]
-    lane = lax.broadcasted_iota(jnp.int32, (WIN, 384), 1)
-
-    def features(g, _):
-        at = pl.ds(pl.multiple_of(384 * g, 128), 384)
-        blocks = [x_ref[4 * g + f].astype(F32) for f in range(4)]
-        for j in range(4):
-            whole = None
-            for f in range(4):
-                s = 96 * ((f - j) % 4)
-                block = blocks[f]
-                if s:
-                    block = jnp.concatenate([block[:, 384 - s :], block[:, : 384 - s]], axis=1)
-                whole = block if whole is None else jnp.where(lane >= 96 * f, block, whole)
-            o_ref[WIN * j : WIN * j + WIN, at] = whole.astype(BF16)
-        return 0
-
-    lax.fori_loop(0, 4, features, 0)
-    for j in range(4):
-        frame = 512 * slab - 4 * EDGE + j + 4 * lax.broadcasted_iota(jnp.int32, (WIN, 128), 0)
-
-        def count(i, number):
-            return number + jnp.where(frame >= ends_ref[i], 1, 0)
-
-        number = lax.fori_loop(0, 32, count, jnp.where(frame >= 0, 0, -1))
-        segment_ref[j] = number.astype(F32)
 
 
 def rest_kernel(
     slab_ref,
     ends_ref,
     x_ref,
-    segment,
-    c_ref,
     w_ref,
     gain_ref,
     bias_ref,
@@ -270,6 +254,7 @@
     carried,
     normed,
     gated,
+    segment,
     sums,
     swished,
     turned,
@@ -290,16 +275,19 @@
             ).start()
         return 0
 
-    def fetch_glu(g, _):
-        c = g // 16
-        m = g - 16 * c
-        base = pl.multiple_of(g * piece + 32, 16)
-        pltpu.make_async_copy(
-            w_ref.at[pl.ds(base, 96), :],
-            wg.at[pl.ds(pl.multiple_of(192 * m + 96 * c, 16), 96), :],
-            sems.at[1],
-        ).start()
-        return 0
+    def fetch_glu(half):
+        def one(i, _):
+            c = i // 8
+            m = 4 * half + i % 4 + 8 * ((i // 4) % 2)
+            base = pl.multiple_of((16 * c + m) * piece + 32, 16)
+            pltpu.make_async_copy(
+                w_ref.at[pl.ds(base, 96), :],
+                wg.at[pl.ds(pl.multiple_of(192 * m + 96 * c, 16), 96), :],
+                sems.at[1 + half],
+            ).start()
+            return 0
+
+        lax.fori_loop(0, 16, one, 0)
 
     def fetch_down(g, _):
         c = g // 16
@@ -308,22 +296,49 @@
         pltpu.make_async_copy(
             w_ref.at[pl.ds(base, 48), :],
             wd.at[pl.ds(pl.multiple_of(96 * m + 48 * c, 16), 48), :],
-            sems.at[2],
+            sems.at[3],
         ).start()
         return 0
 
     lax.fori_loop(0, 32, fetch, 0)
-    lax.fori_loop(0, 32, fetch_glu, 0)
+    fetch_glu(0)
+    fetch_glu(1)
     lax.fori_loop(0, 32, fetch_down, 0)
+
+    for j in range(4):
+        frame = 512 * slab - 4 * EDGE + j + 4 * lax.broadcasted_iota(jnp.int32, (WIN, 128), 0)
+
+        def count(i, number):
+            return number + jnp.where(frame >= ends_ref[i], 1, 0)
+
+        number = lax.fori_loop(0, 32, count, jnp.where(frame >= 0, 0, -1), unroll=4)
+        segment[j] = number.astype(F32)
+
+    lane = lax.broadcasted_iota(jnp.int32, (WIN, 384), 1)
+
+    def features(g, _):
+        at = pl.ds(pl.multiple_of(384 * g, 128), 384)
+        for j in range(4):
+            whole = None
+            for f in range(4):
+                s = 96 * ((f - j) % 4)
+                block = x_ref[4 * g + f, :, 0:384]
+                if s:
+                    block = turn(block, 384 - s)
+                whole = block if whole is None else jnp.where(lane >= 96 * f, block, whole)
+            carried[WIN * j : WIN * j + WIN, at] = whole.astype(F32)
+        return 0
+
+    lax.fori_loop(0, 4, features, 0)
 
     low = lax.broadcasted_iota(jnp.int32, (WIN, 128), 1) < 64
 
     def heads(h, _):
         at = pl.ds(pl.multiple_of(128 * h, 128), 128)
         for j in range(4):
-            part = slice(128 * (j // 2), 128 * (j // 2) + 128)
-            left = c_ref[2 * h, :, part].astype(F32)
-            right = c_ref[2 * h + 1, :, part].astype(F32)
+            part = slice(384 + 128 * (j // 2), 512 + 128 * (j // 2))
+            left = x_ref[2 * h, :, part].astype(F32)
+            right = x_ref[2 * h + 1, :, part].astype(F32)
             if j % 2 == 0:
                 right = pltpu.roll(right, 64, 1)
             else:
@@ -337,7 +352,7 @@
 
     def project(n, _):
         at = pl.ds(pl.multiple_of(256 * n, 256), 256)
-        carried[:, at] = x_ref[:, at].astype(F32) + lax.dot_general(
+        carried[:, at] = carried[:, at] + lax.dot_general(
             ctx[...], wo[at, :], NT, preferred_element_type=F32
         )
         return 0
@@ -353,8 +368,6 @@
         return 0
 
     lax.fori_loop(0, 4 * WIN // 16, norm, 0, unroll=4)
-
-    pltpu.make_async_copy(wg, wg, sems.at[1]).wait()
 
     def glu(n, _):
         value = lax.dot_general(
@@ -369,7 +382,10 @@
                 gated[2 * n + b, j] = out[WIN * j : WIN * j + WIN, 128 * b : 128 * b + 128]
         return 0
 
-    lax.fori_loop(0, 6, glu, 0)
+    for half in range(2):
+        part = wg.at[pl.ds(0, 1536), :]
+        pltpu.make_async_copy(part, part, sems.at[1 + half]).wait()
+        lax.fori_loop(3 * half, 3 * half + 3, glu, 0)
 
     def conv(b, _):
         lanes = [pl.ds(pl.multiple_of(512 * b + 128 * l, 128), 128) for l in range(4)]
@@ -409,7 +425,7 @@
 
     lax.fori_loop(0, 3, conv, 0)
 
-    pltpu.make_async_copy(wd, wd, sems.at[2]).wait()
+    pltpu.make_async_copy(wd, wd, sems.at[3]).wait()
     live = ends_ref[31]
 
     def down(n, _):
@@ -427,6 +443,7 @@
     lax.fori_loop(0, 6, down, 0)
 
 
+HBM = pl.BlockSpec(memory_space=pltpu.HBM)
 SMEM = pl.BlockSpec(memory_space=pltpu.SMEM)
 VMEM = pl.BlockSpec(memory_space=pltpu.VMEM)
 BIG = 60 * 1024 * 1024
@@ -438,12 +455,14 @@
         pack_kernel,
         out_shape=jax.ShapeDtypeStruct((32 * CELL, 384), BF16),
         in_specs=[SMEM, SMEM, SMEM, VMEM],
-        out_specs=VMEM,
+        out_specs=HBM,
         scratch_shapes=[
             pltpu.VMEM((3, rows + 72, 128), F32),
+            pltpu.VMEM((32 * CELL, 384), BF16),
             pltpu.SMEM((32,), jnp.int32),
             pltpu.SMEM((32,), jnp.int32),
             pltpu.SMEM((8,), jnp.int32),
+            pltpu.SemaphoreType.DMA,
         ],
         compiler_params=pltpu.CompilerParams(vmem_limit_bytes=24 * 1024 * 1024),
         cost_estimate=pl.CostEstimate(flops=20_000_000, bytes_accessed=3_200_000, transcendentals=0),
@@ -457,7 +476,7 @@
         attend_kernel,
         out_shape=[jax.ShapeDtypeStruct((4 * CELL, 256), BF16)] * 8,
         in_specs=[SMEM, SMEM, SMEM, VMEM, VMEM, VMEM],
-        out_specs=[VMEM] * 8,
+        out_specs=[HBM] * 8,
         scratch_shapes=[
             pltpu.VMEM((rows + 136, 128), F32),
             pltpu.VMEM((rows + 136, 128), F32),
@@ -466,6 +485,7 @@
             pltpu.SMEM((32,), jnp.int32),
             pltpu.SMEM((32,), jnp.int32),
             pltpu.SMEM((8,), jnp.int32),
+            pltpu.SemaphoreType.DMA((8,)),
         ],
         compiler_params=pltpu.CompilerParams(vmem_limit_bytes=32 * 1024 * 1024),
         cost_estimate=pl.CostEstimate(flops=2_000_000_000, bytes_accessed=4_200_000, transcendentals=2_000_000),
@@ -473,37 +493,30 @@
     )(group, lengths, assignment, q, k, v)
 
 
-def compact(width, group, after, cells, slabs):
+def compact(width, offset, group, after, cells, slabs, onto=None):
     lanes = 4 * width
     return pl.pallas_call(
-        functools.partial(compact_kernel, width),
-        out_shape=jax.ShapeDtypeStruct((slabs, WIN, lanes), BF16),
-        in_specs=[SMEM, SMEM] + [VMEM] * len(cells),
-        out_specs=VMEM,
-        scratch_shapes=[pltpu.VMEM((lanes // 128, 32 * CELL + 80, 128), F32)],
+        functools.partial(compact_kernel, width, offset, len(cells)),
+        out_shape=jax.ShapeDtypeStruct((slabs, WIN, 640), BF16),
+        in_specs=[SMEM, SMEM] + [VMEM] * len(cells) + ([] if onto is None else [HBM]),
+        out_specs=HBM,
+        scratch_shapes=[
+            pltpu.VMEM((lanes // 128, 32 * CELL + 80, 128), F32),
+            pltpu.VMEM((slabs, WIN, lanes), BF16),
+            pltpu.SemaphoreType.DMA,
+        ],
+        input_output_aliases={} if onto is None else {2 + len(cells): 0},
         compiler_params=pltpu.CompilerParams(vmem_limit_bytes=24 * 1024 * 1024),
         cost_estimate=pl.CostEstimate(flops=20_000_000, bytes_accessed=3_200_000, transcendentals=0),
         name="compact_cells",
-    )(group, after, *cells)
-
-
-def widen(slab, ends, x):
-    return pl.pallas_call(
-        widen_kernel,
-        out_shape=[jax.ShapeDtypeStruct((4 * WIN, 1536), BF16), jax.ShapeDtypeStruct((4, WIN, 128), F32)],
-        in_specs=[SMEM, SMEM, VMEM],
-        out_specs=[VMEM, VMEM],
-        compiler_params=pltpu.CompilerParams(vmem_limit_bytes=24 * 1024 * 1024),
-        cost_estimate=pl.CostEstimate(flops=20_000_000, bytes_accessed=4_000_000, transcendentals=0),
-        name="side_by_side",
-    )(slab, ends, x)
-
-
-def rest(slab, ends, x, segment, c, w, gain, bias, taps, scale, shift):
+    )(group, after, *cells, *([] if onto is None else [onto]))
+
+
+def rest(slab, ends, x, w, gain, bias, taps, scale, shift):
     return pl.pallas_call(
         rest_kernel,
         out_shape=jax.ShapeDtypeStruct((512, 1536), BF16),
-        in_specs=[SMEM, SMEM, VMEM, VMEM, VMEM, pl.BlockSpec(memory_space=pl.ANY)] + [VMEM] * 5,
+        in_specs=[SMEM, SMEM, VMEM, HBM] + [VMEM] * 5,
         out_specs=VMEM,
         scratch_shapes=[
             pltpu.VMEM((1536, 1024), BF16),
@@ -513,15 +526,16 @@
             pltpu.VMEM((4 * WIN, 1536), F32),
             pltpu.VMEM((4 * WIN, 1536), BF16),
             pltpu.VMEM((12, 4, WIN, 128), F32),
+            pltpu.VMEM((4, WIN, 128), F32),
             pltpu.VMEM((4, 512, 128), F32),
             pltpu.VMEM((512, 1536), BF16),
             pltpu.VMEM((2, 512, 128), F32),
-            pltpu.SemaphoreType.DMA((3,)),
+            pltpu.SemaphoreType.DMA((4,)),
         ],
         compiler_params=pltpu.CompilerParams(vmem_limit_bytes=BIG),
         cost_estimate=pl.CostEstimate(flops=9_000_000_000, bytes_accessed=25_000_000, transcendentals=2_000_000),
         name="project_and_convolve",
-    )(slab, ends, x, segment, c, w, gain, bias, taps, scale, shift)
+    )(slab, ends, x, w, gain, bias, taps, scale, shift)
 
 
 def target_tables(data_group, lengths, assignment):
@@ -583,21 +597,14 @@
         lax.ppermute(c_cells[s], "dp", [(i, i ^ s) for i in range(groups)]) for s in range(1, groups)
     ]
     first, ends = target_tables(data_group, lengths, assignment)
-    x_slab = lax.all_to_all(
-        compact(96, group, first, [x_here.reshape(-1, 384)], slabs), "mp", split_axis=0, concat_axis=0, tiled=True
-    )
-    c_slab = lax.all_to_all(
-        compact(64, group, first, c_here, slabs), "mp", split_axis=0, concat_axis=0, tiled=True
-    )
-    slab = slab.reshape(1)
-    x_wide, segment = widen(slab, ends, x_slab)
+    windows = compact(96, 0, group, first, [x_here.reshape(-1, 384)], slabs)
+    windows = compact(64, 384, group, first, c_here, slabs, onto=windows)
+    slab_rows = lax.all_to_all(windows, "mp", split_axis=0, concat_axis=0, tiled=True)
     row = lambda a: a.reshape(1, -1)
     return rest(
-        slab,
+        slab.reshape(1),
         ends,
-        x_wide,
-        segment,
-        c_slab,
+        slab_rows,
         weights,
         row(norm_gain),
         row(norm_bias),

time: 169 us -> 167 us (0.988)
  the two profiles are of different devices: /device:TPU:8 before, /device:TPU:0 now
where the time goes in v3:
time: 167 us; the launch traced here: 165 us
  waiting for transfers between devices  59.4 us (36%)
  Pallas kernels  58.5 us (35%)
  starting transfers between devices  21.9 us (13%)
  between operations  13.6 us (8%)
  local copies, waits for them, and re-layouts  9.29 us (6%)
  other arithmetic  1.76 us (1%)
    all_to_all x1, waiting for transfers between devices, on_device(): lax.all_to_all(windows, 'mp', split_axis=0, concat_axis=0, tiled=True)  50.5 us
    pallas_call x1, Pallas kernels, rest(): pl.pallas_call(rest_kernel, out_shape=jax.ShapeDtypeStruct((512, 1536), B...  37.9 us
    ppermute x7, starting transfers between devices, on_device(): lax.ppermute(c_cells[s], 'dp', [(i, i ^ s) for i in range(groups)])  9.32 us
    ppermute x7, waiting for transfers between devices, on_device(): lax.ppermute(c_cells[s], 'dp', [(i, i ^ s) for i in range(groups)])  8.89 us
    pallas_call x1, Pallas kernels, attend(): pl.pallas_call(attend_kernel, out_shape=[jax.ShapeDtypeStruct((4 * CELL,...  8.35 us
    all_to_all x1, starting transfers between devices, on_device(): lax.all_to_all(windows, 'mp', split_axis=0, concat_axis=0, tiled=True)  8.07 us
    pallas_call x2, Pallas kernels, compact(): pl.pallas_call(functools.partial(compact_kernel, width, offset, len(cells...  7.1 us
    unnamed x26, local copies, waits for them, and re-layouts  5.89 us
  transfers between devices with their start and end apart: 10, of which 5 were waited for; matrix products, arithmetic and copies ran while one was open for 2% of the time, Pallas kernels for 13%

profile of v3, /device:TPU:0, one launch (start us, length us, event | category | flops | bytes accessed | tf_op | source)
XLA Modules:
  0.0 164.5 jit_solution(17770493727533210069)
XLA Ops:
  6.5 1.0 dynamic-slice_bitcast_fusion.2
  7.7 0.9 pad_maximum_fusion
  8.6 0.7 copy-done.2
  9.3 5.1 %pack_cells.1 = bf16[2048,384]{1,0:T(8,128)(2,1)S(1)} custom-call(s32[1]{0:T(128)} %bitcast.1.group_ref, s32[256]{0:T(256)S(1)} %copy-done.3, s32[256]{0:T(256)S(1)} %copy-done.4, bf16[2048,384]{1,0:T(8,128)(2,1)S(1)} %bitcast.16), custom_call_target="tpu_custom_call" | custom-call | flops 20000000 | bytes 3200000 | tf_op jit(solution)/shard_map/pack_cells/pallas_call | solution.py:454
  14.5 1.1 copy-done.1
  15.6 4.6 %all-to-all-start = ((bf16[8,256,384]{2,1,0:T(8,128)(2,1)}), bf16[8,256,384]{2,1,0:T(8,128)(2,1)S(1)}, u32[]{:S(2)}, u32[]{:S(2)}) async-start(bf16[8,256,384]{2,1,0:T(8,128)(2,1)} %bitcast.15), calls=%async_computation | async-start | bytes 3145728 | tf_op jit(solution)/shard_map/all_to_all | solution.py:583
  20.1 1.2 copy-done.5
  21.4 1.3 copy-done.6
  22.7 1.4 copy-done.7
  24.1 8.3 %attend_cells.1 = (bf16[256,256]{1,0:T(8,128)(2,1)S(1)}, bf16[256,256]{1,0:T(8,128)(2,1)S(1)}, bf16[256,256]{1,0:T(8,128)(2,1)S(1)}, bf16[256,256]{1,0:T(8,128)(...) custom-call(s32[1]{0:T(128)} %bitcast.1.group_ref, ...), custom_call_target="tpu_custom_call" | custom-call | flops 2000000000 | bytes 4200000 | tf_op jit(solution)/shard_map/attend_cells/pallas_call | solution.py:475
  32.9 1.7 %collective-permute-start.1 = (bf16[256,256]{1,0:T(8,128)(2,1)S(1)}, bf16[256,256]{1,0:T(8,128)(2,1)S(1)}, u32[]{:S(2)}, u32[]{:S(2)}) collective-permute-start(bf16[256,256]{1,0:T(8,128)(2,1)S(1)} %get-tuple-element.20), channel_id=1, source_target_pairs={{0,32},{16,48},{32,0},{48,16},{64,96},{80,112},{96,64},{112,80},{1... | collective-permute-start | bytes 393224 | tf_op jit(solution)/shard_map/ppermute | solution.py:597
  34.6 3.2 %collective-permute-start.3 = (bf16[256,256]{1,0:T(8,128)(2,1)}, bf16[256,256]{1,0:T(8,128)(2,1)S(1)}, u32[]{:S(2)}, u32[]{:S(2)}) collective-permute-start(bf16[256,256]{1,0:T(8,128)(2,1)} %get-tuple-element.22), channel_id=1, source_target_pairs={{0,64},{16,80},{32,96},{48,112},{64,0},{80,16},{96,32},{112,48},{1... | collective-permute-start | bytes 393224 | tf_op jit(solution)/shard_map/ppermute | solution.py:597
  38.0 3.0 %collective-permute-start.5 = (bf16[256,256]{1,0:T(8,128)(2,1)S(1)}, bf16[256,256]{1,0:T(8,128)(2,1)S(1)}, u32[]{:S(2)}, u32[]{:S(2)}) collective-permute-start(bf16[256,256]{1,0:T(8,128)(2,1)S(1)} %get-tuple-element.24), channel_id=1, source_target_pairs={{0,96},{16,112},{32,64},{48,80},{64,32},{80,48},{96,0},{112,16},{1... | collective-permute-start | bytes 393224 | tf_op jit(solution)/shard_map/ppermute | solution.py:597
  41.1 2.5 %collective-permute-done.1.rest_2_ = bf16[256,256]{1,0:T(8,128)(2,1)S(1)} collective-permute-done((bf16[256,256]{1,0:T(8,128)(2,1)S(1)}, bf16[256,256]{1,0:T(8,128)(2,1)S(1)}, u32[]{:S(2)}, u32[]{:S(2)}) %collective-permute-start.1) | collective-permute-done | bytes 131104 | tf_op jit(solution)/shard_map/ppermute | solution.py:597
  43.5 0.8 collective-permute-start.6
  44.6 4.4 %compact_cells.2.rest_8_ = bf16[16,144,640]{2,1,0:T(8,128)(2,1)} custom-call(s32[1]{0:T(128)} %bitcast.1.group_ref, s32[32]{0:T(128)S(1)} %select_reduce_fusion.2.after_ref, bf16[2048,384]{1,0:T(8,128)(2,1)S(1)} %bitcast.14), custom_call_target="tpu_custom_call" | custom-call | flops 20000000 | bytes 3200000 | tf_op jit(solution)/shard_map/compact_cells/pallas_call | solution.py:498
  49.0 1.7 %collective-permute-done.3.rest_4_ = bf16[256,256]{1,0:T(8,128)(2,1)S(1)} collective-permute-done((bf16[256,256]{1,0:T(8,128)(2,1)}, bf16[256,256]{1,0:T(8,128)(2,1)S(1)}, u32[]{:S(2)}, u32[]{:S(2)}) %collective-permute-start.3) | collective-permute-done | bytes 131104 | tf_op jit(solution)/shard_map/ppermute | solution.py:597
  50.7 1.9 %collective-permute-done.4.rest_5_ = bf16[256,256]{1,0:T(8,128)(2,1)S(1)} collective-permute-done((bf16[256,256]{1,0:T(8,128)(2,1)}, bf16[256,256]{1,0:T(8,128)(2,1)S(1)}, u32[]{:S(2)}, u32[]{:S(2)}) %collective-permute-start.4) | collective-permute-done | bytes 131104 | tf_op jit(solution)/shard_map/ppermute | solution.py:597
  52.6 2.8 %collective-permute-done.6.rest_7_ = bf16[256,256]{1,0:T(8,128)(2,1)S(1)} collective-permute-done((bf16[256,256]{1,0:T(8,128)(2,1)S(1)}, bf16[256,256]{1,0:T(8,128)(2,1)S(1)}, u32[]{:S(2)}, u32[]{:S(2)}) %collective-permute-start.6) | collective-permute-done | bytes 131104 | tf_op jit(solution)/shard_map/ppermute | solution.py:597
  55.4 2.7 %compact_cells.3 = bf16[16,144,640]{2,1,0:T(8,128)(2,1)} custom-call(s32[1]{0:T(128)} %bitcast.1.group_ref, s32[32]{0:T(128)S(1)} %select_reduce_fusion.2.after_ref, bf16[256,256]{1,0:T(8,128)(2,1)S(1)} %get-tuple-element.18.rest_0_, bf16[256,256]{1,0:T(8,128)(2,1)S(1)} %collective-permute-done.rest_1_, ...), custom_call_target="tpu_custom_call", output_to_operand_aliasing={{}: (10, {})} | custom-call | flops 20000000 | bytes 3200000 | tf_op jit(solution)/shard_map/compact_cells/pallas_call | solution.py:498
  58.2 8.1 %all-to-all-start.1 = ((bf16[16,144,640]{2,1,0:T(8,128)(2,1)}), bf16[16,144,640]{2,1,0:T(8,128)(2,1)}, u32[]{:S(2)}, u32[]{:S(2)}) async-start(bf16[16,144,640]{2,1,0:T(8,128)(2,1)} %compact_cells.3), calls=%async_computation.1 | async-start | bytes 5898240 | tf_op jit(solution)/shard_map/all_to_all | solution.py:602
  68.6 0.6 reshape.51.shift_ref
  69.2 50.5 %all-to-all-done.1.x_ref = bf16[16,144,640]{2,1,0:T(8,128)(2,1)} async-done(((bf16[16,144,640]{2,1,0:T(8,128)(2,1)}), bf16[16,144,640]{2,1,0:T(8,128)(2,1)}, u32[]{:S(2)}, u32[]{:S(2)}) %all-to-all-start.1) | async-done | bytes 2949152 | tf_op jit(solution)/shard_map/all_to_all | solution.py:602
  119.7 37.9 %project_and_convolve.1 = bf16[512,1536]{1,0:T(8,128)(2,1)} custom-call(s32[1]{0:T(128)} %bitcast.slab_ref, s32[32]{0:T(128)} %add.16.ends_ref, bf16[16,144,640]{2,1,0:T(8,128)(2,1)} %all-to-all-done.1.x_ref, bf16[5632,1536]{1,0:T(8,128)(2,1)} %all-gather.2.cloned.1.call-done.w_ref, f32[1,1536]{1,0:T(1,128)} %reshape.48.gain_ref, ...), custom_call_target="tpu_custom_call" | custom-call | flops 8999999488 | bytes 25000000 | tf_op jit(solution)/shard_map/project_and_convolve/pallas_call | solution.py:516
  (42 shorter events, 3.5 us)
Async XLA Ops:
  6.5 1.1 copy-start
  6.5 1.2 copy-start.8
  6.5 113.2 %all-gather.2.cloned.1.call-start = ((), (), s32[]{:S(2)}) async-start(), calls=%async_computation.2 | async-start | bytes 17842176 | tf_op jit(solution)/shard_map/all_gather | solution.py:579
  7.7 1.6 copy-start.2
  7.7 1.6 copy-start.3
  7.7 1.6 copy-start.4
  14.4 1.1 copy-start.1
  15.6 29.0 %all-to-all-start = ((bf16[8,256,384]{2,1,0:T(8,128)(2,1)}), bf16[8,256,384]{2,1,0:T(8,128)(2,1)S(1)}, u32[]{:S(2)}, u32[]{:S(2)}) async-start(bf16[8,256,384]{2,1,0:T(8,128)(2,1)} %bitcast.15), calls=%async_computation | async-start | bytes 3145728 | tf_op jit(solution)/shard_map/all_to_all | solution.py:583
  20.1 1.2 copy-start.5
  21.4 1.3 copy-start.6
  22.7 1.4 copy-start.7
  32.4 5.6 %collective-permute-start = (bf16[256,256]{1,0:T(8,128)(2,1)S(1)}, bf16[256,256]{1,0:T(8,128)(2,1)S(1)}, u32[]{:S(2)}, u32[]{:S(2)}) collective-permute-start(bf16[256,256]{1,0:T(8,128)(2,1)S(1)} %get-tuple-element.19), channel_id=1, source_target_pairs={{0,16},{16,0},{32,48},{48,32},{64,80},{80,64},{96,112},{112,96},{1... | collective-permute-start | bytes 393224 | tf_op jit(solution)/shard_map/ppermute | solution.py:597
  32.9 10.6 %collective-permute-start.1 = (bf16[256,256]{1,0:T(8,128)(2,1)S(1)}, bf16[256,256]{1,0:T(8,128)(2,1)S(1)}, u32[]{:S(2)}, u32[]{:S(2)}) collective-permute-start(bf16[256,256]{1,0:T(8,128)(2,1)S(1)} %get-tuple-element.20), channel_id=1, source_target_pairs={{0,32},{16,48},{32,0},{48,16},{64,96},{80,112},{96,64},{112,80},{1... | collective-permute-start | bytes 393224 | tf_op jit(solution)/shard_map/ppermute | solution.py:597
  34.6 14.4 %collective-permute-start.2 = (bf16[256,256]{1,0:T(8,128)(2,1)}, bf16[256,256]{1,0:T(8,128)(2,1)S(1)}, u32[]{:S(2)}, u32[]{:S(2)}) collective-permute-start(bf16[256,256]{1,0:T(8,128)(2,1)} %get-tuple-element.21), channel_id=1, source_target_pairs={{0,48},{16,32},{32,16},{48,0},{64,112},{80,96},{96,80},{112,64},{1... | collective-permute-start | bytes 393224 | tf_op jit(solution)/shard_map/ppermute | solution.py:597
  34.6 16.1 %collective-permute-start.3 = (bf16[256,256]{1,0:T(8,128)(2,1)}, bf16[256,256]{1,0:T(8,128)(2,1)S(1)}, u32[]{:S(2)}, u32[]{:S(2)}) collective-permute-start(bf16[256,256]{1,0:T(8,128)(2,1)} %get-tuple-element.22), channel_id=1, source_target_pairs={{0,64},{16,80},{32,96},{48,112},{64,0},{80,16},{96,32},{112,48},{1... | collective-permute-start | bytes 393224 | tf_op jit(solution)/shard_map/ppermute | solution.py:597
  37.8 14.8 %collective-permute-start.4 = (bf16[256,256]{1,0:T(8,128)(2,1)}, bf16[256,256]{1,0:T(8,128)(2,1)S(1)}, u32[]{:S(2)}, u32[]{:S(2)}) collective-permute-start(bf16[256,256]{1,0:T(8,128)(2,1)} %get-tuple-element.23), channel_id=1, source_target_pairs={{0,80},{16,64},{32,112},{48,96},{64,16},{80,0},{96,48},{112,32},{1... | collective-permute-start | bytes 393224 | tf_op jit(solution)/shard_map/ppermute | solution.py:597
  38.0 14.5 %collective-permute-start.5 = (bf16[256,256]{1,0:T(8,128)(2,1)S(1)}, bf16[256,256]{1,0:T(8,128)(2,1)S(1)}, u32[]{:S(2)}, u32[]{:S(2)}) collective-permute-start(bf16[256,256]{1,0:T(8,128)(2,1)S(1)} %get-tuple-element.24), channel_id=1, source_target_pairs={{0,96},{16,112},{32,64},{48,80},{64,32},{80,48},{96,0},{112,16},{1... | collective-permute-start | bytes 393224 | tf_op jit(solution)/shard_map/ppermute | solution.py:597
  43.5 11.9 %collective-permute-start.6 = (bf16[256,256]{1,0:T(8,128)(2,1)S(1)}, bf16[256,256]{1,0:T(8,128)(2,1)S(1)}, u32[]{:S(2)}, u32[]{:S(2)}) collective-permute-start(bf16[256,256]{1,0:T(8,128)(2,1)S(1)} %get-tuple-element.25), channel_id=1, source_target_pairs={{0,112},{16,96},{32,80},{48,64},{64,48},{80,32},{96,16},{112,0},{1... | collective-permute-start | bytes 393224 | tf_op jit(solution)/shard_map/ppermute | solution.py:597
  58.1 8.7 %copy-start.9 = (f32[1536]{0:T(1024)S(1)}, f32[1536]{0:T(1024)}, u32[]{:S(2)}) copy-start(f32[1536]{0:T(1024)} %param.21) | copy-start | bytes 18436
  58.2 9.3 %copy-start.10 = (f32[1536]{0:T(1024)S(1)}, f32[1536]{0:T(1024)}, u32[]{:S(2)}) copy-start(f32[1536]{0:T(1024)} %param.22) | copy-start | bytes 18436
  58.2 9.8 %copy-start.11 = (f32[1536]{0:T(1024)S(1)}, f32[1536]{0:T(1024)}, u32[]{:S(2)}) copy-start(f32[1536]{0:T(1024)} %param.25) | copy-start | bytes 18436
  58.2 10.4 %copy-start.12 = (f32[1536]{0:T(1024)S(1)}, f32[1536]{0:T(1024)}, u32[]{:S(2)}) copy-start(f32[1536]{0:T(1024)} %param.26) | copy-start | bytes 18436
  58.2 61.6 %all-to-all-start.1 = ((bf16[16,144,640]{2,1,0:T(8,128)(2,1)}), bf16[16,144,640]{2,1,0:T(8,128)(2,1)}, u32[]{:S(2)}, u32[]{:S(2)}) async-start(bf16[16,144,640]{2,1,0:T(8,128)(2,1)} %compact_cells.3), calls=%async_computation.1 | async-start | bytes 5898240 | tf_op jit(solution)/shard_map/all_to_all | solution.py:602
Sparse Core Ops, SparseCore 0:
  9.7 102.6 all-gather.1

commit v4 on v3

--- a/solution.py
+++ b/solution.py
@@ -261,49 +261,24 @@
     sems,
 ):
     slab = slab_ref[0]
-    piece = 176
-
-    def fetch(g, _):
-        c = g // 16
-        m = g - 16 * c
-        base = pl.multiple_of(g * piece, 16)
-        for s in range(3):
-            pltpu.make_async_copy(
-                w_ref.at[pl.ds(base, 32), pl.ds(512 * s, 512)],
-                wo.at[pl.ds(pl.multiple_of(96 * m + 32 * s, 16), 32), pl.ds(pl.multiple_of(512 * c, 512), 512)],
-                sems.at[0],
-            ).start()
-        return 0
-
-    def fetch_glu(half):
-        def one(i, _):
-            c = i // 8
-            m = 4 * half + i % 4 + 8 * ((i // 4) % 2)
-            base = pl.multiple_of((16 * c + m) * piece + 32, 16)
-            pltpu.make_async_copy(
-                w_ref.at[pl.ds(base, 96), :],
-                wg.at[pl.ds(pl.multiple_of(192 * m + 96 * c, 16), 96), :],
-                sems.at[1 + half],
-            ).start()
-            return 0
-
-        lax.fori_loop(0, 16, one, 0)
-
-    def fetch_down(g, _):
-        c = g // 16
-        m = g - 16 * c
-        base = pl.multiple_of(g * piece + 128, 16)
+    wo3, wg3, wd3 = wo.reshape(16, 96, 1024), wg.reshape(16, 192, 1536), wd.reshape(16, 96, 1536)
+    rows = [pl.ds(48 * i, 48) for i in range(4)]
+    for e in range(8):
         pltpu.make_async_copy(
-            w_ref.at[pl.ds(base, 48), :],
-            wd.at[pl.ds(pl.multiple_of(96 * m + 48 * c, 16), 48), :],
-            sems.at[3],
+            w_ref.at[e, :, :, pl.ds(768, 256)], wo3.at[:, rows[e % 2], pl.ds(256 * (e // 2), 256)], sems.at[0]
         ).start()
-        return 0
-
-    lax.fori_loop(0, 32, fetch, 0)
-    fetch_glu(0)
-    fetch_glu(1)
-    lax.fori_loop(0, 32, fetch_down, 0)
+    for half in range(2):
+        for e in range(8):
+            for first in (4 * half, 8 + 4 * half):
+                pltpu.make_async_copy(
+                    w_ref.at[e, pl.ds(first, 4), :, pl.ds(0, 768)],
+                    wg3.at[pl.ds(first, 4), rows[e % 4], pl.ds(768 * (e // 4), 768)],
+                    sems.at[1 + half],
+                ).start()
+    for e in range(8):
+        pltpu.make_async_copy(
+            w_ref.at[e, :, :, pl.ds(1024, 384)], wd3.at[:, rows[e % 2], pl.ds(384 * (e // 2), 384)], sems.at[3]
+        ).start()
 
     for j in range(4):
         frame = 512 * slab - 4 * EDGE + j + 4 * lax.broadcasted_iota(jnp.int32, (WIN, 128), 0)
@@ -569,14 +544,11 @@
     slab = lax.axis_index("mp").astype(jnp.int32)
     groups = lax.axis_size("dp")
     slabs = lax.axis_size("mp")
-    core = data_group % 2
-    op = lax.dynamic_slice_in_dim(out_proj.T, core * 512, 512, 1)
-    op = jnp.concatenate([op[0:32], op[32:64], op[64:96]], axis=1)
-    glu = lax.dynamic_slice_in_dim(glu_proj.T, core * 96, 96, 0)
-    dn = lax.dynamic_slice_in_dim(down_proj.T, core * 48, 48, 0)
-    mine = jnp.concatenate([op, glu, dn], axis=0)
-    chips = [[(2 * p + c) * slabs + m for c in range(2) for m in range(slabs)] for p in range(groups // 2)]
-    weights = lax.all_gather(mine, ("dp", "mp"), axis=0, tiled=True, axis_index_groups=chips)
+    part = lax.dynamic_slice(glu_proj.T, (48 * (data_group % 4), 768 * (data_group // 4)), (48, 768))
+    op = lax.dynamic_slice(out_proj.T, (48 * (data_group % 2), 256 * (data_group // 2)), (48, 256))
+    dn = lax.dynamic_slice(down_proj.T, (48 * (data_group % 2), 384 * (data_group // 2)), (48, 384))
+    mine = jnp.concatenate([part, op, dn], axis=1)
+    weights = lax.all_gather(mine, ("dp", "mp"), axis=0, tiled=True).reshape(groups, slabs, 48, 1408)
 
     group = data_group.reshape(1)
     x_cells = pack(group, lengths, assignment, residual.reshape(residual.shape[0], 384))

time: 167 us -> 181 us (1.084)
  waiting for transfers between devices: 59.4 us -> 73.2 us
  local copies, waits for them, and re-layouts: 9.29 us -> 11.6 us
    all_gather x1, waiting for transfers between devices: 0.01 us -> 5.34 us  [on_device(): lax.all_gather(mine, ('dp', 'mp'), axis=0, tiled=True)]
    ppermute x7, waiting for transfers between devices: 8.89 us -> 13.7 us  [on_device(): lax.ppermute(c_cells[s], 'dp', [(i, i ^ s) for i in range(groups)])]
    all_to_all x1, waiting for transfers between devices: 50.5 us -> 54.1 us  [on_device(): lax.all_to_all(windows, 'mp', split_axis=0, concat_axis=0, tiled=True)]
    unnamed x26 -> x28, local copies, waits for them, and re-layouts: 5.89 us -> 7.64 us
  transfers between devices with their start and end apart: 10 -> 10, of which waited for: 5 -> 5; matrix products, arithmetic and copies ran while one was open for 2% -> 2% of each run, Pallas kernels for 13% -> 12%
where the time goes in v4:
time: 181 us; the launch traced here: 180 us
  waiting for transfers between devices  73.2 us (40%)
  Pallas kernels  57.3 us (32%)
  starting transfers between devices  22.4 us (12%)
  between operations  13.6 us (8%)
  local copies, waits for them, and re-layouts  11.6 us (6%)
    all_to_all x1, waiting for transfers between devices, on_device(): lax.all_to_all(windows, 'mp', split_axis=0, concat_axis=0, tiled=True)  54.1 us
    pallas_call x1, Pallas kernels, rest(): pl.pallas_call(rest_kernel, out_shape=jax.ShapeDtypeStruct((512, 1536), B...  36.6 us
    ppermute x7, waiting for transfers between devices, on_device(): lax.ppermute(c_cells[s], 'dp', [(i, i ^ s) for i in range(groups)])  13.7 us
    ppermute x7, starting transfers between devices, on_device(): lax.ppermute(c_cells[s], 'dp', [(i, i ^ s) for i in range(groups)])  9.05 us
    all_to_all x1, starting transfers between devices, on_device(): lax.all_to_all(windows, 'mp', split_axis=0, concat_axis=0, tiled=True)  8.81 us
    pallas_call x1, Pallas kernels, attend(): pl.pallas_call(attend_kernel, out_shape=[jax.ShapeDtypeStruct((4 * CELL,...  8.36 us
    unnamed x28, local copies, waits for them, and re-layouts  7.64 us
    pallas_call x2, Pallas kernels, compact(): pl.pallas_call(functools.partial(compact_kernel, width, offset, len(cells...  7.21 us
  transfers between devices with their start and end apart: 10, of which 5 were waited for; matrix products, arithmetic and copies ran while one was open for 2% of the time, Pallas kernels for 12%

profile of v4, /device:TPU:0, one launch (start us, length us, event | category | flops | bytes accessed | tf_op | source)
XLA Modules:
  0.0 179.7 jit_solution(6569341175610756848)
XLA Ops:
  6.5 0.8 dynamic-slice_bitcast_fusion.1
  7.4 0.7 dynamic-slice_bitcast_fusion.2
  8.8 1.4 copy-done.2
  10.2 0.7 copy-done.3
  10.9 0.7 copy-done.5
  11.6 5.1 %pack_cells.1 = bf16[2048,384]{1,0:T(8,128)(2,1)S(1)} custom-call(s32[1]{0:T(128)} %bitcast.1.group_ref, s32[256]{0:T(256)S(1)} %copy-done.3, s32[256]{0:T(256)S(1)} %copy-done.5, bf16[2048,384]{1,0:T(8,128)(2,1)S(1)} %bitcast.17), custom_call_target="tpu_custom_call" | custom-call | flops 20000000 | bytes 3200000 | tf_op jit(solution)/shard_map/pack_cells/pallas_call | solution.py:429
  16.8 1.1 copy-done.1
  17.9 4.6 %all-to-all-start = ((bf16[8,256,384]{2,1,0:T(8,128)(2,1)}), bf16[8,256,384]{2,1,0:T(8,128)(2,1)S(1)}, u32[]{:S(2)}, u32[]{:S(2)}) async-start(bf16[8,256,384]{2,1,0:T(8,128)(2,1)} %bitcast.16), calls=%async_computation | async-start | bytes 3145728 | tf_op jit(solution)/shard_map/all_to_all | solution.py:555
  22.5 1.2 copy-done.7
  23.7 1.2 copy-done.8
  25.0 1.2 copy-done.9
  26.2 8.4 %attend_cells.1 = (bf16[256,256]{1,0:T(8,128)(2,1)S(1)}, bf16[256,256]{1,0:T(8,128)(2,1)S(1)}, bf16[256,256]{1,0:T(8,128)(2,1)S(1)}, bf16[256,256]{1,0:T(8,128)(...) custom-call(s32[1]{0:T(128)} %bitcast.1.group_ref, ...), custom_call_target="tpu_custom_call" | custom-call | flops 2000000000 | bytes 4200000 | tf_op jit(solution)/shard_map/attend_cells/pallas_call | solution.py:450
  35.1 1.7 collective-permute-start.1
  36.8 3.2 %collective-permute-start.3 = (bf16[256,256]{1,0:T(8,128)(2,1)}, bf16[256,256]{1,0:T(8,128)(2,1)S(1)}, u32[]{:S(2)}, u32[]{:S(2)}) collective-permute-start(bf16[256,256]{1,0:T(8,128)(2,1)} %get-tuple-element.22), channel_id=1, source_target_pairs={{0,64},{16,80},{32,96},{48,112},{64,0},{80,16},{96,32},{112,48},{1... | collective-permute-start | bytes 393224 | tf_op jit(solution)/shard_map/ppermute | solution.py:569
  40.2 3.0 %collective-permute-start.5 = (bf16[256,256]{1,0:T(8,128)(2,1)S(1)}, bf16[256,256]{1,0:T(8,128)(2,1)S(1)}, u32[]{:S(2)}, u32[]{:S(2)}) collective-permute-start(bf16[256,256]{1,0:T(8,128)(2,1)S(1)} %get-tuple-element.24), channel_id=1, source_target_pairs={{0,96},{16,112},{32,64},{48,80},{64,32},{80,48},{96,0},{112,16},{1... | collective-permute-start | bytes 393224 | tf_op jit(solution)/shard_map/ppermute | solution.py:569
  43.2 4.6 %collective-permute-done.1.rest_2_ = bf16[256,256]{1,0:T(8,128)(2,1)S(1)} collective-permute-done((bf16[256,256]{1,0:T(8,128)(2,1)S(1)}, bf16[256,256]{1,0:T(8,128)(2,1)S(1)}, u32[]{:S(2)}, u32[]{:S(2)}) %collective-permute-start.1) | collective-permute-done | bytes 131104 | tf_op jit(solution)/shard_map/ppermute | solution.py:569
  48.6 4.4 %compact_cells.2.rest_8_ = bf16[16,144,640]{2,1,0:T(8,128)(2,1)} custom-call(s32[1]{0:T(128)} %bitcast.1.group_ref, s32[32]{0:T(128)S(1)} %select_reduce_fusion.2.after_ref, bf16[2048,384]{1,0:T(8,128)(2,1)S(1)} %bitcast.15), custom_call_target="tpu_custom_call" | custom-call | flops 20000000 | bytes 3200000 | tf_op jit(solution)/shard_map/compact_cells/pallas_call | solution.py:473
  53.0 6.3 %collective-permute-done.3.rest_4_ = bf16[256,256]{1,0:T(8,128)(2,1)S(1)} collective-permute-done((bf16[256,256]{1,0:T(8,128)(2,1)}, bf16[256,256]{1,0:T(8,128)(2,1)S(1)}, u32[]{:S(2)}, u32[]{:S(2)}) %collective-permute-start.3) | collective-permute-done | bytes 131104 | tf_op jit(solution)/shard_map/ppermute | solution.py:569
  59.3 2.9 %collective-permute-done.4.rest_5_ = bf16[256,256]{1,0:T(8,128)(2,1)S(1)} collective-permute-done((bf16[256,256]{1,0:T(8,128)(2,1)}, bf16[256,256]{1,0:T(8,128)(2,1)S(1)}, u32[]{:S(2)}, u32[]{:S(2)}) %collective-permute-start.4) | collective-permute-done | bytes 131104 | tf_op jit(solution)/shard_map/ppermute | solution.py:569
  62.2 2.8 %compact_cells.3 = bf16[16,144,640]{2,1,0:T(8,128)(2,1)} custom-call(s32[1]{0:T(128)} %bitcast.1.group_ref, s32[32]{0:T(128)S(1)} %select_reduce_fusion.2.after_ref, bf16[256,256]{1,0:T(8,128)(2,1)S(1)} %get-tuple-element.18.rest_0_, bf16[256,256]{1,0:T(8,128)(2,1)S(1)} %collective-permute-done.rest_1_, ...), custom_call_target="tpu_custom_call", output_to_operand_aliasing={{}: (10, {})} | custom-call | flops 20000000 | bytes 3200000 | tf_op jit(solution)/shard_map/compact_cells/pallas_call | solution.py:473
  65.0 8.8 %all-to-all-start.1 = ((bf16[16,144,640]{2,1,0:T(8,128)(2,1)}), bf16[16,144,640]{2,1,0:T(8,128)(2,1)}, u32[]{:S(2)}, u32[]{:S(2)}) async-start(bf16[16,144,640]{2,1,0:T(8,128)(2,1)} %compact_cells.3), calls=%async_computation.1 | async-start | bytes 5898240 | tf_op jit(solution)/shard_map/all_to_all | solution.py:574
  76.8 54.1 %all-to-all-done.1.x_ref = bf16[16,144,640]{2,1,0:T(8,128)(2,1)} async-done(((bf16[16,144,640]{2,1,0:T(8,128)(2,1)}), bf16[16,144,640]{2,1,0:T(8,128)(2,1)}, u32[]{:S(2)}, u32[]{:S(2)}) %all-to-all-start.1) | async-done | bytes 2949152 | tf_op jit(solution)/shard_map/all_to_all | solution.py:574
  130.9 5.3 %all-gather.2.cloned.1.call-done = bf16[6144,1408]{1,0:T(8,128)(2,1)} async-done(((bf16[48,1408]{1,0:T(8,128)(2,1)}), bf16[6144,1408]{1,0:T(8,128)(2,1)}) %all-gather.2.cloned.1.call-update) | async-done | bytes 17301520 | tf_op jit(solution)/shard_map/all_gather | solution.py:551
  136.2 36.6 %project_and_convolve.1 = bf16[512,1536]{1,0:T(8,128)(2,1)} custom-call(s32[1]{0:T(128)} %bitcast.slab_ref, s32[32]{0:T(128)} %add.29.ends_ref, bf16[16,144,640]{2,1,0:T(8,128)(2,1)} %all-to-all-done.1.x_ref, bf16[8,16,48,1408]{3,2,1,0:T(8,128)(2,1)} %bitcast.21, f32[1,1536]{1,0:T(1,128)} %reshape.52.gain_ref, f32[1,1536]{1,0:T(1,128)} %reshape.53.bias_ref, ...), custom_call_target="tpu_custom_call" | custom-call | flops 8999999488 | bytes 25000000 | tf_op jit(solution)/shard_map/project_and_convolve/pallas_call | solution.py:491
  (43 shorter events, 5.2 us)
Async XLA Ops:
  6.5 1.6 copy-start
  6.5 129.7 %all-gather.2.cloned.1.call-start = ((), (), s32[]{:S(2)}) async-start(), calls=%async_computation.2 | async-start | bytes 17436672 | tf_op jit(solution)/shard_map/all_gather | solution.py:551
  8.8 1.4 copy-start.2
  10.2 0.7 copy-start.3
  10.9 0.7 copy-start.5
  11.6 10.9 %copy-start.4 = (s32[256]{0:T(256)S(1)}, s32[256]{0:T(256)}, u32[]{:S(2)}) copy-start(s32[256]{0:T(256)} %lengths_ref.3) | copy-start | bytes 3076
  11.6 10.9 %copy-start.6 = (s32[256]{0:T(256)S(1)}, s32[256]{0:T(256)}, u32[]{:S(2)}) copy-start(s32[256]{0:T(256)} %assignment_ref.3) | copy-start | bytes 3076
  16.7 1.1 copy-start.1
  17.9 30.7 %all-to-all-start = ((bf16[8,256,384]{2,1,0:T(8,128)(2,1)}), bf16[8,256,384]{2,1,0:T(8,128)(2,1)S(1)}, u32[]{:S(2)}, u32[]{:S(2)}) async-start(bf16[8,256,384]{2,1,0:T(8,128)(2,1)} %bitcast.16), calls=%async_computation | async-start | bytes 3145728 | tf_op jit(solution)/shard_map/all_to_all | solution.py:555
  22.5 1.3 copy-start.7
  23.7 1.2 copy-start.8
  24.9 1.2 copy-start.9
  34.5 5.7 %collective-permute-start = (bf16[256,256]{1,0:T(8,128)(2,1)S(1)}, bf16[256,256]{1,0:T(8,128)(2,1)S(1)}, u32[]{:S(2)}, u32[]{:S(2)}) collective-permute-start(bf16[256,256]{1,0:T(8,128)(2,1)S(1)} %get-tuple-element.19), channel_id=1, source_target_pairs={{0,16},{16,0},{32,48},{48,32},{64,80},{80,64},{96,112},{112,96},{1... | collective-permute-start | bytes 393224 | tf_op jit(solution)/shard_map/ppermute | solution.py:569
  35.1 12.7 %collective-permute-start.1 = (bf16[256,256]{1,0:T(8,128)(2,1)S(1)}, bf16[256,256]{1,0:T(8,128)(2,1)S(1)}, u32[]{:S(2)}, u32[]{:S(2)}) collective-permute-start(bf16[256,256]{1,0:T(8,128)(2,1)S(1)} %get-tuple-element.20), channel_id=1, source_target_pairs={{0,32},{16,48},{32,0},{48,16},{64,96},{80,112},{96,64},{112,80},{1... | collective-permute-start | bytes 393224 | tf_op jit(solution)/shard_map/ppermute | solution.py:569
  36.8 16.2 %collective-permute-start.2 = (bf16[256,256]{1,0:T(8,128)(2,1)}, bf16[256,256]{1,0:T(8,128)(2,1)S(1)}, u32[]{:S(2)}, u32[]{:S(2)}) collective-permute-start(bf16[256,256]{1,0:T(8,128)(2,1)} %get-tuple-element.21), channel_id=1, source_target_pairs={{0,48},{16,32},{32,16},{48,0},{64,112},{80,96},{96,80},{112,64},{1... | collective-permute-start | bytes 393224 | tf_op jit(solution)/shard_map/ppermute | solution.py:569
  36.8 22.5 %collective-permute-start.3 = (bf16[256,256]{1,0:T(8,128)(2,1)}, bf16[256,256]{1,0:T(8,128)(2,1)S(1)}, u32[]{:S(2)}, u32[]{:S(2)}) collective-permute-start(bf16[256,256]{1,0:T(8,128)(2,1)} %get-tuple-element.22), channel_id=1, source_target_pairs={{0,64},{16,80},{32,96},{48,112},{64,0},{80,16},{96,32},{112,48},{1... | collective-permute-start | bytes 393224 | tf_op jit(solution)/shard_map/ppermute | solution.py:569
  40.0 22.2 %collective-permute-start.4 = (bf16[256,256]{1,0:T(8,128)(2,1)}, bf16[256,256]{1,0:T(8,128)(2,1)S(1)}, u32[]{:S(2)}, u32[]{:S(2)}) collective-permute-start(bf16[256,256]{1,0:T(8,128)(2,1)} %get-tuple-element.23), channel_id=1, source_target_pairs={{0,80},{16,64},{32,112},{48,96},{64,16},{80,0},{96,48},{112,32},{1... | collective-permute-start | bytes 393224 | tf_op jit(solution)/shard_map/ppermute | solution.py:569
  40.2 21.9 %collective-permute-start.5 = (bf16[256,256]{1,0:T(8,128)(2,1)S(1)}, bf16[256,256]{1,0:T(8,128)(2,1)S(1)}, u32[]{:S(2)}, u32[]{:S(2)}) collective-permute-start(bf16[256,256]{1,0:T(8,128)(2,1)S(1)} %get-tuple-element.24), channel_id=1, source_target_pairs={{0,96},{16,112},{32,64},{48,80},{64,32},{80,48},{96,0},{112,16},{1... | collective-permute-start | bytes 393224 | tf_op jit(solution)/shard_map/ppermute | solution.py:569
  47.8 14.4 %collective-permute-start.6 = (bf16[256,256]{1,0:T(8,128)(2,1)S(1)}, bf16[256,256]{1,0:T(8,128)(2,1)S(1)}, u32[]{:S(2)}, u32[]{:S(2)}) collective-permute-start(bf16[256,256]{1,0:T(8,128)(2,1)S(1)} %get-tuple-element.25), channel_id=1, source_target_pairs={{0,112},{16,96},{32,80},{48,64},{64,48},{80,32},{96,16},{112,0},{1... | collective-permute-start | bytes 393224 | tf_op jit(solution)/shard_map/ppermute | solution.py:569
  64.9 9.4 %copy-start.10 = (f32[1536]{0:T(1024)S(1)}, f32[1536]{0:T(1024)}, u32[]{:S(2)}) copy-start(f32[1536]{0:T(1024)} %param.21) | copy-start | bytes 18436
  65.0 10.0 %copy-start.11 = (f32[1536]{0:T(1024)S(1)}, f32[1536]{0:T(1024)}, u32[]{:S(2)}) copy-start(f32[1536]{0:T(1024)} %param.22) | copy-start | bytes 18436
  65.0 10.6 %copy-start.12 = (f32[1536]{0:T(1024)S(1)}, f32[1536]{0:T(1024)}, u32[]{:S(2)}) copy-start(f32[1536]{0:T(1024)} %param.25) | copy-start | bytes 18436
  65.0 11.2 %copy-start.13 = (f32[1536]{0:T(1024)S(1)}, f32[1536]{0:T(1024)}, u32[]{:S(2)}) copy-start(f32[1536]{0:T(1024)} %param.26) | copy-start | bytes 18436
  65.0 65.9 %all-to-all-start.1 = ((bf16[16,144,640]{2,1,0:T(8,128)(2,1)}), bf16[16,144,640]{2,1,0:T(8,128)(2,1)}, u32[]{:S(2)}, u32[]{:S(2)}) async-start(bf16[16,144,640]{2,1,0:T(8,128)(2,1)} %compact_cells.3), calls=%async_computation.1 | async-start | bytes 5898240 | tf_op jit(solution)/shard_map/all_to_all | solution.py:574
Sparse Core Ops, SparseCore 0:
  10.3 125.9 all-gather.1

commit v5 on v4

--- a/solution.py
+++ b/solution.py
@@ -239,7 +239,7 @@
 def rest_kernel(
     slab_ref,
     ends_ref,
-    x_ref,
+    r_ref,
     w_ref,
     gain_ref,
     bias_ref,
@@ -247,6 +247,7 @@
     scale_ref,
     shift_ref,
     o_ref,
+    x_ref,
     wo,
     wg,
     wd,
@@ -258,27 +259,35 @@
     sums,
     swished,
     turned,
+    sent,
     sems,
+    xsems,
+    osems,
 ):
     slab = slab_ref[0]
+    arrived = []
+    for q in range(4):
+        part = (pl.ds(4 * q, 4), slice(None), slice(None))
+        arrived.append(pltpu.make_async_copy(r_ref.at[part], x_ref.at[part], xsems.at[q]))
+        arrived[q].start()
     wo3, wg3, wd3 = wo.reshape(16, 96, 1024), wg.reshape(16, 192, 1536), wd.reshape(16, 96, 1536)
-    rows = [pl.ds(48 * i, 48) for i in range(4)]
-    for e in range(8):
-        pltpu.make_async_copy(
-            w_ref.at[e, :, :, pl.ds(768, 256)], wo3.at[:, rows[e % 2], pl.ds(256 * (e // 2), 256)], sems.at[0]
-        ).start()
+    for c in range(2):
+        for s in range(3):
+            pltpu.make_async_copy(
+                w_ref.at[c, :, pl.ds(0, 32), pl.ds(512 * s, 512)],
+                wo3.at[:, pl.ds(32 * s, 32), pl.ds(512 * c, 512)],
+                sems.at[0],
+            ).start()
     for half in range(2):
-        for e in range(8):
-            for first in (4 * half, 8 + 4 * half):
+        for first in (4 * half, 8 + 4 * half):
+            for c in range(2):
                 pltpu.make_async_copy(
-                    w_ref.at[e, pl.ds(first, 4), :, pl.ds(0, 768)],
-                    wg3.at[pl.ds(first, 4), rows[e % 4], pl.ds(768 * (e // 4), 768)],
+                    w_ref.at[c, pl.ds(first, 4), pl.ds(32, 96), :],
+                    wg3.at[pl.ds(first, 4), pl.ds(96 * c, 96), :],
                     sems.at[1 + half],
                 ).start()
-    for e in range(8):
-        pltpu.make_async_copy(
-            w_ref.at[e, :, :, pl.ds(1024, 384)], wd3.at[:, rows[e % 2], pl.ds(384 * (e // 2), 384)], sems.at[3]
-        ).start()
+    for c in range(2):
+        pltpu.make_async_copy(w_ref.at[c, :, pl.ds(128, 48), :], wd3.at[:, pl.ds(48 * c, 48), :], sems.at[3]).start()
 
     for j in range(4):
         frame = 512 * slab - 4 * EDGE + j + 4 * lax.broadcasted_iota(jnp.int32, (WIN, 128), 0)
@@ -289,6 +298,8 @@
         number = lax.fori_loop(0, 32, count, jnp.where(frame >= 0, 0, -1), unroll=4)
         segment[j] = number.astype(F32)
 
+    for copy in arrived:
+        copy.wait()
     lane = lax.broadcasted_iota(jnp.int32, (WIN, 384), 1)
 
     def features(g, _):
@@ -304,7 +315,7 @@
             carried[WIN * j : WIN * j + WIN, at] = whole.astype(F32)
         return 0
 
-    lax.fori_loop(0, 4, features, 0)
+    lax.fori_loop(0, 4, features, 0, unroll=2)
 
     low = lax.broadcasted_iota(jnp.int32, (WIN, 128), 1) < 64
 
@@ -321,7 +332,7 @@
             ctx[WIN * j : WIN * j + WIN, at] = jnp.where(low, left, right).astype(BF16)
         return 0
 
-    lax.fori_loop(0, 8, heads, 0)
+    lax.fori_loop(0, 8, heads, 0, unroll=4)
 
     pltpu.make_async_copy(wo, wo, sems.at[0]).wait()
 
@@ -332,7 +343,7 @@
         )
         return 0
 
-    lax.fori_loop(0, 6, project, 0)
+    lax.fori_loop(0, 6, project, 0, unroll=6)
 
     def norm(i, _):
         at = pl.ds(pl.multiple_of(16 * i, 16), 16)
@@ -342,7 +353,7 @@
         normed[at, :] = (centred * lax.rsqrt(variance + EPS) * gain_ref[...] + bias_ref[...]).astype(BF16)
         return 0
 
-    lax.fori_loop(0, 4 * WIN // 16, norm, 0, unroll=4)
+    lax.fori_loop(0, 4 * WIN // 16, norm, 0, unroll=6)
 
     def glu(n, _):
         value = lax.dot_general(
@@ -360,7 +371,7 @@
     for half in range(2):
         part = wg.at[pl.ds(0, 1536), :]
         pltpu.make_async_copy(part, part, sems.at[1 + half]).wait()
-        lax.fori_loop(3 * half, 3 * half + 3, glu, 0)
+        lax.fori_loop(3 * half, 3 * half + 3, glu, 0, unroll=3)
 
     def conv(b, _):
         lanes = [pl.ds(pl.multiple_of(512 * b + 128 * l, 128), 128) for l in range(4)]
@@ -392,7 +403,7 @@
                             sums[l, rows[j], :] = total[l, j]
                 return 0
 
-            lax.fori_loop(0, 16, chunk, 0)
+            lax.fori_loop(0, 16, chunk, 0, unroll=2)
         for l, at in enumerate(lanes):
             affine = sums[l] * scale_ref[:, at] + shift_ref[:, at]
             swished[:, at] = (affine * jax.nn.sigmoid(affine)).astype(BF16)
@@ -412,10 +423,14 @@
             rows = jnp.where(frame < live, rows, 0.0)
             for b in range(2):
                 turned[b, pl.ds(j, 128, stride=4), :] = rows[:, 128 * b : 128 * b + 128]
-        o_ref[:, at] = jnp.concatenate([turned[0], turned[1]], axis=1).astype(BF16)
-        return 0
-
-    lax.fori_loop(0, 6, down, 0)
+        sent[:, at] = jnp.concatenate([turned[0], turned[1]], axis=1).astype(BF16)
+        pltpu.make_async_copy(sent.at[:, at], o_ref.at[:, at], osems.at[n]).start()
+        return 0
+
+    lax.fori_loop(0, 6, down, 0, unroll=6)
+    for n in range(6):
+        at = pl.ds(256 * n, 256)
+        pltpu.make_async_copy(sent.at[:, at], o_ref.at[:, at], osems.at[n]).wait()
 
 
 HBM = pl.BlockSpec(memory_space=pltpu.HBM)
@@ -491,9 +506,10 @@
     return pl.pallas_call(
         rest_kernel,
         out_shape=jax.ShapeDtypeStruct((512, 1536), BF16),
-        in_specs=[SMEM, SMEM, VMEM, HBM] + [VMEM] * 5,
-        out_specs=VMEM,
+        in_specs=[SMEM, SMEM, HBM, HBM] + [VMEM] * 5,
+        out_specs=HBM,
         scratch_shapes=[
+            pltpu.VMEM((16, WIN, 640), BF16),
             pltpu.VMEM((1536, 1024), BF16),
             pltpu.VMEM((3072, 1536), BF16),
             pltpu.VMEM((1536, 1536), BF16),
@@ -505,7 +521,10 @@
             pltpu.VMEM((4, 512, 128), F32),
             pltpu.VMEM((512, 1536), BF16),
             pltpu.VMEM((2, 512, 128), F32),
+            pltpu.VMEM((512, 1536), BF16),
             pltpu.SemaphoreType.DMA((4,)),
+            pltpu.SemaphoreType.DMA((4,)),
+            pltpu.SemaphoreType.DMA((6,)),
         ],
         compiler_params=pltpu.CompilerParams(vmem_limit_bytes=BIG),
         cost_estimate=pl.CostEstimate(flops=9_000_000_000, bytes_accessed=25_000_000, transcendentals=2_000_000),
@@ -544,11 +563,14 @@
     slab = lax.axis_index("mp").astype(jnp.int32)
     groups = lax.axis_size("dp")
     slabs = lax.axis_size("mp")
-    part = lax.dynamic_slice(glu_proj.T, (48 * (data_group % 4), 768 * (data_group // 4)), (48, 768))
-    op = lax.dynamic_slice(out_proj.T, (48 * (data_group % 2), 256 * (data_group // 2)), (48, 256))
-    dn = lax.dynamic_slice(down_proj.T, (48 * (data_group % 2), 384 * (data_group // 2)), (48, 384))
-    mine = jnp.concatenate([part, op, dn], axis=1)
-    weights = lax.all_gather(mine, ("dp", "mp"), axis=0, tiled=True).reshape(groups, slabs, 48, 1408)
+    core = data_group % 2
+    op = lax.dynamic_slice_in_dim(out_proj.T, core * 512, 512, 1)
+    op = jnp.concatenate([op[0:32], op[32:64], op[64:96]], axis=1)
+    glu = lax.dynamic_slice_in_dim(glu_proj.T, core * 96, 96, 0)
+    dn = lax.dynamic_slice_in_dim(down_proj.T, core * 48, 48, 0)
+    mine = jnp.concatenate([op, glu, dn], axis=0)
+    chips = [[(2 * p + c) * slabs + m for c in range(2) for m in range(slabs)] for p in range(groups // 2)]
+    weights = lax.all_gather(mine, ("dp", "mp"), axis=0, tiled=True, axis_index_groups=chips).reshape(2, slabs, 176, 1536)
 
     group = data_group.reshape(1)
     x_cells = pack(group, lengths, assignment, residual.reshape(residual.shape[0], 384))

time: 181 us -> 160 us (0.88)
  waiting for transfers between devices: 73.2 us -> 59.4 us
  Pallas kernels: 57.3 us -> 51.3 us
  local copies, waits for them, and re-layouts: 11.6 us -> 9.29 us
    pallas_call x1, Pallas kernels: 36.6 us -> 30.6 us  [rest(): pl.pallas_call(rest_kernel, out_shape=jax.ShapeDtypeStruct((512, 1536), B...]
    all_gather x1, waiting for transfers between devices: 5.34 us -> 0.01 us  [on_device(): lax.all_gather(mine, ('dp', 'mp'), axis=0, tiled=True, axis_index_groups=...]
    ppermute x7, waiting for transfers between devices: 13.7 us -> 8.87 us  [on_device(): lax.ppermute(c_cells[s], 'dp', [(i, i ^ s) for i in range(groups)])]
    all_to_all x1, waiting for transfers between devices: 54.1 us -> 50.5 us  [on_device(): lax.all_to_all(windows, 'mp', split_axis=0, concat_axis=0, tiled=True)]
    unnamed x28 -> x26, local copies, waits for them, and re-layouts: 7.64 us -> 5.89 us
  transfers between devices with their start and end apart: 10 -> 10, of which waited for: 5 -> 5; matrix products, arithmetic and copies ran while one was open for 2% -> 2% of each run, Pallas kernels for 12% -> 13%
where the time goes in v5:
time: 160 us; the launch traced here: 157 us
  waiting for transfers between devices  59.4 us (37%)
  Pallas kernels  51.3 us (32%)
  starting transfers between devices  21.9 us (14%)
  between operations  13.6 us (8%)
  local copies, waits for them, and re-layouts  9.29 us (6%)
  other arithmetic  1.76 us (1%)
    all_to_all x1, waiting for transfers between devices, on_device(): lax.all_to_all(windows, 'mp', split_axis=0, concat_axis=0, tiled=True)  50.5 us
    pallas_call x1, Pallas kernels, rest(): pl.pallas_call(rest_kernel, out_shape=jax.ShapeDtypeStruct((512, 1536), B...  30.6 us
    ppermute x7, starting transfers between devices, on_device(): lax.ppermute(c_cells[s], 'dp', [(i, i ^ s) for i in range(groups)])  9.28 us
    ppermute x7, waiting for transfers between devices, on_device(): lax.ppermute(c_cells[s], 'dp', [(i, i ^ s) for i in range(groups)])  8.87 us
    pallas_call x1, Pallas kernels, attend(): pl.pallas_call(attend_kernel, out_shape=[jax.ShapeDtypeStruct((4 * CELL,...  8.36 us
    all_to_all x1, starting transfers between devices, on_device(): lax.all_to_all(windows, 'mp', split_axis=0, concat_axis=0, tiled=True)  8.08 us
    pallas_call x2, Pallas kernels, compact(): pl.pallas_call(functools.partial(compact_kernel, width, offset, len(cells...  7.21 us
    unnamed x26, local copies, waits for them, and re-layouts  5.89 us
  transfers between devices with their start and end apart: 10, of which 5 were waited for; matrix products, arithmetic and copies ran while one was open for 2% of the time, Pallas kernels for 13%

profile of v5, /device:TPU:0, one launch (start us, length us, event | category | flops | bytes accessed | tf_op | source)
XLA Modules:
  0.0 157.2 jit_solution(8477715056389057390)
XLA Ops:
  6.5 1.0 dynamic-slice_bitcast_fusion.2
  7.7 0.9 pad_maximum_fusion
  8.6 0.7 copy-done.2
  9.3 5.1 %pack_cells.1 = bf16[2048,384]{1,0:T(8,128)(2,1)S(1)} custom-call(s32[1]{0:T(128)} %bitcast.1.group_ref, s32[256]{0:T(256)S(1)} %copy-done.3, s32[256]{0:T(256)S(1)} %copy-done.4, bf16[2048,384]{1,0:T(8,128)(2,1)S(1)} %bitcast.17), custom_call_target="tpu_custom_call" | custom-call | flops 20000000 | bytes 3200000 | tf_op jit(solution)/shard_map/pack_cells/pallas_call | solution.py:444
  14.5 1.1 copy-done.1
  15.6 4.6 %all-to-all-start = ((bf16[8,256,384]{2,1,0:T(8,128)(2,1)}), bf16[8,256,384]{2,1,0:T(8,128)(2,1)S(1)}, u32[]{:S(2)}, u32[]{:S(2)}) async-start(bf16[8,256,384]{2,1,0:T(8,128)(2,1)} %bitcast.16), calls=%async_computation | async-start | bytes 3145728 | tf_op jit(solution)/shard_map/all_to_all | solution.py:577
  20.1 1.2 copy-done.5
  21.4 1.3 copy-done.6
  22.7 1.4 copy-done.7
  24.1 8.4 %attend_cells.1 = (bf16[256,256]{1,0:T(8,128)(2,1)S(1)}, bf16[256,256]{1,0:T(8,128)(2,1)S(1)}, bf16[256,256]{1,0:T(8,128)(2,1)S(1)}, bf16[256,256]{1,0:T(8,128)(...) custom-call(s32[1]{0:T(128)} %bitcast.1.group_ref, ...), custom_call_target="tpu_custom_call" | custom-call | flops 2000000000 | bytes 4200000 | tf_op jit(solution)/shard_map/attend_cells/pallas_call | solution.py:465
  32.9 1.7 %collective-permute-start.1 = (bf16[256,256]{1,0:T(8,128)(2,1)S(1)}, bf16[256,256]{1,0:T(8,128)(2,1)S(1)}, u32[]{:S(2)}, u32[]{:S(2)}) collective-permute-start(bf16[256,256]{1,0:T(8,128)(2,1)S(1)} %get-tuple-element.20), channel_id=1, source_target_pairs={{0,32},{16,48},{32,0},{48,16},{64,96},{80,112},{96,64},{112,80},{1... | collective-permute-start | bytes 393224 | tf_op jit(solution)/shard_map/ppermute | solution.py:591
  34.6 3.2 %collective-permute-start.3 = (bf16[256,256]{1,0:T(8,128)(2,1)}, bf16[256,256]{1,0:T(8,128)(2,1)S(1)}, u32[]{:S(2)}, u32[]{:S(2)}) collective-permute-start(bf16[256,256]{1,0:T(8,128)(2,1)} %get-tuple-element.22), channel_id=1, source_target_pairs={{0,64},{16,80},{32,96},{48,112},{64,0},{80,16},{96,32},{112,48},{1... | collective-permute-start | bytes 393224 | tf_op jit(solution)/shard_map/ppermute | solution.py:591
  38.1 3.0 %collective-permute-start.5 = (bf16[256,256]{1,0:T(8,128)(2,1)S(1)}, bf16[256,256]{1,0:T(8,128)(2,1)S(1)}, u32[]{:S(2)}, u32[]{:S(2)}) collective-permute-start(bf16[256,256]{1,0:T(8,128)(2,1)S(1)} %get-tuple-element.24), channel_id=1, source_target_pairs={{0,96},{16,112},{32,64},{48,80},{64,32},{80,48},{96,0},{112,16},{1... | collective-permute-start | bytes 393224 | tf_op jit(solution)/shard_map/ppermute | solution.py:591
  41.0 2.5 %collective-permute-done.1.rest_2_ = bf16[256,256]{1,0:T(8,128)(2,1)S(1)} collective-permute-done((bf16[256,256]{1,0:T(8,128)(2,1)S(1)}, bf16[256,256]{1,0:T(8,128)(2,1)S(1)}, u32[]{:S(2)}, u32[]{:S(2)}) %collective-permute-start.1) | collective-permute-done | bytes 131104 | tf_op jit(solution)/shard_map/ppermute | solution.py:591
  43.5 0.8 collective-permute-start.6
  44.6 4.4 %compact_cells.2.rest_8_ = bf16[16,144,640]{2,1,0:T(8,128)(2,1)} custom-call(s32[1]{0:T(128)} %bitcast.1.group_ref, s32[32]{0:T(128)S(1)} %select_reduce_fusion.2.after_ref, bf16[2048,384]{1,0:T(8,128)(2,1)S(1)} %bitcast.15), custom_call_target="tpu_custom_call" | custom-call | flops 20000000 | bytes 3200000 | tf_op jit(solution)/shard_map/compact_cells/pallas_call | solution.py:488
  49.0 1.7 %collective-permute-done.3.rest_4_ = bf16[256,256]{1,0:T(8,128)(2,1)S(1)} collective-permute-done((bf16[256,256]{1,0:T(8,128)(2,1)}, bf16[256,256]{1,0:T(8,128)(2,1)S(1)}, u32[]{:S(2)}, u32[]{:S(2)}) %collective-permute-start.3) | collective-permute-done | bytes 131104 | tf_op jit(solution)/shard_map/ppermute | solution.py:591
  50.7 1.9 %collective-permute-done.4.rest_5_ = bf16[256,256]{1,0:T(8,128)(2,1)S(1)} collective-permute-done((bf16[256,256]{1,0:T(8,128)(2,1)}, bf16[256,256]{1,0:T(8,128)(2,1)S(1)}, u32[]{:S(2)}, u32[]{:S(2)}) %collective-permute-start.4) | collective-permute-done | bytes 131104 | tf_op jit(solution)/shard_map/ppermute | solution.py:591
  52.6 2.8 %collective-permute-done.6.rest_7_ = bf16[256,256]{1,0:T(8,128)(2,1)S(1)} collective-permute-done((bf16[256,256]{1,0:T(8,128)(2,1)S(1)}, bf16[256,256]{1,0:T(8,128)(2,1)S(1)}, u32[]{:S(2)}, u32[]{:S(2)}) %collective-permute-start.6) | collective-permute-done | bytes 131104 | tf_op jit(solution)/shard_map/ppermute | solution.py:591
  55.4 2.8 %compact_cells.3 = bf16[16,144,640]{2,1,0:T(8,128)(2,1)} custom-call(s32[1]{0:T(128)} %bitcast.1.group_ref, s32[32]{0:T(128)S(1)} %select_reduce_fusion.2.after_ref, bf16[256,256]{1,0:T(8,128)(2,1)S(1)} %get-tuple-element.18.rest_0_, bf16[256,256]{1,0:T(8,128)(2,1)S(1)} %collective-permute-done.rest_1_, ...), custom_call_target="tpu_custom_call", output_to_operand_aliasing={{}: (10, {})} | custom-call | flops 20000000 | bytes 3200000 | tf_op jit(solution)/shard_map/compact_cells/pallas_call | solution.py:488
  58.3 8.1 %all-to-all-start.1 = ((bf16[16,144,640]{2,1,0:T(8,128)(2,1)}), bf16[16,144,640]{2,1,0:T(8,128)(2,1)}, u32[]{:S(2)}, u32[]{:S(2)}) async-start(bf16[16,144,640]{2,1,0:T(8,128)(2,1)} %compact_cells.3), calls=%async_computation.1 | async-start | bytes 5898240 | tf_op jit(solution)/shard_map/all_to_all | solution.py:596
  68.7 0.6 reshape.55.shift_ref
  69.3 50.5 %all-to-all-done.1.r_ref = bf16[16,144,640]{2,1,0:T(8,128)(2,1)} async-done(((bf16[16,144,640]{2,1,0:T(8,128)(2,1)}), bf16[16,144,640]{2,1,0:T(8,128)(2,1)}, u32[]{:S(2)}, u32[]{:S(2)}) %all-to-all-start.1) | async-done | bytes 2949152 | tf_op jit(solution)/shard_map/all_to_all | solution.py:596
  119.8 30.6 %project_and_convolve.1 = bf16[512,1536]{1,0:T(8,128)(2,1)} custom-call(s32[1]{0:T(128)} %bitcast.slab_ref, s32[32]{0:T(128)} %add.16.ends_ref, bf16[16,144,640]{2,1,0:T(8,128)(2,1)} %all-to-all-done.1.r_ref, bf16[2,16,176,1536]{3,2,1,0:T(8,128)(2,1)} %bitcast.21, f32[1,1536]{1,0:T(1,128)} %reshape.52.gain_ref, f32[1,1536]{1,0:T(1,128)} %reshape.53.bias_ref, ...), custom_call_target="tpu_custom_call" | custom-call | flops 8999999488 | bytes 25000000 | tf_op jit(solution)/shard_map/project_and_convolve/pallas_call | solution.py:506
  (42 shorter events, 3.5 us)
Async XLA Ops:
  6.5 1.1 copy-start
  6.5 1.2 copy-start.8
  6.5 113.2 %all-gather.2.cloned.1.call-start = ((), (), s32[]{:S(2)}) async-start(), calls=%async_computation.2 | async-start | bytes 17842176 | tf_op jit(solution)/shard_map/all_gather | solution.py:573
  7.7 1.6 %copy-start.2 = (bf16[2048,1,384]{2,0,1:T(8,128)(2,1)S(1)}, bf16[2048,1,384]{2,0,1:T(8,128)(2,1)}, u32[]{:S(2)}) copy-start(bf16[2048,1,384]{2,0,1:T(8,128)(2,1)} %param.17) | copy-start | bytes 4718596
  7.7 1.6 %copy-start.3 = (s32[256]{0:T(256)S(1)}, s32[256]{0:T(256)}, u32[]{:S(2)}) copy-start(s32[256]{0:T(256)} %lengths_ref.3) | copy-start | bytes 3076
  7.7 1.6 %copy-start.4 = (s32[256]{0:T(256)S(1)}, s32[256]{0:T(256)}, u32[]{:S(2)}) copy-start(s32[256]{0:T(256)} %assignment_ref.3) | copy-start | bytes 3076
  14.4 1.1 copy-start.1
  15.6 29.0 %all-to-all-start = ((bf16[8,256,384]{2,1,0:T(8,128)(2,1)}), bf16[8,256,384]{2,1,0:T(8,128)(2,1)S(1)}, u32[]{:S(2)}, u32[]{:S(2)}) async-start(bf16[8,256,384]{2,1,0:T(8,128)(2,1)} %bitcast.16), calls=%async_computation | async-start | bytes 3145728 | tf_op jit(solution)/shard_map/all_to_all | solution.py:577
  20.1 1.2 copy-start.5
  21.4 1.3 copy-start.6
  22.7 1.4 copy-start.7
  32.4 5.6 %collective-permute-start = (bf16[256,256]{1,0:T(8,128)(2,1)S(1)}, bf16[256,256]{1,0:T(8,128)(2,1)S(1)}, u32[]{:S(2)}, u32[]{:S(2)}) collective-permute-start(bf16[256,256]{1,0:T(8,128)(2,1)S(1)} %get-tuple-element.19), channel_id=1, source_target_pairs={{0,16},{16,0},{32,48},{48,32},{64,80},{80,64},{96,112},{112,96},{1... | collective-permute-start | bytes 393224 | tf_op jit(solution)/shard_map/ppermute | solution.py:591
  32.9 10.6 %collective-permute-start.1 = (bf16[256,256]{1,0:T(8,128)(2,1)S(1)}, bf16[256,256]{1,0:T(8,128)(2,1)S(1)}, u32[]{:S(2)}, u32[]{:S(2)}) collective-permute-start(bf16[256,256]{1,0:T(8,128)(2,1)S(1)} %get-tuple-element.20), channel_id=1, source_target_pairs={{0,32},{16,48},{32,0},{48,16},{64,96},{80,112},{96,64},{112,80},{1... | collective-permute-start | bytes 393224 | tf_op jit(solution)/shard_map/ppermute | solution.py:591
  34.6 14.4 %collective-permute-start.2 = (bf16[256,256]{1,0:T(8,128)(2,1)}, bf16[256,256]{1,0:T(8,128)(2,1)S(1)}, u32[]{:S(2)}, u32[]{:S(2)}) collective-permute-start(bf16[256,256]{1,0:T(8,128)(2,1)} %get-tuple-element.21), channel_id=1, source_target_pairs={{0,48},{16,32},{32,16},{48,0},{64,112},{80,96},{96,80},{112,64},{1... | collective-permute-start | bytes 393224 | tf_op jit(solution)/shard_map/ppermute | solution.py:591
  34.6 16.1 %collective-permute-start.3 = (bf16[256,256]{1,0:T(8,128)(2,1)}, bf16[256,256]{1,0:T(8,128)(2,1)S(1)}, u32[]{:S(2)}, u32[]{:S(2)}) collective-permute-start(bf16[256,256]{1,0:T(8,128)(2,1)} %get-tuple-element.22), channel_id=1, source_target_pairs={{0,64},{16,80},{32,96},{48,112},{64,0},{80,16},{96,32},{112,48},{1... | collective-permute-start | bytes 393224 | tf_op jit(solution)/shard_map/ppermute | solution.py:591
  37.8 14.8 %collective-permute-start.4 = (bf16[256,256]{1,0:T(8,128)(2,1)}, bf16[256,256]{1,0:T(8,128)(2,1)S(1)}, u32[]{:S(2)}, u32[]{:S(2)}) collective-permute-start(bf16[256,256]{1,0:T(8,128)(2,1)} %get-tuple-element.23), channel_id=1, source_target_pairs={{0,80},{16,64},{32,112},{48,96},{64,16},{80,0},{96,48},{112,32},{1... | collective-permute-start | bytes 393224 | tf_op jit(solution)/shard_map/ppermute | solution.py:591
  38.1 14.5 %collective-permute-start.5 = (bf16[256,256]{1,0:T(8,128)(2,1)S(1)}, bf16[256,256]{1,0:T(8,128)(2,1)S(1)}, u32[]{:S(2)}, u32[]{:S(2)}) collective-permute-start(bf16[256,256]{1,0:T(8,128)(2,1)S(1)} %get-tuple-element.24), channel_id=1, source_target_pairs={{0,96},{16,112},{32,64},{48,80},{64,32},{80,48},{96,0},{112,16},{1... | collective-permute-start | bytes 393224 | tf_op jit(solution)/shard_map/ppermute | solution.py:591
  43.5 11.9 %collective-permute-start.6 = (bf16[256,256]{1,0:T(8,128)(2,1)S(1)}, bf16[256,256]{1,0:T(8,128)(2,1)S(1)}, u32[]{:S(2)}, u32[]{:S(2)}) collective-permute-start(bf16[256,256]{1,0:T(8,128)(2,1)S(1)} %get-tuple-element.25), channel_id=1, source_target_pairs={{0,112},{16,96},{32,80},{48,64},{64,48},{80,32},{96,16},{112,0},{1... | collective-permute-start | bytes 393224 | tf_op jit(solution)/shard_map/ppermute | solution.py:591
  58.2 8.7 %copy-start.9 = (f32[1536]{0:T(1024)S(1)}, f32[1536]{0:T(1024)}, u32[]{:S(2)}) copy-start(f32[1536]{0:T(1024)} %param.21) | copy-start | bytes 18436
  58.2 9.3 %copy-start.10 = (f32[1536]{0:T(1024)S(1)}, f32[1536]{0:T(1024)}, u32[]{:S(2)}) copy-start(f32[1536]{0:T(1024)} %param.22) | copy-start | bytes 18436
  58.2 9.9 %copy-start.11 = (f32[1536]{0:T(1024)S(1)}, f32[1536]{0:T(1024)}, u32[]{:S(2)}) copy-start(f32[1536]{0:T(1024)} %param.25) | copy-start | bytes 18436
  58.2 10.4 %copy-start.12 = (f32[1536]{0:T(1024)S(1)}, f32[1536]{0:T(1024)}, u32[]{:S(2)}) copy-start(f32[1536]{0:T(1024)} %param.26) | copy-start | bytes 18436
  58.3 61.5 %all-to-all-start.1 = ((bf16[16,144,640]{2,1,0:T(8,128)(2,1)}), bf16[16,144,640]{2,1,0:T(8,128)(2,1)}, u32[]{:S(2)}, u32[]{:S(2)}) async-start(bf16[16,144,640]{2,1,0:T(8,128)(2,1)} %compact_cells.3), calls=%async_computation.1 | async-start | bytes 5898240 | tf_op jit(solution)/shard_map/all_to_all | solution.py:596
Sparse Core Ops, SparseCore 0:
  9.7 102.5 all-gather.1

commit v6 on v5

--- a/solution.py
+++ b/solution.py
@@ -84,11 +84,19 @@
 
 
 def attend_kernel(
-    group_ref, lengths_ref, assignment_ref, q_ref, k_ref, v_ref, *rest
+    group_ref, lengths_ref, assignment_ref, q_hbm, k_hbm, v_hbm, *rest
 ):
-    outs, (qf, kf, vf, o_ref, start_ref, size_ref, seen_ref, sem) = rest[:8], rest[8:]
+    outs, (q_ref, k_ref, v_ref, qf, kf, vf, o_ref, start_ref, size_ref, seen_ref, sem, arrivals) = rest[:8], rest[8:]
+    inputs = [
+        pltpu.make_async_copy(source, target, arrivals.at[i])
+        for i, (source, target) in enumerate(((q_hbm, q_ref), (k_hbm, k_ref), (v_hbm, v_ref)))
+    ]
+    for copy in inputs:
+        copy.start()
     cell_tables(group_ref[0], lengths_ref, assignment_ref, start_ref, size_ref, seen_ref)
     rows = q_ref.shape[0]
+    for copy in inputs:
+        copy.wait()
 
     def widen(i, _):
         r = pl.multiple_of(i * 128, 128)
@@ -315,7 +323,7 @@
             carried[WIN * j : WIN * j + WIN, at] = whole.astype(F32)
         return 0
 
-    lax.fori_loop(0, 4, features, 0, unroll=2)
+    lax.fori_loop(0, 4, features, 0, unroll=4)
 
     low = lax.broadcasted_iota(jnp.int32, (WIN, 128), 1) < 64
 
@@ -332,7 +340,7 @@
             ctx[WIN * j : WIN * j + WIN, at] = jnp.where(low, left, right).astype(BF16)
         return 0
 
-    lax.fori_loop(0, 8, heads, 0, unroll=4)
+    lax.fori_loop(0, 8, heads, 0, unroll=8)
 
     pltpu.make_async_copy(wo, wo, sems.at[0]).wait()
 
@@ -403,7 +411,7 @@
                             sums[l, rows[j], :] = total[l, j]
                 return 0
 
-            lax.fori_loop(0, 16, chunk, 0, unroll=2)
+            lax.fori_loop(0, 16, chunk, 0, unroll=4)
         for l, at in enumerate(lanes):
             affine = sums[l] * scale_ref[:, at] + shift_ref[:, at]
             swished[:, at] = (affine * jax.nn.sigmoid(affine)).astype(BF16)
@@ -454,7 +462,7 @@
             pltpu.SMEM((8,), jnp.int32),
             pltpu.SemaphoreType.DMA,
         ],
-        compiler_params=pltpu.CompilerParams(vmem_limit_bytes=24 * 1024 * 1024),
+        compiler_params=pltpu.CompilerParams(vmem_limit_bytes=BIG),
         cost_estimate=pl.CostEstimate(flops=20_000_000, bytes_accessed=3_200_000, transcendentals=0),
         name="pack_cells",
     )(group, lengths, assignment, x)
@@ -465,9 +473,12 @@
     return pl.pallas_call(
         attend_kernel,
         out_shape=[jax.ShapeDtypeStruct((4 * CELL, 256), BF16)] * 8,
-        in_specs=[SMEM, SMEM, SMEM, VMEM, VMEM, VMEM],
+        in_specs=[SMEM, SMEM, SMEM, HBM, HBM, HBM],
         out_specs=[HBM] * 8,
         scratch_shapes=[
+            pltpu.VMEM((rows, 128), BF16),
+            pltpu.VMEM((rows, 128), BF16),
+            pltpu.VMEM((rows, 128), BF16),
             pltpu.VMEM((rows + 136, 128), F32),
             pltpu.VMEM((rows + 136, 128), F32),
             pltpu.VMEM((rows + 136, 128), F32),
@@ -476,8 +487,9 @@
             pltpu.SMEM((32,), jnp.int32),
             pltpu.SMEM((8,), jnp.int32),
             pltpu.SemaphoreType.DMA((8,)),
+            pltpu.SemaphoreType.DMA((3,)),
         ],
-        compiler_params=pltpu.CompilerParams(vmem_limit_bytes=32 * 1024 * 1024),
+        compiler_params=pltpu.CompilerParams(vmem_limit_bytes=BIG),
         cost_estimate=pl.CostEstimate(flops=2_000_000_000, bytes_accessed=4_200_000, transcendentals=2_000_000),
         name="attend_cells",
     )(group, lengths, assignment, q, k, v)
@@ -587,9 +599,10 @@
         value_rows.reshape(-1, 128),
     )
     x_here, first_cells = lax.optimization_barrier((x_here, c_cells[0]))
-    c_here = [first_cells] + [
-        lax.ppermute(c_cells[s], "dp", [(i, i ^ s) for i in range(groups)]) for s in range(1, groups)
-    ]
+    c_here = {0: first_cells}
+    for s in (5, 4, 3, 7, 2, 6, 1):
+        c_here[s] = lax.ppermute(c_cells[s], "dp", [(i, i ^ s) for i in range(groups)])
+    c_here = [c_here[s] for s in range(groups)]
     first, ends = target_tables(data_group, lengths, assignment)
     windows = compact(96, 0, group, first, [x_here.reshape(-1, 384)], slabs)
     windows = compact(64, 384, group, first, c_here, slabs, onto=windows)

time: 160 us -> 158 us (0.988)
  local copies, waits for them, and re-layouts: 9.29 us -> 3.61 us
  waiting for transfers between devices: 59.4 us -> 63.9 us
    unnamed x26 -> x18, local copies, waits for them, and re-layouts: 5.89 us -> 0.2 us
    ppermute x7, waiting for transfers between devices: 8.87 us -> 11.3 us  [on_device(): lax.ppermute(c_cells[s], 'dp', [(i, i ^ s) for i in range(groups)])]
    all_to_all x1, waiting for transfers between devices: 50.5 us -> 52.6 us  [on_device(): lax.all_to_all(windows, 'mp', split_axis=0, concat_axis=0, tiled=True)]
  transfers between devices with their start and end apart: 10 -> 10, of which waited for: 5 -> 5; matrix products, arithmetic and copies ran while one was open for 2% -> 2% of each run, Pallas kernels for 13% -> 14%
where the time goes in v6:
time: 158 us; the launch traced here: 156 us
  waiting for transfers between devices  63.9 us (40%)
  Pallas kernels  50.9 us (32%)
  starting transfers between devices  22 us (14%)
  between operations  13.6 us (9%)
  local copies, waits for them, and re-layouts  3.61 us (2%)
  other arithmetic  1.72 us (1%)
    all_to_all x1, waiting for transfers between devices, on_device(): lax.all_to_all(windows, 'mp', split_axis=0, concat_axis=0, tiled=True)  52.6 us
    pallas_call x1, Pallas kernels, rest(): pl.pallas_call(rest_kernel, out_shape=jax.ShapeDtypeStruct((512, 1536), B...  29.2 us
    ppermute x7, waiting for transfers between devices, on_device(): lax.ppermute(c_cells[s], 'dp', [(i, i ^ s) for i in range(groups)])  11.3 us
    pallas_call x1, Pallas kernels, attend(): pl.pallas_call(attend_kernel, out_shape=[jax.ShapeDtypeStruct((4 * CELL,...  9.96 us
    ppermute x7, starting transfers between devices, on_device(): lax.ppermute(c_cells[s], 'dp', [(i, i ^ s) for i in range(groups)])  9.38 us
    all_to_all x1, starting transfers between devices, on_device(): lax.all_to_all(windows, 'mp', split_axis=0, concat_axis=0, tiled=True)  8.08 us
    pallas_call x2, Pallas kernels, compact(): pl.pallas_call(functools.partial(compact_kernel, width, offset, len(cells...  7.07 us
    pallas_call x1, Pallas kernels, pack(): pl.pallas_call(pack_kernel, out_shape=jax.ShapeDtypeStruct((32 * CELL, 38...  4.64 us
  transfers between devices with their start and end apart: 10, of which 5 were waited for; matrix products, arithmetic and copies ran while one was open for 2% of the time, Pallas kernels for 14%

profile of v6, /device:TPU:0, one launch (start us, length us, event | category | flops | bytes accessed | tf_op | source)
XLA Modules:
  0.0 155.7 jit_solution(16462837402296817401)
XLA Ops:
  6.5 1.0 dynamic-slice_bitcast_fusion.2
  7.7 0.8 pad_maximum_fusion
  8.6 4.6 %pack_cells.1 = bf16[2048,384]{1,0:T(8,128)(2,1)} custom-call(s32[1]{0:T(128)} %bitcast.1.group_ref, s32[256]{0:T(256)} %lengths_ref.3, s32[256]{0:T(256)} %assignment_ref.3, bf16[2048,384]{1,0:T(8,128)(2,1)} %bitcast.17), custom_call_target="tpu_custom_call" | custom-call | flops 20000000 | bytes 3200000 | tf_op jit(solution)/shard_map/pack_cells/pallas_call | solution.py:452
  13.3 4.6 %all-to-all-start = ((bf16[8,256,384]{2,1,0:T(8,128)(2,1)}), bf16[8,256,384]{2,1,0:T(8,128)(2,1)S(1)}, u32[]{:S(2)}, u32[]{:S(2)}) async-start(bf16[8,256,384]{2,1,0:T(8,128)(2,1)} %bitcast.16), calls=%async_computation | async-start | bytes 3145728 | tf_op jit(solution)/shard_map/all_to_all | solution.py:589
  17.8 10.0 %attend_cells.1 = (bf16[256,256]{1,0:T(8,128)(2,1)}, bf16[256,256]{1,0:T(8,128)(2,1)}, bf16[256,256]{1,0:T(8,128)(2,1)}, bf16[256,256]{1,0:T(8,128)(2,1)}, bf16[...) custom-call(s32[1]{0:T(128)} %bitcast.1.group_ref, ...), custom_call_target="tpu_custom_call" | custom-call | flops 2000000000 | bytes 4200000 | tf_op jit(solution)/shard_map/attend_cells/pallas_call | solution.py:473
  27.8 0.6 collective-permute-start
  28.4 1.7 %collective-permute-start.1 = (bf16[256,256]{1,0:T(8,128)(2,1)}, bf16[256,256]{1,0:T(8,128)(2,1)S(1)}, u32[]{:S(2)}, u32[]{:S(2)}) collective-permute-start(bf16[256,256]{1,0:T(8,128)(2,1)} %get-tuple-element.20), channel_id=1, source_target_pairs={{0,32},{16,48},{32,0},{48,16},{64,96},{80,112},{96,64},{112,80},{1... | collective-permute-start | bytes 393224 | tf_op jit(solution)/shard_map/ppermute | solution.py:604
  30.0 3.2 %collective-permute-start.3 = (bf16[256,256]{1,0:T(8,128)(2,1)}, bf16[256,256]{1,0:T(8,128)(2,1)S(1)}, u32[]{:S(2)}, u32[]{:S(2)}) collective-permute-start(bf16[256,256]{1,0:T(8,128)(2,1)} %get-tuple-element.22), channel_id=1, source_target_pairs={{0,64},{16,80},{32,96},{48,112},{64,0},{80,16},{96,32},{112,48},{1... | collective-permute-start | bytes 393224 | tf_op jit(solution)/shard_map/ppermute | solution.py:604
  33.5 3.0 %collective-permute-start.5 = (bf16[256,256]{1,0:T(8,128)(2,1)}, bf16[256,256]{1,0:T(8,128)(2,1)S(1)}, u32[]{:S(2)}, u32[]{:S(2)}) collective-permute-start(bf16[256,256]{1,0:T(8,128)(2,1)} %get-tuple-element.24), channel_id=1, source_target_pairs={{0,96},{16,112},{32,64},{48,80},{64,32},{80,48},{96,0},{112,16},{1... | collective-permute-start | bytes 393224 | tf_op jit(solution)/shard_map/ppermute | solution.py:604
  36.5 4.7 %collective-permute-done.1.rest_2_ = bf16[256,256]{1,0:T(8,128)(2,1)S(1)} collective-permute-done((bf16[256,256]{1,0:T(8,128)(2,1)}, bf16[256,256]{1,0:T(8,128)(2,1)S(1)}, u32[]{:S(2)}, u32[]{:S(2)}) %collective-permute-start.1) | collective-permute-done | bytes 131104 | tf_op jit(solution)/shard_map/ppermute | solution.py:604
  41.2 0.8 collective-permute-start.6
  42.3 4.3 %compact_cells.2.rest_8_ = bf16[16,144,640]{2,1,0:T(8,128)(2,1)} custom-call(s32[1]{0:T(128)} %bitcast.1.group_ref, s32[32]{0:T(128)S(1)} %select_reduce_fusion.2.after_ref, bf16[2048,384]{1,0:T(8,128)(2,1)S(1)} %bitcast.15), custom_call_target="tpu_custom_call" | custom-call | flops 20000000 | bytes 3200000 | tf_op jit(solution)/shard_map/compact_cells/pallas_call | solution.py:500
  46.6 1.8 %collective-permute-done.3.rest_4_ = bf16[256,256]{1,0:T(8,128)(2,1)S(1)} collective-permute-done((bf16[256,256]{1,0:T(8,128)(2,1)}, bf16[256,256]{1,0:T(8,128)(2,1)S(1)}, u32[]{:S(2)}, u32[]{:S(2)}) %collective-permute-start.3) | collective-permute-done | bytes 131104 | tf_op jit(solution)/shard_map/ppermute | solution.py:604
  48.4 1.9 %collective-permute-done.4.rest_5_ = bf16[256,256]{1,0:T(8,128)(2,1)S(1)} collective-permute-done((bf16[256,256]{1,0:T(8,128)(2,1)}, bf16[256,256]{1,0:T(8,128)(2,1)S(1)}, u32[]{:S(2)}, u32[]{:S(2)}) %collective-permute-start.4) | collective-permute-done | bytes 131104 | tf_op jit(solution)/shard_map/ppermute | solution.py:604
  50.3 2.9 %collective-permute-done.6.rest_7_ = bf16[256,256]{1,0:T(8,128)(2,1)S(1)} collective-permute-done((bf16[256,256]{1,0:T(8,128)(2,1)}, bf16[256,256]{1,0:T(8,128)(2,1)S(1)}, u32[]{:S(2)}, u32[]{:S(2)}) %collective-permute-start.6) | collective-permute-done | bytes 131104 | tf_op jit(solution)/shard_map/ppermute | solution.py:604
  53.2 2.7 %compact_cells.3 = bf16[16,144,640]{2,1,0:T(8,128)(2,1)} custom-call(s32[1]{0:T(128)} %bitcast.1.group_ref, s32[32]{0:T(128)S(1)} %select_reduce_fusion.2.after_ref, bf16[256,256]{1,0:T(8,128)(2,1)S(1)} %copy-done.1, bf16[256,256]{1,0:T(8,128)(2,1)S(1)} %collective-permute-done.rest_1_, ...), custom_call_target="tpu_custom_call", output_to_operand_aliasing={{}: (10, {})} | custom-call | flops 20000000 | bytes 3200000 | tf_op jit(solution)/shard_map/compact_cells/pallas_call | solution.py:500
  56.0 8.1 %all-to-all-start.1 = ((bf16[16,144,640]{2,1,0:T(8,128)(2,1)}), bf16[16,144,640]{2,1,0:T(8,128)(2,1)}, u32[]{:S(2)}, u32[]{:S(2)}) async-start(bf16[16,144,640]{2,1,0:T(8,128)(2,1)} %compact_cells.3), calls=%async_computation.1 | async-start | bytes 5898240 | tf_op jit(solution)/shard_map/all_to_all | solution.py:609
  64.1 0.5 add.16.ends_ref
  64.6 0.6 reshape.52.gain_ref
  65.2 0.6 reshape.53.bias_ref
  65.8 0.6 reshape.54.scale_ref
  66.4 0.6 reshape.55.shift_ref
  67.0 52.6 %all-to-all-done.1.r_ref = bf16[16,144,640]{2,1,0:T(8,128)(2,1)} async-done(((bf16[16,144,640]{2,1,0:T(8,128)(2,1)}), bf16[16,144,640]{2,1,0:T(8,128)(2,1)}, u32[]{:S(2)}, u32[]{:S(2)}) %all-to-all-start.1) | async-done | bytes 2949152 | tf_op jit(solution)/shard_map/all_to_all | solution.py:609
  119.6 29.2 %project_and_convolve.1 = bf16[512,1536]{1,0:T(8,128)(2,1)} custom-call(s32[1]{0:T(128)} %bitcast.slab_ref, s32[32]{0:T(128)} %add.16.ends_ref, bf16[16,144,640]{2,1,0:T(8,128)(2,1)} %all-to-all-done.1.r_ref, bf16[2,16,176,1536]{3,2,1,0:T(8,128)(2,1)} %bitcast.18, f32[1,1536]{1,0:T(1,128)} %reshape.52.gain_ref, f32[1,1536]{1,0:T(1,128)} %reshape.53.bias_ref, ...), custom_call_target="tpu_custom_call" | custom-call | flops 8999999488 | bytes 25000000 | tf_op jit(solution)/shard_map/project_and_convolve/pallas_call | solution.py:518
  (34 shorter events, 0.7 us)
Async XLA Ops:
  6.5 1.1 copy-start
  6.5 1.2 copy-start.2
  6.5 113.1 %all-gather.2.cloned.1.call-start = ((), (), s32[]{:S(2)}) async-start(), calls=%async_computation.2 | async-start | bytes 17842176 | tf_op jit(solution)/shard_map/all_gather | solution.py:585
  13.3 29.0 %all-to-all-start = ((bf16[8,256,384]{2,1,0:T(8,128)(2,1)}), bf16[8,256,384]{2,1,0:T(8,128)(2,1)S(1)}, u32[]{:S(2)}, u32[]{:S(2)}) async-start(bf16[8,256,384]{2,1,0:T(8,128)(2,1)} %bitcast.16), calls=%async_computation | async-start | bytes 3145728 | tf_op jit(solution)/shard_map/all_to_all | solution.py:589
  17.8 15.5 %copy-start.8 = (s32[256]{0:T(256)S(1)}, s32[256]{0:T(256)}, u32[]{:S(2)}) copy-start(s32[256]{0:T(256)} %assignment_ref.3) | copy-start | bytes 3076
  17.8 24.2 %copy-start.7 = (s32[256]{0:T(256)S(1)}, s32[256]{0:T(256)}, u32[]{:S(2)}) copy-start(s32[256]{0:T(256)} %lengths_ref.3) | copy-start | bytes 3076
  27.8 5.7 %collective-permute-start = (bf16[256,256]{1,0:T(8,128)(2,1)}, bf16[256,256]{1,0:T(8,128)(2,1)S(1)}, u32[]{:S(2)}, u32[]{:S(2)}) collective-permute-start(bf16[256,256]{1,0:T(8,128)(2,1)} %get-tuple-element.19), channel_id=1, source_target_pairs={{0,16},{16,0},{32,48},{48,32},{64,80},{80,64},{96,112},{112,96},{1... | collective-permute-start | bytes 393224 | tf_op jit(solution)/shard_map/ppermute | solution.py:604
  28.4 12.8 %collective-permute-start.1 = (bf16[256,256]{1,0:T(8,128)(2,1)}, bf16[256,256]{1,0:T(8,128)(2,1)S(1)}, u32[]{:S(2)}, u32[]{:S(2)}) collective-permute-start(bf16[256,256]{1,0:T(8,128)(2,1)} %get-tuple-element.20), channel_id=1, source_target_pairs={{0,32},{16,48},{32,0},{48,16},{64,96},{80,112},{96,64},{112,80},{1... | collective-permute-start | bytes 393224 | tf_op jit(solution)/shard_map/ppermute | solution.py:604
  30.0 16.6 %collective-permute-start.2 = (bf16[256,256]{1,0:T(8,128)(2,1)}, bf16[256,256]{1,0:T(8,128)(2,1)S(1)}, u32[]{:S(2)}, u32[]{:S(2)}) collective-permute-start(bf16[256,256]{1,0:T(8,128)(2,1)} %get-tuple-element.21), channel_id=1, source_target_pairs={{0,48},{16,32},{32,16},{48,0},{64,112},{80,96},{96,80},{112,64},{1... | collective-permute-start | bytes 393224 | tf_op jit(solution)/shard_map/ppermute | solution.py:604
  30.0 18.4 %collective-permute-start.3 = (bf16[256,256]{1,0:T(8,128)(2,1)}, bf16[256,256]{1,0:T(8,128)(2,1)S(1)}, u32[]{:S(2)}, u32[]{:S(2)}) collective-permute-start(bf16[256,256]{1,0:T(8,128)(2,1)} %get-tuple-element.22), channel_id=1, source_target_pairs={{0,64},{16,80},{32,96},{48,112},{64,0},{80,16},{96,32},{112,48},{1... | collective-permute-start | bytes 393224 | tf_op jit(solution)/shard_map/ppermute | solution.py:604
  33.2 17.0 %collective-permute-start.4 = (bf16[256,256]{1,0:T(8,128)(2,1)}, bf16[256,256]{1,0:T(8,128)(2,1)S(1)}, u32[]{:S(2)}, u32[]{:S(2)}) collective-permute-start(bf16[256,256]{1,0:T(8,128)(2,1)} %get-tuple-element.23), channel_id=1, source_target_pairs={{0,80},{16,64},{32,112},{48,96},{64,16},{80,0},{96,48},{112,32},{1... | collective-permute-start | bytes 393224 | tf_op jit(solution)/shard_map/ppermute | solution.py:604
  33.5 16.8 %collective-permute-start.5 = (bf16[256,256]{1,0:T(8,128)(2,1)}, bf16[256,256]{1,0:T(8,128)(2,1)S(1)}, u32[]{:S(2)}, u32[]{:S(2)}) collective-permute-start(bf16[256,256]{1,0:T(8,128)(2,1)} %get-tuple-element.24), channel_id=1, source_target_pairs={{0,96},{16,112},{32,64},{48,80},{64,32},{80,48},{96,0},{112,16},{1... | collective-permute-start | bytes 393224 | tf_op jit(solution)/shard_map/ppermute | solution.py:604
  41.2 12.0 %collective-permute-start.6 = (bf16[256,256]{1,0:T(8,128)(2,1)}, bf16[256,256]{1,0:T(8,128)(2,1)S(1)}, u32[]{:S(2)}, u32[]{:S(2)}) collective-permute-start(bf16[256,256]{1,0:T(8,128)(2,1)} %get-tuple-element.25), channel_id=1, source_target_pairs={{0,112},{16,96},{32,80},{48,64},{64,48},{80,32},{96,16},{112,0},{1... | collective-permute-start | bytes 393224 | tf_op jit(solution)/shard_map/ppermute | solution.py:604
  42.3 10.9 %copy-start.1 = (bf16[256,256]{1,0:T(8,128)(2,1)S(1)}, bf16[256,256]{1,0:T(8,128)(2,1)}, u32[]{:S(2)}) copy-start(bf16[256,256]{1,0:T(8,128)(2,1)} %get-tuple-element.18.rest_0_) | copy-start | bytes 393220
  55.9 8.7 %copy-start.3 = (f32[1536]{0:T(1024)S(1)}, f32[1536]{0:T(1024)}, u32[]{:S(2)}) copy-start(f32[1536]{0:T(1024)} %param.21) | copy-start | bytes 18436
  56.0 9.2 %copy-start.4 = (f32[1536]{0:T(1024)S(1)}, f32[1536]{0:T(1024)}, u32[]{:S(2)}) copy-start(f32[1536]{0:T(1024)} %param.22) | copy-start | bytes 18436
  56.0 9.8 %copy-start.5 = (f32[1536]{0:T(1024)S(1)}, f32[1536]{0:T(1024)}, u32[]{:S(2)}) copy-start(f32[1536]{0:T(1024)} %param.25) | copy-start | bytes 18436
  56.0 10.4 %copy-start.6 = (f32[1536]{0:T(1024)S(1)}, f32[1536]{0:T(1024)}, u32[]{:S(2)}) copy-start(f32[1536]{0:T(1024)} %param.26) | copy-start | bytes 18436
  56.0 63.6 %all-to-all-start.1 = ((bf16[16,144,640]{2,1,0:T(8,128)(2,1)}), bf16[16,144,640]{2,1,0:T(8,128)(2,1)}, u32[]{:S(2)}, u32[]{:S(2)}) async-start(bf16[16,144,640]{2,1,0:T(8,128)(2,1)} %compact_cells.3), calls=%async_computation.1 | async-start | bytes 5898240 | tf_op jit(solution)/shard_map/all_to_all | solution.py:609
Sparse Core Ops, SparseCore 0:
  9.7 103.0 all-gather.1

commit v7 on v6

--- a/solution.py
+++ b/solution.py
@@ -306,8 +306,6 @@
         number = lax.fori_loop(0, 32, count, jnp.where(frame >= 0, 0, -1), unroll=4)
         segment[j] = number.astype(F32)
 
-    for copy in arrived:
-        copy.wait()
     lane = lax.broadcasted_iota(jnp.int32, (WIN, 384), 1)
 
     def features(g, _):
@@ -323,8 +321,6 @@
             carried[WIN * j : WIN * j + WIN, at] = whole.astype(F32)
         return 0
 
-    lax.fori_loop(0, 4, features, 0, unroll=4)
-
     low = lax.broadcasted_iota(jnp.int32, (WIN, 128), 1) < 64
 
     def heads(h, _):
@@ -340,7 +336,11 @@
             ctx[WIN * j : WIN * j + WIN, at] = jnp.where(low, left, right).astype(BF16)
         return 0
 
-    lax.fori_loop(0, 8, heads, 0, unroll=8)
+    for q in range(4):
+        arrived[q].wait()
+        features(q, 0)
+        heads(2 * q, 0)
+        heads(2 * q + 1, 0)
 
     pltpu.make_async_copy(wo, wo, sems.at[0]).wait()
 
@@ -361,7 +361,7 @@
         normed[at, :] = (centred * lax.rsqrt(variance + EPS) * gain_ref[...] + bias_ref[...]).astype(BF16)
         return 0
 
-    lax.fori_loop(0, 4 * WIN // 16, norm, 0, unroll=6)
+    lax.fori_loop(0, 4 * WIN // 16, norm, 0, unroll=12)
 
     def glu(n, _):
         value = lax.dot_general(
@@ -411,7 +411,7 @@
                             sums[l, rows[j], :] = total[l, j]
                 return 0
 
-            lax.fori_loop(0, 16, chunk, 0, unroll=4)
+            lax.fori_loop(0, 16, chunk, 0, unroll=8)
         for l, at in enumerate(lanes):
             affine = sums[l] * scale_ref[:, at] + shift_ref[:, at]
             swished[:, at] = (affine * jax.nn.sigmoid(affine)).astype(BF16)

time: 158 us -> 157 us (level)
  no operation moved by 1% of the time
where the time goes in v7:
time: 157 us; the launch traced here: 155 us
  waiting for transfers between devices  63.8 us (41%)
  Pallas kernels  50 us (32%)
  starting transfers between devices  22 us (14%)
  between operations  13.6 us (9%)
  local copies, waits for them, and re-layouts  3.61 us (2%)
  other arithmetic  1.72 us (1%)
    all_to_all x1, waiting for transfers between devices, on_device(): lax.all_to_all(windows, 'mp', split_axis=0, concat_axis=0, tiled=True)  52.5 us
    pallas_call x1, Pallas kernels, rest(): pl.pallas_call(rest_kernel, out_shape=jax.ShapeDtypeStruct((512, 1536), B...  28.3 us
    ppermute x7, waiting for transfers between devices, on_device(): lax.ppermute(c_cells[s], 'dp', [(i, i ^ s) for i in range(groups)])  11.2 us
    pallas_call x1, Pallas kernels, attend(): pl.pallas_call(attend_kernel, out_shape=[jax.ShapeDtypeStruct((4 * CELL,...  9.97 us
    ppermute x7, starting transfers between devices, on_device(): lax.ppermute(c_cells[s], 'dp', [(i, i ^ s) for i in range(groups)])  9.36 us
    all_to_all x1, starting transfers between devices, on_device(): lax.all_to_all(windows, 'mp', split_axis=0, concat_axis=0, tiled=True)  8.08 us
    pallas_call x2, Pallas kernels, compact(): pl.pallas_call(functools.partial(compact_kernel, width, offset, len(cells...  7.14 us
    pallas_call x1, Pallas kernels, pack(): pl.pallas_call(pack_kernel, out_shape=jax.ShapeDtypeStruct((32 * CELL, 38...  4.65 us
  transfers between devices with their start and end apart: 10, of which 5 were waited for; matrix products, arithmetic and copies ran while one was open for 2% of the time, Pallas kernels for 14%

profile of v7, /device:TPU:0, one launch (start us, length us, event | category | flops | bytes accessed | tf_op | source)
XLA Modules:
  0.0 154.7 jit_solution(17981135529924038120)
XLA Ops:
  6.5 1.0 dynamic-slice_bitcast_fusion.2
  7.7 0.8 pad_maximum_fusion
  8.6 4.6 %pack_cells.1 = bf16[2048,384]{1,0:T(8,128)(2,1)} custom-call(s32[1]{0:T(128)} %bitcast.1.group_ref, s32[256]{0:T(256)} %lengths_ref.3, s32[256]{0:T(256)} %assignment_ref.3, bf16[2048,384]{1,0:T(8,128)(2,1)} %bitcast.17), custom_call_target="tpu_custom_call" | custom-call | flops 20000000 | bytes 3200000 | tf_op jit(solution)/shard_map/pack_cells/pallas_call | solution.py:452
  13.3 4.6 %all-to-all-start = ((bf16[8,256,384]{2,1,0:T(8,128)(2,1)}), bf16[8,256,384]{2,1,0:T(8,128)(2,1)S(1)}, u32[]{:S(2)}, u32[]{:S(2)}) async-start(bf16[8,256,384]{2,1,0:T(8,128)(2,1)} %bitcast.16), calls=%async_computation | async-start | bytes 3145728 | tf_op jit(solution)/shard_map/all_to_all | solution.py:589
  17.8 10.0 %attend_cells.1 = (bf16[256,256]{1,0:T(8,128)(2,1)}, bf16[256,256]{1,0:T(8,128)(2,1)}, bf16[256,256]{1,0:T(8,128)(2,1)}, bf16[256,256]{1,0:T(8,128)(2,1)}, bf16[...) custom-call(s32[1]{0:T(128)} %bitcast.1.group_ref, ...), custom_call_target="tpu_custom_call" | custom-call | flops 2000000000 | bytes 4200000 | tf_op jit(solution)/shard_map/attend_cells/pallas_call | solution.py:473
  27.8 0.5 collective-permute-start
  28.4 1.7 %collective-permute-start.1 = (bf16[256,256]{1,0:T(8,128)(2,1)}, bf16[256,256]{1,0:T(8,128)(2,1)S(1)}, u32[]{:S(2)}, u32[]{:S(2)}) collective-permute-start(bf16[256,256]{1,0:T(8,128)(2,1)} %get-tuple-element.20), channel_id=1, source_target_pairs={{0,32},{16,48},{32,0},{48,16},{64,96},{80,112},{96,64},{112,80},{1... | collective-permute-start | bytes 393224 | tf_op jit(solution)/shard_map/ppermute | solution.py:604
  30.1 3.2 %collective-permute-start.3 = (bf16[256,256]{1,0:T(8,128)(2,1)}, bf16[256,256]{1,0:T(8,128)(2,1)S(1)}, u32[]{:S(2)}, u32[]{:S(2)}) collective-permute-start(bf16[256,256]{1,0:T(8,128)(2,1)} %get-tuple-element.22), channel_id=1, source_target_pairs={{0,64},{16,80},{32,96},{48,112},{64,0},{80,16},{96,32},{112,48},{1... | collective-permute-start | bytes 393224 | tf_op jit(solution)/shard_map/ppermute | solution.py:604
  33.5 3.0 %collective-permute-start.5 = (bf16[256,256]{1,0:T(8,128)(2,1)}, bf16[256,256]{1,0:T(8,128)(2,1)S(1)}, u32[]{:S(2)}, u32[]{:S(2)}) collective-permute-start(bf16[256,256]{1,0:T(8,128)(2,1)} %get-tuple-element.24), channel_id=1, source_target_pairs={{0,96},{16,112},{32,64},{48,80},{64,32},{80,48},{96,0},{112,16},{1... | collective-permute-start | bytes 393224 | tf_op jit(solution)/shard_map/ppermute | solution.py:604
  36.5 4.7 %collective-permute-done.1.rest_2_ = bf16[256,256]{1,0:T(8,128)(2,1)S(1)} collective-permute-done((bf16[256,256]{1,0:T(8,128)(2,1)}, bf16[256,256]{1,0:T(8,128)(2,1)S(1)}, u32[]{:S(2)}, u32[]{:S(2)}) %collective-permute-start.1) | collective-permute-done | bytes 131104 | tf_op jit(solution)/shard_map/ppermute | solution.py:604
  41.2 0.8 collective-permute-start.6
  42.3 4.4 %compact_cells.2.rest_8_ = bf16[16,144,640]{2,1,0:T(8,128)(2,1)} custom-call(s32[1]{0:T(128)} %bitcast.1.group_ref, s32[32]{0:T(128)S(1)} %select_reduce_fusion.2.after_ref, bf16[2048,384]{1,0:T(8,128)(2,1)S(1)} %bitcast.15), custom_call_target="tpu_custom_call" | custom-call | flops 20000000 | bytes 3200000 | tf_op jit(solution)/shard_map/compact_cells/pallas_call | solution.py:500
  46.7 1.7 %collective-permute-done.3.rest_4_ = bf16[256,256]{1,0:T(8,128)(2,1)S(1)} collective-permute-done((bf16[256,256]{1,0:T(8,128)(2,1)}, bf16[256,256]{1,0:T(8,128)(2,1)S(1)}, u32[]{:S(2)}, u32[]{:S(2)}) %collective-permute-start.3) | collective-permute-done | bytes 131104 | tf_op jit(solution)/shard_map/ppermute | solution.py:604
  48.4 1.9 %collective-permute-done.4.rest_5_ = bf16[256,256]{1,0:T(8,128)(2,1)S(1)} collective-permute-done((bf16[256,256]{1,0:T(8,128)(2,1)}, bf16[256,256]{1,0:T(8,128)(2,1)S(1)}, u32[]{:S(2)}, u32[]{:S(2)}) %collective-permute-start.4) | collective-permute-done | bytes 131104 | tf_op jit(solution)/shard_map/ppermute | solution.py:604
  50.3 2.9 %collective-permute-done.6.rest_7_ = bf16[256,256]{1,0:T(8,128)(2,1)S(1)} collective-permute-done((bf16[256,256]{1,0:T(8,128)(2,1)}, bf16[256,256]{1,0:T(8,128)(2,1)S(1)}, u32[]{:S(2)}, u32[]{:S(2)}) %collective-permute-start.6) | collective-permute-done | bytes 131104 | tf_op jit(solution)/shard_map/ppermute | solution.py:604
  53.2 2.8 %compact_cells.3 = bf16[16,144,640]{2,1,0:T(8,128)(2,1)} custom-call(s32[1]{0:T(128)} %bitcast.1.group_ref, s32[32]{0:T(128)S(1)} %select_reduce_fusion.2.after_ref, bf16[256,256]{1,0:T(8,128)(2,1)S(1)} %copy-done.1, bf16[256,256]{1,0:T(8,128)(2,1)S(1)} %collective-permute-done.rest_1_, ...), custom_call_target="tpu_custom_call", output_to_operand_aliasing={{}: (10, {})} | custom-call | flops 20000000 | bytes 3200000 | tf_op jit(solution)/shard_map/compact_cells/pallas_call | solution.py:500
  56.0 8.1 %all-to-all-start.1 = ((bf16[16,144,640]{2,1,0:T(8,128)(2,1)}), bf16[16,144,640]{2,1,0:T(8,128)(2,1)}, u32[]{:S(2)}, u32[]{:S(2)}) async-start(bf16[16,144,640]{2,1,0:T(8,128)(2,1)} %compact_cells.3), calls=%async_computation.1 | async-start | bytes 5898240 | tf_op jit(solution)/shard_map/all_to_all | solution.py:609
  64.1 0.5 add.16.ends_ref
  64.6 0.6 reshape.52.gain_ref
  65.2 0.6 reshape.53.bias_ref
  65.8 0.6 reshape.54.scale_ref
  66.4 0.6 reshape.55.shift_ref
  67.0 52.5 %all-to-all-done.1.r_ref = bf16[16,144,640]{2,1,0:T(8,128)(2,1)} async-done(((bf16[16,144,640]{2,1,0:T(8,128)(2,1)}), bf16[16,144,640]{2,1,0:T(8,128)(2,1)}, u32[]{:S(2)}, u32[]{:S(2)}) %all-to-all-start.1) | async-done | bytes 2949152 | tf_op jit(solution)/shard_map/all_to_all | solution.py:609
  119.6 28.3 %project_and_convolve.1 = bf16[512,1536]{1,0:T(8,128)(2,1)} custom-call(s32[1]{0:T(128)} %bitcast.slab_ref, s32[32]{0:T(128)} %add.16.ends_ref, bf16[16,144,640]{2,1,0:T(8,128)(2,1)} %all-to-all-done.1.r_ref, bf16[2,16,176,1536]{3,2,1,0:T(8,128)(2,1)} %bitcast.18, f32[1,1536]{1,0:T(1,128)} %reshape.52.gain_ref, f32[1,1536]{1,0:T(1,128)} %reshape.53.bias_ref, ...), custom_call_target="tpu_custom_call" | custom-call | flops 8999999488 | bytes 25000000 | tf_op jit(solution)/shard_map/project_and_convolve/pallas_call | solution.py:518
  (34 shorter events, 0.7 us)
Async XLA Ops:
  6.5 1.1 copy-start
  6.5 1.2 copy-start.2
  6.5 113.0 %all-gather.2.cloned.1.call-start = ((), (), s32[]{:S(2)}) async-start(), calls=%async_computation.2 | async-start | bytes 17842176 | tf_op jit(solution)/shard_map/all_gather | solution.py:585
  13.3 29.0 %all-to-all-start = ((bf16[8,256,384]{2,1,0:T(8,128)(2,1)}), bf16[8,256,384]{2,1,0:T(8,128)(2,1)S(1)}, u32[]{:S(2)}, u32[]{:S(2)}) async-start(bf16[8,256,384]{2,1,0:T(8,128)(2,1)} %bitcast.16), calls=%async_computation | async-start | bytes 3145728 | tf_op jit(solution)/shard_map/all_to_all | solution.py:589
  17.8 15.5 %copy-start.8 = (s32[256]{0:T(256)S(1)}, s32[256]{0:T(256)}, u32[]{:S(2)}) copy-start(s32[256]{0:T(256)} %assignment_ref.3) | copy-start | bytes 3076
  17.8 24.2 %copy-start.7 = (s32[256]{0:T(256)S(1)}, s32[256]{0:T(256)}, u32[]{:S(2)}) copy-start(s32[256]{0:T(256)} %lengths_ref.3) | copy-start | bytes 3076
  27.8 5.7 %collective-permute-start = (bf16[256,256]{1,0:T(8,128)(2,1)}, bf16[256,256]{1,0:T(8,128)(2,1)S(1)}, u32[]{:S(2)}, u32[]{:S(2)}) collective-permute-start(bf16[256,256]{1,0:T(8,128)(2,1)} %get-tuple-element.19), channel_id=1, source_target_pairs={{0,16},{16,0},{32,48},{48,32},{64,80},{80,64},{96,112},{112,96},{1... | collective-permute-start | bytes 393224 | tf_op jit(solution)/shard_map/ppermute | solution.py:604
  28.4 12.8 %collective-permute-start.1 = (bf16[256,256]{1,0:T(8,128)(2,1)}, bf16[256,256]{1,0:T(8,128)(2,1)S(1)}, u32[]{:S(2)}, u32[]{:S(2)}) collective-permute-start(bf16[256,256]{1,0:T(8,128)(2,1)} %get-tuple-element.20), channel_id=1, source_target_pairs={{0,32},{16,48},{32,0},{48,16},{64,96},{80,112},{96,64},{112,80},{1... | collective-permute-start | bytes 393224 | tf_op jit(solution)/shard_map/ppermute | solution.py:604
  30.1 16.6 %collective-permute-start.2 = (bf16[256,256]{1,0:T(8,128)(2,1)}, bf16[256,256]{1,0:T(8,128)(2,1)S(1)}, u32[]{:S(2)}, u32[]{:S(2)}) collective-permute-start(bf16[256,256]{1,0:T(8,128)(2,1)} %get-tuple-element.21), channel_id=1, source_target_pairs={{0,48},{16,32},{32,16},{48,0},{64,112},{80,96},{96,80},{112,64},{1... | collective-permute-start | bytes 393224 | tf_op jit(solution)/shard_map/ppermute | solution.py:604
  30.1 18.4 %collective-permute-start.3 = (bf16[256,256]{1,0:T(8,128)(2,1)}, bf16[256,256]{1,0:T(8,128)(2,1)S(1)}, u32[]{:S(2)}, u32[]{:S(2)}) collective-permute-start(bf16[256,256]{1,0:T(8,128)(2,1)} %get-tuple-element.22), channel_id=1, source_target_pairs={{0,64},{16,80},{32,96},{48,112},{64,0},{80,16},{96,32},{112,48},{1... | collective-permute-start | bytes 393224 | tf_op jit(solution)/shard_map/ppermute | solution.py:604
  33.2 17.0 %collective-permute-start.4 = (bf16[256,256]{1,0:T(8,128)(2,1)}, bf16[256,256]{1,0:T(8,128)(2,1)S(1)}, u32[]{:S(2)}, u32[]{:S(2)}) collective-permute-start(bf16[256,256]{1,0:T(8,128)(2,1)} %get-tuple-element.23), channel_id=1, source_target_pairs={{0,80},{16,64},{32,112},{48,96},{64,16},{80,0},{96,48},{112,32},{1... | collective-permute-start | bytes 393224 | tf_op jit(solution)/shard_map/ppermute | solution.py:604
  33.5 16.8 %collective-permute-start.5 = (bf16[256,256]{1,0:T(8,128)(2,1)}, bf16[256,256]{1,0:T(8,128)(2,1)S(1)}, u32[]{:S(2)}, u32[]{:S(2)}) collective-permute-start(bf16[256,256]{1,0:T(8,128)(2,1)} %get-tuple-element.24), channel_id=1, source_target_pairs={{0,96},{16,112},{32,64},{48,80},{64,32},{80,48},{96,0},{112,16},{1... | collective-permute-start | bytes 393224 | tf_op jit(solution)/shard_map/ppermute | solution.py:604
  41.2 12.0 %collective-permute-start.6 = (bf16[256,256]{1,0:T(8,128)(2,1)}, bf16[256,256]{1,0:T(8,128)(2,1)S(1)}, u32[]{:S(2)}, u32[]{:S(2)}) collective-permute-start(bf16[256,256]{1,0:T(8,128)(2,1)} %get-tuple-element.25), channel_id=1, source_target_pairs={{0,112},{16,96},{32,80},{48,64},{64,48},{80,32},{96,16},{112,0},{1... | collective-permute-start | bytes 393224 | tf_op jit(solution)/shard_map/ppermute | solution.py:604
  42.3 10.9 %copy-start.1 = (bf16[256,256]{1,0:T(8,128)(2,1)S(1)}, bf16[256,256]{1,0:T(8,128)(2,1)}, u32[]{:S(2)}) copy-start(bf16[256,256]{1,0:T(8,128)(2,1)} %get-tuple-element.18.rest_0_) | copy-start | bytes 393220
  56.0 8.7 %copy-start.3 = (f32[1536]{0:T(1024)S(1)}, f32[1536]{0:T(1024)}, u32[]{:S(2)}) copy-start(f32[1536]{0:T(1024)} %param.21) | copy-start | bytes 18436
  56.0 9.2 %copy-start.4 = (f32[1536]{0:T(1024)S(1)}, f32[1536]{0:T(1024)}, u32[]{:S(2)}) copy-start(f32[1536]{0:T(1024)} %param.22) | copy-start | bytes 18436
  56.0 9.8 %copy-start.5 = (f32[1536]{0:T(1024)S(1)}, f32[1536]{0:T(1024)}, u32[]{:S(2)}) copy-start(f32[1536]{0:T(1024)} %param.25) | copy-start | bytes 18436
  56.0 10.4 %copy-start.6 = (f32[1536]{0:T(1024)S(1)}, f32[1536]{0:T(1024)}, u32[]{:S(2)}) copy-start(f32[1536]{0:T(1024)} %param.26) | copy-start | bytes 18436
  56.0 63.5 %all-to-all-start.1 = ((bf16[16,144,640]{2,1,0:T(8,128)(2,1)}), bf16[16,144,640]{2,1,0:T(8,128)(2,1)}, u32[]{:S(2)}, u32[]{:S(2)}) async-start(bf16[16,144,640]{2,1,0:T(8,128)(2,1)} %compact_cells.3), calls=%async_computation.1 | async-start | bytes 5898240 | tf_op jit(solution)/shard_map/all_to_all | solution.py:609
Sparse Core Ops, SparseCore 0:
  9.7 103.0 all-gather.1
